TPU v7x, 32 devices: a whole 2x2x4 slice. The times are simulated.
32 devices in a mesh: ens: 2 (over y), ty: 4 (over z), tx: 4 (over x, core).
Axes of the slice: x: 2, y: 2, z: 4, core: 2. Of those that a mesh axis runs over, the one named last changes fastest.
Arguments:
- perturbations: bfloat16 [32, 3, 512, 512], P('ens', None, 'ty', 'tx'), may hold values from -1 to 1
- ens_weights: float32 [32, 512, 512], P('ens', 'ty', 'tx'), may hold values from -6 to 6
- control: float32 [3, 512, 512], P(None, 'ty', 'tx'), may hold values from -6 to 6
- static_std: float32 [3, 512, 512], P(None, 'ty', 'tx'), may hold values from 0.2 to 1
- courant: float32 [512, 512], P('ty', 'tx'), may hold values from 0.05 to 0.4
- land_mask: int32 [512, 512], P('ty', 'tx'), may hold values 0 or 1
- band_offsets: int32 [32], replicated, may hold values from 0 to 31
- band_weights: float32 [32], replicated, may hold values from 0.05 to 1
- obs_cells: int32 [4, 4, 6, 512], P('ty', 'tx'), may hold values from 0 to 16383
- obs_values: float32 [4, 4, 6, 512], P('ty', 'tx'), may hold values from -4 to 4
- obs_weights: float32 [4, 4, 6, 512], P('ty', 'tx'), may hold values from 0.5 to 2
Outputs:
- control_new: float32 [3, 512, 512], P(None, 'ty', 'tx')
- weights_new: float32 [32, 512, 512], P('ens', 'ty', 'tx')
- cost_value: float32 [], replicated
Inputs may be any that keep to these rules, and one draw needn't show every extreme that they name: `obs_cells`: row-major index of a cell within the observing tile of 128 x 128 cells.
All inputs are finite; a program needn't handle non-finite values. No bound on the sum of `land_mask` on one device may be relied on, other than what follows from the above.
Results may differ from a plain program's by a relative error of at most 0.0003.
Values may be sent and summed in bfloat16 or wider, within the bound.
No kernel may reach another device: no remote copies, remote signals or barrier semaphores. Data moves between devices by JAX's collectives and lax.ppermute only.
A program may use at most 128 MiB of HBM per device.

v0:
```python
import functools
import math

import jax
import jax.numpy as jnp
from jax import lax
from jax.experimental import pallas as pl
from jax.experimental.pallas import tpu as pltpu
from jax.sharding import PartitionSpec as P

step_length = 0.25
SUB = 16
F32 = jnp.float32
BF16 = jnp.bfloat16
VMEM = pl.BlockSpec(memory_space=pltpu.VMEM)
SMEM = pl.BlockSpec(memory_space=pltpu.SMEM)


def call(kernel, outs, ins, scratch=(), smem=0, flops=0, name=None):
    out_shape = [jax.ShapeDtypeStruct(s, d) for s, d in outs]
    moved = sum(math.prod(s) * jnp.dtype(d).itemsize for s, d in outs)
    moved += sum(x.size * x.dtype.itemsize for x in ins)
    return pl.pallas_call(
        kernel,
        out_shape=out_shape,
        in_specs=[SMEM] * smem + [VMEM] * (len(ins) - smem),
        out_specs=[VMEM] * len(outs),
        scratch_shapes=list(scratch),
        compiler_params=pltpu.CompilerParams(vmem_limit_bytes=40 * 1024 * 1024),
        cost_estimate=pl.CostEstimate(flops=flops, bytes_accessed=moved, transcendentals=0),
        name=name,
    )(*ins)


def split(x):
    hi = x.astype(BF16)
    return hi, (x - hi.astype(F32)).astype(BF16)


def folded(x):
    cols = x.shape[-1]
    return jnp.sum(x.reshape(-1, 8, cols), axis=0)


def maps_kernel(steps, cells_ref, values_ref, weights_ref, control_ref, maps_ref, cost_ref):
    rows, cols = maps_ref.shape[1:]
    count = cells_ref.shape[1]
    shift = cols.bit_length() - 1
    row_iota = lax.broadcasted_iota(jnp.int32, (rows, count), 0)
    col_iota = lax.broadcasted_iota(jnp.int32, (cols, count), 0)
    for t in range(steps):
        cells = cells_ref[t : t + 1, :]
        weight = weights_ref[t : t + 1, :]
        product = weight * values_ref[t : t + 1, :]
        at_row = jnp.where(row_iota == (cells >> shift), 1.0, 0.0).astype(BF16)
        hit = col_iota == (cells & (cols - 1))
        parts = []
        for value in (weight, product):
            for piece in split(value):
                parts.append(jnp.where(hit, piece.astype(F32), 0.0).astype(BF16))
        sums = lax.dot_general(
            at_row,
            jnp.concatenate(parts, axis=0),
            (((1,), (1,)), ((), ())),
            preferred_element_type=F32,
        )
        maps_ref[t] = sums[:, :cols] + sums[:, cols : 2 * cols]
        maps_ref[steps + t] = sums[:, 2 * cols : 3 * cols] + sums[:, 3 * cols :]
    value = values_ref[...]
    fixed = jnp.sum(weights_ref[...] * value * value, axis=0, keepdims=True)
    line = sum(fixed[:, k : k + cols] for k in range(0, count, cols))
    first = lax.broadcasted_iota(jnp.int32, (8, cols), 0) == 0
    control = control_ref[...]
    cost_ref[...] = folded(control * control) + jnp.where(first, line, 0.0)


def expand(small, rows, cols):
    left = lax.broadcasted_iota(jnp.int32, (rows * SUB, rows), 0) // SUB
    left = (left == lax.broadcasted_iota(jnp.int32, (rows * SUB, rows), 1)).astype(F32).astype(BF16)
    right = lax.broadcasted_iota(jnp.int32, (cols, cols * SUB), 1) // SUB
    right = (right == lax.broadcasted_iota(jnp.int32, (cols, cols * SUB), 0)).astype(F32).astype(BF16)
    wide = jnp.dot(small, right, preferred_element_type=F32).astype(BF16)
    full = jnp.dot(left, wide, preferred_element_type=F32)
    row = lax.broadcasted_iota(jnp.int32, full.shape, 0) % SUB
    col = lax.broadcasted_iota(jnp.int32, full.shape, 1) % SUB
    return jnp.where(row == col, full, 0.0).astype(BF16)


def pair_of(ref, y):
    members, _, cols = ref.shape
    blocks = [ref[:, y + k * SUB : y + (k + 1) * SUB, :].reshape(members * SUB, cols) for k in (0, 1)]
    return jnp.concatenate(blocks, axis=1)


def add_share(beta, perturbations_ref, share_ref, y):
    members = perturbations_ref.shape[0]
    cols = perturbations_ref.shape[3]
    for k in (0, 1):
        part = beta[:, k * cols : (k + 1) * cols].reshape(members, SUB, cols)
        rows = slice(y + k * SUB, y + (k + 1) * SUB)
        for c in range(3):
            term = part[0] * perturbations_ref[0, c, rows, :].astype(F32)
            for i in range(1, members):
                term = term + part[i] * perturbations_ref[i, c, rows, :].astype(F32)
            share_ref[c, rows, :] += term


def own_kernel(groups, to_beta_ref, to_grad_ref, alpha_ref, perturbations_ref, kron_beta_ref, kron_grad_ref, share_ref, square_ref):
    members, rows, cols = alpha_ref.shape
    for g in range(groups):
        kron_beta_ref[g] = expand(to_beta_ref[g], members, members)
        kron_grad_ref[g] = expand(to_grad_ref[g], members, members)
    share_ref[...] = jnp.zeros_like(share_ref)
    matrix = kron_beta_ref[0]
    square = jnp.zeros((8, cols), F32)
    for y in range(0, rows, 2 * SUB):
        alpha = pair_of(alpha_ref, y)
        square = square + folded(alpha[:, :cols] * alpha[:, :cols]) + folded(alpha[:, cols:] * alpha[:, cols:])
        hi, lo = split(alpha)
        beta = jnp.dot(matrix, hi, preferred_element_type=F32) + jnp.dot(matrix, lo, preferred_element_type=F32)
        add_share(beta, perturbations_ref, share_ref, y)
    square_ref[...] = square


def share_kernel(groups, *refs):
    others = refs[: groups - 1]
    kron_ref, perturbations_ref, own_ref, square_ref, out_ref = refs[groups - 1 :]
    _, rows, cols = own_ref.shape
    share_ref = out_ref
    for c in range(3):
        share_ref[c, :, :] = own_ref[c]
    for y in range(0, rows, 2 * SUB):
        beta = None
        for g, other in enumerate(others):
            term = jnp.dot(kron_ref[g + 1], pair_of(other, y), preferred_element_type=F32)
            beta = term if beta is None else beta + term
        add_share(beta, perturbations_ref, share_ref, y)
    out_ref[3, :8, :] = square_ref[...]


def increment_kernel(scale, halo, own_ref, other_ref, std_ref, control_ref, early_ref, inc_ref, top_ref, bottom_ref, cost_ref):
    rows = inc_ref.shape[1]
    inc = std_ref[...] * control_ref[...] + scale * (own_ref[:3] + other_ref[:3])
    inc_ref[...] = inc
    top_ref[...] = inc[:, :halo]
    bottom_ref[...] = inc[:, rows - halo :]
    cost_ref[...] = early_ref[...] + own_ref[3, :8, :] + other_ref[3, :8, :]


def lane_pack(fields, widths):
    cols = fields[0].shape[1]
    lane = lax.broadcasted_iota(jnp.int32, fields[0].shape, 1)
    left = right = None
    at = 0
    for field, width in zip(fields, widths):
        to_left = field if at == 0 else pltpu.roll(field, at, 1)
        to_right = field if at == 0 else pltpu.roll(field, cols - at, 1)
        left = to_left if left is None else jnp.where(lane >= at, to_left, left)
        right = to_right if right is None else jnp.where(lane < cols - at, to_right, right)
        at += width
    return left, right


def lane_unpack(from_right, from_left, at, width):
    cols = from_right.shape[1]
    lane = lax.broadcasted_iota(jnp.int32, from_right.shape, 1)
    if at:
        from_right = pltpu.roll(from_right, cols - at, 1)
        from_left = pltpu.roll(from_left, at, 1)
    return jnp.where(lane < width, from_right, jnp.where(lane >= cols - width, from_left, 0.0))


def tall(tile, below, above, gap):
    parts = [tile, below]
    if gap:
        parts.append(jnp.zeros((gap, tile.shape[1]), F32))
    parts.append(above)
    return jnp.concatenate(parts, axis=0)


def pack_kernel(halo, inc_ref, below_ref, above_ref, left_ref, right_ref):
    fields = [tall(inc_ref[c], below_ref[c], above_ref[c], 0) for c in range(3)]
    left_ref[...], right_ref[...] = lane_pack(fields, [halo] * 3)


def edges_kernel(steps, halo, reach, maps_ref, courant_ref, mask_ref, top_ref, bottom_ref):
    rows = courant_ref.shape[0]
    for k in range(2 * steps):
        top_ref[k * reach : (k + 1) * reach, :] = maps_ref[k, :reach, :]
        bottom_ref[k * reach : (k + 1) * reach, :] = maps_ref[k, rows - reach :, :]
    at = 2 * steps * reach
    for field in (courant_ref[...], mask_ref[...].astype(F32)):
        top_ref[at : at + halo, :] = field[:halo]
        bottom_ref[at : at + halo, :] = field[rows - halo :]
        at += halo


def static_rows(steps, halo, reach, maps_ref, courant_ref, mask_ref, below_ref, above_ref):
    def one(tile, at, size):
        return tall(tile, below_ref[at : at + size, :], above_ref[at : at + size, :], 2 * (halo - size))

    maps = [one(maps_ref[k], k * reach, reach) for k in range(2 * steps)]
    at = 2 * steps * reach
    courant = one(courant_ref[...], at, halo)
    wet = one(mask_ref[...].astype(F32), at + halo, halo)
    return maps, courant, wet


def static_pack_kernel(steps, halo, reach, maps_ref, courant_ref, mask_ref, below_ref, above_ref, left_ref, right_ref):
    maps, courant, wet = static_rows(steps, halo, reach, maps_ref, courant_ref, mask_ref, below_ref, above_ref)
    width = 2 * steps
    widths = [width] * steps + [halo]
    left_ref[0], right_ref[0] = lane_pack(maps[:steps] + [courant], widths)
    left_ref[1], right_ref[1] = lane_pack(maps[steps:] + [wet], widths)


def model_kernel(
    steps,
    halo,
    reach,
    side_ref,
    inc_ref,
    below_ref,
    above_ref,
    from_right_ref,
    from_left_ref,
    maps_ref,
    courant_ref,
    mask_ref,
    s_below_ref,
    s_above_ref,
    s_right_ref,
    s_left_ref,
    early_ref,
    std_ref,
    control_ref,
    perturbations_ref,
    lam_ref,
    control_new_ref,
    cost_ref,
    product_ref,
    source_ref,
):
    _, rows, cols = inc_ref.shape
    members = perturbations_ref.shape[0]
    height_ext = rows + 2 * halo
    width_ext = 2 * cols

    def east(x):
        return pltpu.roll(x, width_ext - 1, 1) - pltpu.roll(x, 1, 1)

    def north(x):
        return pltpu.roll(x, height_ext - 1, 0) - pltpu.roll(x, 1, 0)

    maps, courant, wet = static_rows(steps, halo, reach, maps_ref, courant_ref, mask_ref, s_below_ref, s_above_ref)
    width = 2 * steps

    def with_sides(field, right, left, at, size):
        return jnp.concatenate([field, lane_unpack(right, left, at, size)], axis=1)

    full_maps = []
    for part in (0, 1):
        for t in range(steps):
            full_maps.append(
                with_sides(maps[part * steps + t], s_right_ref[part], s_left_ref[part], t * width, width)
            )
    courant = with_sides(courant, s_right_ref[0], s_left_ref[0], steps * width, halo)
    wet = with_sides(wet, s_right_ref[1], s_left_ref[1], steps * width, halo)
    state = [
        with_sides(
            tall(inc_ref[c], below_ref[c], above_ref[c], 0), from_right_ref[...], from_left_ref[...], c * halo, halo
        )
        for c in range(3)
    ]
    row = lax.broadcasted_iota(jnp.int32, (height_ext, width_ext), 0)
    below_outside = side_ref[1] == 1
    above_outside = side_ref[0] == 1
    outside = ((row >= rows) & (row < rows + halo) & below_outside) | ((row >= rows + halo) & above_outside)
    half_inside = jnp.where(outside, 0.0, 0.5)
    half_wet = 0.5 * wet
    half_both = half_wet * courant
    height, u, v = state[0], wet * state[1], wet * state[2]
    total = early_ref[...]
    for t in range(steps):
        u = u - half_wet * east(height)
        v = v - half_wet * north(height)
        height = height - half_inside * (east(courant * u) + north(courant * v))
        source = full_maps[t] * height - full_maps[steps + t]
        source_ref[t] = source
        total = total + folded(height[:rows, :cols] * (source[:rows, :cols] - full_maps[steps + t][:rows, :cols]))
    cost_ref[...] = jnp.broadcast_to(total[None], (cost_ref.shape[0] // 8, 8, cols)).reshape(cost_ref.shape)
    adj = source_ref[steps - 1]
    adj_u = adj_v = None
    for t in range(steps - 1, -1, -1):
        if t < steps - 1:
            adj = adj + source_ref[t]
        du = half_both * east(adj)
        dv = half_both * north(adj)
        adj_u = du if adj_u is None else adj_u + du
        adj_v = dv if adj_v is None else adj_v + dv
        adj = adj + half_inside * (east(adj_u) + north(adj_v))
    lam = [x[:rows, :cols] for x in (adj, adj_u, adj_v)]
    for c in range(3):
        lam_ref[c] = lam[c]
        old = control_ref[c]
        control_new_ref[c] = old - step_length * (old + std_ref[c] * lam[c])
    for i in range(members):
        product_ref[i] = products(perturbations_ref, lam_ref, i, slice(0, rows)).astype(BF16)


def products(perturbations_ref, lam_ref, i, rows):
    total = perturbations_ref[i, 0, rows, :].astype(F32) * lam_ref[0, rows, :]
    for c in (1, 2):
        total = total + perturbations_ref[i, c, rows, :].astype(F32) * lam_ref[c, rows, :]
    return total


def base_kernel(scale, kron_ref, alpha_ref, perturbations_ref, lam_ref, out_ref, product_ref):
    members, rows, cols = alpha_ref.shape
    for i in range(members):
        product_ref[i] = products(perturbations_ref, lam_ref, i, slice(0, rows))
    matrix = kron_ref[0]
    for y in range(0, rows, 2 * SUB):
        hi, lo = split(pair_of(product_ref, y))
        grad = jnp.dot(matrix, hi, preferred_element_type=F32) + jnp.dot(matrix, lo, preferred_element_type=F32)
        for k in (0, 1):
            at = slice(y + k * SUB, y + (k + 1) * SUB)
            part = grad[:, k * cols : (k + 1) * cols].reshape(members, SUB, cols)
            old = alpha_ref[:, at, :]
            out_ref[:, at, :] = old - step_length * (old + scale * part)


def final_kernel(groups, scale, *refs):
    others = refs[: groups - 1]
    kron_ref, base_ref, out_ref = refs[groups - 1 :]
    members, rows, cols = base_ref.shape
    for y in range(0, rows, 2 * SUB):
        grad = None
        for g, other in enumerate(others):
            term = jnp.dot(kron_ref[g + 1], pair_of(other, y), preferred_element_type=F32)
            grad = term if grad is None else grad + term
        for k in (0, 1):
            at = slice(y + k * SUB, y + (k + 1) * SUB)
            part = grad[:, k * cols : (k + 1) * cols].reshape(members, SUB, cols)
            out_ref[:, at, :] = base_ref[:, at, :] - (step_length * scale) * part


def to_others(x, groups):
    return [lax.ppermute(x, "ens", [(i, (i - k) % groups) for i in range(groups)]) for k in range(1, groups)]


def body(
    perturbations,
    ens_weights,
    control,
    static_std,
    courant,
    land_mask,
    band_offsets,
    band_weights,
    obs_cells,
    obs_values,
    obs_weights,
):
    own, _, rows, cols = perturbations.shape
    groups = lax.axis_size("ens")
    n_ty, n_tx = lax.axis_size("ty"), lax.axis_size("tx")
    members = own * groups
    steps = obs_cells.shape[2]
    halo = 4 * steps
    reach = -(-2 * steps // 8) * 8
    scale = 1.0 / math.sqrt(members)
    ens_index = lax.axis_index("ens")
    down = [(i, i + 1) for i in range(n_ty - 1)]
    up = [(i + 1, i) for i in range(n_ty - 1)]
    right = [(i, (i + 1) % n_tx) for i in range(n_tx)]
    left = [(j, i) for i, j in right]

    alpha_others = to_others(ens_weights.astype(BF16), groups)

    cells, values, weights = (x.reshape(steps, x.shape[-1]) for x in (obs_cells, obs_values, obs_weights))
    maps, early = call(
        functools.partial(maps_kernel, steps),
        [((2 * steps, rows, cols), F32), ((8, cols), F32)],
        [cells, values, weights, control],
        flops=2 * steps * 4 * rows * cols * cells.shape[1],
        name="maps",
    )
    edge_rows = 2 * steps * reach + 2 * halo
    s_top, s_bottom = call(
        functools.partial(edges_kernel, steps, halo, reach),
        [((edge_rows, cols), F32)] * 2,
        [maps, courant, land_mask],
        name="edges",
    )
    s_above = lax.ppermute(s_bottom, "ty", down)
    s_below = lax.ppermute(s_top, "ty", up)
    s_to_left, s_to_right = call(
        functools.partial(static_pack_kernel, steps, halo, reach),
        [((2, rows + 2 * halo, cols), F32)] * 2,
        [maps, courant, land_mask, s_below, s_above],
        name="static_pack",
    )
    s_from_left = lax.ppermute(s_to_right, "tx", right)
    s_from_right = lax.ppermute(s_to_left, "tx", left)

    offsets = lax.dynamic_slice_in_dim(jnp.concatenate([band_offsets, band_offsets]), ens_index * own, members)
    first = ens_index * own
    index = jnp.arange(members, dtype=jnp.int32)

    def coefficients(shift):
        place = jnp.mod(shift, members)
        return jnp.sum(jnp.where(place[..., None] == index, band_weights, 0.0), axis=-1).astype(BF16)

    to_beta = coefficients(
        first + index[:own][None, :, None] - offsets.reshape(groups, own)[:, None, :]
    )
    to_grad = coefficients(
        first + index.reshape(groups, own)[:, None, :] - offsets[:own][None, :, None]
    )
    wide = own * SUB
    kron_beta, kron_grad, own_share, square = call(
        functools.partial(own_kernel, groups),
        [((groups, wide, wide), BF16)] * 2 + [((3, rows, cols), F32), ((8, cols), F32)],
        [to_beta, to_grad, ens_weights, perturbations],
        name="own",
    )
    (share,) = call(
        functools.partial(share_kernel, groups),
        [((4, rows, cols), F32)],
        [*alpha_others, kron_beta, perturbations, own_share, square],
        name="share",
    )
    if groups == 2:
        (share_other,) = to_others(share, groups)
    else:
        share = lax.psum(share, "ens")
        share_other = jnp.zeros_like(share)
    inc, top, bottom, early = call(
        functools.partial(increment_kernel, scale, halo),
        [((3, rows, cols), F32), ((3, halo, cols), F32), ((3, halo, cols), F32), ((8, cols), F32)],
        [share, share_other, static_std, control, early],
        name="increment",
    )
    above = lax.ppermute(bottom, "ty", down)
    below = lax.ppermute(top, "ty", up)
    to_left, to_right = call(
        functools.partial(pack_kernel, halo),
        [((rows + 2 * halo, cols), F32)] * 2,
        [inc, below, above],
        name="pack",
    )
    from_left = lax.ppermute(to_right, "tx", right)
    from_right = lax.ppermute(to_left, "tx", left)

    ty_index = lax.axis_index("ty")
    side = jnp.stack([ty_index == 0, ty_index == n_ty - 1]).astype(jnp.int32)
    lam, control_new, cost_terms, product = call(
        functools.partial(model_kernel, steps, halo, reach),
        [
            ((3, rows, cols), F32),
            ((3, rows, cols), F32),
            ((n_ty * n_tx * 8, cols), F32),
            ((own, rows, cols), BF16),
        ],
        [
            side,
            inc,
            below,
            above,
            from_right,
            from_left,
            maps,
            courant,
            land_mask,
            s_below,
            s_above,
            s_from_right,
            s_from_left,
            early,
            static_std,
            control,
            perturbations,
        ],
        scratch=[pltpu.VMEM((steps, rows + 2 * halo, 2 * cols), F32)],
        smem=1,
        name="model",
    )
    product_others = to_others(product, groups)
    terms = lax.all_to_all(cost_terms, ("ty", "tx"), 0, 0, tiled=True)
    cost_value = jnp.sum(terms) * (0.5 / ((3 + members) * rows * cols * n_ty * n_tx))
    (base,) = call(
        functools.partial(base_kernel, scale),
        [((own, rows, cols), F32)],
        [kron_grad, ens_weights, perturbations, lam],
        scratch=[pltpu.VMEM((own, rows, cols), F32)],
        name="base",
    )
    (weights_new,) = call(
        functools.partial(final_kernel, groups, scale),
        [((own, rows, cols), F32)],
        [*product_others, kron_grad, base],
        name="final",
    )
    return (control_new, weights_new, cost_value)


def solution(mesh):
    return jax.shard_map(
        body,
        mesh=mesh,
        in_specs=(
            P("ens", None, "ty", "tx"),
            P("ens", "ty", "tx"),
            P(None, "ty", "tx"),
            P(None, "ty", "tx"),
            P("ty", "tx"),
            P("ty", "tx"),
            P(),
            P(),
            P("ty", "tx", None, None),
            P("ty", "tx", None, None),
            P("ty", "tx", None, None),
        ),
        out_specs=(P(None, "ty", "tx"), P("ens", "ty", "tx"), P()),
        check_vma=False,
    )
```

profile of v0, /device:TPU:0, one launch (start us, length us, event | category | flops | bytes accessed | tf_op | source)
XLA Modules:
  0.0 78.2 jit_solution(8122762760417487982)
XLA Ops:
  0.7 1.4 %convert_element_type.13 = bf16[16,128,128]{2,1,0:T(8,128)(2,1)S(1)} convert(f32[16,128,128]{2,1,0:T(8,128)} %alpha_ref.3) | non-fusion elementwise | flops 262144 | bytes 1572864 | tf_op jit(solution)/shard_map/convert_element_type | solution.py:379
  2.1 3.0 %collective-permute-start = (bf16[16,128,128]{2,1,0:T(8,128)(2,1)S(1)}, bf16[16,128,128]{2,1,0:T(8,128)(2,1)S(1)}, u32[]{:S(2)}, u32[]{:S(2)}) collective-permute-start(bf16[16,128,128]{2,1,0:T(8,128)(2,1)S(1)} %convert_element_type.13), channel_id=1, source_target_pairs={{0,16},{16,0},{1,17},{17,1},{2,18},{18,2},{3,19},{19,3},{4,20},{20... | collective-permute-start | bytes 1572872 | tf_op jit(solution)/shard_map/ppermute | solution.py:349
  5.5 0.4 select_reduce_fusion
  5.9 1.2 %copy-done.1 = f32[16,128,128]{2,1,0:T(8,128)S(1)} copy-done((f32[16,128,128]{2,1,0:T(8,128)S(1)}, f32[16,128,128]{2,1,0:T(8,128)}, u32[]{:S(2)}) %copy-start.1) | copy-done | bytes 1048600
  7.1 0.9 %own.1 = (bf16[2,256,256]{2,1,0:T(8,128)(2,1)S(1)}, bf16[2,256,256]{2,1,0:T(8,128)(2,1)S(1)}, f32[3,128,128]{2,1,0:T(8,128)S(1)}, f32[8,128]{1,0:T(8,128)S(1)}) custom-call(bf16[2,16,16]{2,1,0:T(8,128)(2,1)S(1)} %get-tuple-element.44.to_beta_ref, bf16[2,16,16]{2,1,0:T(8,128)(2,1)S(1)} %get-tuple-element.43.to_grad_ref, f32[16,128,128]{2,1,0:T(8,128)S(1)} %copy-done.1, ...), custom_call_target="tpu_custom_call" | custom-call | bytes 3348480 | tf_op jit(solution)/shard_map/own/pallas_call | solution.py:23
  8.1 9.0 %collective-permute-done.refs_0_ = bf16[16,128,128]{2,1,0:T(8,128)(2,1)S(1)} collective-permute-done((bf16[16,128,128]{2,1,0:T(8,128)(2,1)S(1)}, bf16[16,128,128]{2,1,0:T(8,128)(2,1)S(1)}, u32[]{:S(2)}, u32[]{:S(2)}) %collective-permute-start) | collective-permute-done | bytes 524320 | tf_op jit(solution)/shard_map/ppermute | solution.py:349
  17.1 0.5 share.1.own_ref
  17.5 1.8 %collective-permute-start.1 = (f32[4,128,128]{2,1,0:T(8,128)S(1)}, f32[4,128,128]{2,1,0:T(8,128)S(1)}, u32[]{:S(2)}, u32[]{:S(2)}) collective-permute-start(f32[4,128,128]{2,1,0:T(8,128)S(1)} %share.1.own_ref), channel_id=1, source_target_pairs={{0,16},{16,0},{1,17},{17,1},{2,18},{18,2},{3,19},{19,3},{4,20},{20... | collective-permute-start | bytes 786440 | tf_op jit(solution)/shard_map/ppermute | solution.py:349
  19.4 1.2 %maps.1 = (f32[12,128,128]{2,1,0:T(8,128)S(1)}, f32[8,128]{1,0:T(8,128)S(1)}) custom-call(s32[6,512]{1,0:T(8,128)S(1)} %bitcast.12, f32[6,512]{1,0:T(8,128)S(1)} %get-tuple-element.48.values_ref, f32[6,512]{1,0:T(8,128)S(1)} %get-tuple-element.47.weights_ref, f32[3,128,128]{2,1,0:T(8,128)S(1)} %copy-done.10), custom_call_target="tpu_custom_call" | custom-call | flops 402653184 | bytes 1024000 | tf_op jit(solution)/shard_map/maps/pallas_call | solution.py:23
  20.7 1.3 %collective-permute-start.6 = (f32[240,128]{1,0:T(8,128)S(1)}, f32[240,128]{1,0:T(8,128)S(1)}, u32[]{:S(2)}, u32[]{:S(2)}) collective-permute-start(f32[240,128]{1,0:T(8,128)S(1)} %get-tuple-element.33), channel_id=1, source_target_pairs={{4,0},{8,4},{12,8},{5,1},{9,5},{13,9},{6,2},{10,6},{14,10},{7,3},{... | collective-permute-start | bytes 368648 | tf_op jit(solution)/shard_map/ppermute | solution.py:397
  22.0 4.6 %collective-permute-start.7 = (f32[240,128]{1,0:T(8,128)S(1)}, f32[240,128]{1,0:T(8,128)S(1)}, u32[]{:S(2)}, u32[]{:S(2)}) collective-permute-start(f32[240,128]{1,0:T(8,128)S(1)} %get-tuple-element.34), channel_id=1, source_target_pairs={{0,4},{4,8},{8,12},{1,5},{5,9},{9,13},{2,6},{6,10},{10,14},{3,7},{... | collective-permute-start | bytes 368648 | tf_op jit(solution)/shard_map/ppermute | solution.py:396
  26.5 0.9 %collective-permute-done.6.below_ref.s_below_ref = f32[240,128]{1,0:T(8,128)S(1)} collective-permute-done((f32[240,128]{1,0:T(8,128)S(1)}, f32[240,128]{1,0:T(8,128)S(1)}, u32[]{:S(2)}, u32[]{:S(2)}) %collective-permute-start.6) | collective-permute-done | bytes 122912 | tf_op jit(solution)/shard_map/ppermute | solution.py:397
  27.4 1.5 %collective-permute-done.7.above_ref.s_above_ref = f32[240,128]{1,0:T(8,128)S(1)} collective-permute-done((f32[240,128]{1,0:T(8,128)S(1)}, f32[240,128]{1,0:T(8,128)S(1)}, u32[]{:S(2)}, u32[]{:S(2)}) %collective-permute-start.7) | collective-permute-done | bytes 122912 | tf_op jit(solution)/shard_map/ppermute | solution.py:396
  28.9 0.6 static_pack.1
  29.6 0.5 collective-permute-start.9
  30.1 0.7 increment.1
  30.8 1.3 %collective-permute-start.2 = (f32[3,24,128]{2,1,0:T(8,128)}, f32[3,24,128]{2,1,0:T(8,128)S(1)}, u32[]{:S(2)}, u32[]{:S(2)}) collective-permute-start(f32[3,24,128]{2,1,0:T(8,128)} %get-tuple-element.28), channel_id=1, source_target_pairs={{4,0},{8,4},{12,8},{5,1},{9,5},{13,9},{6,2},{10,6},{14,10},{7,3},{... | collective-permute-start | bytes 110600 | tf_op jit(solution)/shard_map/ppermute | solution.py:446
  32.1 5.0 %collective-permute-start.3 = (f32[3,24,128]{2,1,0:T(8,128)S(1)}, f32[3,24,128]{2,1,0:T(8,128)S(1)}, u32[]{:S(2)}, u32[]{:S(2)}) collective-permute-start(f32[3,24,128]{2,1,0:T(8,128)S(1)} %get-tuple-element.29), channel_id=1, source_target_pairs={{0,4},{4,8},{8,12},{1,5},{5,9},{9,13},{2,6},{6,10},{10,14},{3,7},{... | collective-permute-start | bytes 110600 | tf_op jit(solution)/shard_map/ppermute | solution.py:445
  37.0 0.2 collective-permute-done.2.below_ref
  37.2 1.5 %collective-permute-done.3.above_ref = f32[3,24,128]{2,1,0:T(8,128)S(1)} collective-permute-done((f32[3,24,128]{2,1,0:T(8,128)S(1)}, f32[3,24,128]{2,1,0:T(8,128)S(1)}, u32[]{:S(2)}, u32[]{:S(2)}) %collective-permute-start.3) | collective-permute-done | bytes 36896 | tf_op jit(solution)/shard_map/ppermute | solution.py:445
  38.7 0.2 pack.1
  38.9 0.5 collective-permute-start.4
  39.5 0.7 copy-done.22
  40.2 0.7 copy-done.24
  40.9 0.6 collective-permute-done.4.from_right_ref
  41.4 2.7 %collective-permute-done.5.from_left_ref = f32[176,128]{1,0:T(8,128)S(1)} collective-permute-done((f32[176,128]{1,0:T(8,128)S(1)}, f32[176,128]{1,0:T(8,128)S(1)}, u32[]{:S(2)}, u32[]{:S(2)}) %collective-permute-start.5) | collective-permute-done | bytes 90144 | tf_op jit(solution)/shard_map/ppermute | solution.py:453
  44.2 0.9 %copy-done.9 = f32[3,128,128]{2,1,0:T(8,128)S(1)} copy-done((f32[3,128,128]{2,1,0:T(8,128)S(1)}, f32[3,128,128]{2,1,0:T(8,128)}, u32[]{:S(2)}) %copy-start.9) | copy-done | bytes 196632
  45.1 0.9 %copy-done.11 = f32[3,128,128]{2,1,0:T(8,128)S(1)} copy-done((f32[3,128,128]{2,1,0:T(8,128)S(1)}, f32[3,128,128]{2,1,0:T(8,128)}, u32[]{:S(2)}) %copy-start.11) | copy-done | bytes 196632
  46.0 0.9 %copy-done.13 = f32[3,128,128]{2,1,0:T(8,128)S(1)} copy-done((f32[3,128,128]{2,1,0:T(8,128)S(1)}, f32[3,128,128]{2,1,0:T(8,128)}, u32[]{:S(2)}) %copy-start.13) | copy-done | bytes 196632
  46.9 0.9 %copy-done.17 = f32[240,128]{1,0:T(8,128)S(1)} copy-done((f32[240,128]{1,0:T(8,128)S(1)}, f32[240,128]{1,0:T(8,128)}, u32[]{:S(2)}) %copy-start.17) | copy-done | bytes 122904
  47.8 0.9 %copy-done.19 = f32[240,128]{1,0:T(8,128)S(1)} copy-done((f32[240,128]{1,0:T(8,128)S(1)}, f32[240,128]{1,0:T(8,128)}, u32[]{:S(2)}) %copy-start.19) | copy-done | bytes 122904
  48.7 0.9 %copy-done.23 = f32[2,176,128]{2,1,0:T(8,128)S(1)} copy-done((f32[2,176,128]{2,1,0:T(8,128)S(1)}, f32[2,176,128]{2,1,0:T(8,128)}, u32[]{:S(2)}) %copy-start.23) | copy-done | bytes 180248
  49.7 0.9 %copy-done.25 = f32[2,176,128]{2,1,0:T(8,128)S(1)} copy-done((f32[2,176,128]{2,1,0:T(8,128)S(1)}, f32[2,176,128]{2,1,0:T(8,128)}, u32[]{:S(2)}) %copy-start.25) | copy-done | bytes 180248
  50.6 0.8 copy-done.27
  51.4 0.8 copy-done.29
  52.1 6.2 %model.1 = (f32[3,128,128]{2,1,0:T(8,128)S(1)}, f32[3,128,128]{2,1,0:T(8,128)}, f32[128,128]{1,0:T(8,128)S(1)}, bf16[16,128,128]{2,1,0:T(8,128)(2,1)}) custom-call(s32[2]{0:T(128)S(1)} %add_convert_fusion.side_ref, f32[3,128,128]{2,1,0:T(8,128)S(1)} %copy-done.13, f32[3,24,128]{2,1,0:T(8,128)S(1)} %copy-done.27, f32[3,24,128]{2,1,0:T(8,128)S(1)} %copy-done.29, ...), custom_call_target="tpu_custom_call" | custom-call | bytes 4927496 | tf_op jit(solution)/shard_map/model/pallas_call | solution.py:23
  58.3 0.7 copy-done.20
  59.0 0.6 copy-done.30
  59.6 0.2 collective-permute-start.10
  59.8 6.6 %all-to-all-start = ((f32[16,8,128]{2,1,0:T(8,128)}), f32[16,8,128]{2,1,0:T(8,128)S(1)}, u32[]{:S(2)}, u32[]{:S(2)}) async-start(f32[16,8,128]{2,1,0:T(8,128)} %bitcast.11), calls=%async_computation | async-start | bytes 131072 | tf_op jit(solution)/shard_map/all_to_all | solution.py:490
  66.4 0.9 %copy-done.6 = bf16[2,256,256]{2,1,0:T(8,128)(2,1)S(1)} copy-done((bf16[2,256,256]{2,1,0:T(8,128)(2,1)S(1)}, bf16[2,256,256]{2,1,0:T(8,128)(2,1)}, u32[]{:S(2)}) %copy-start.6) | copy-done | bytes 262168
  67.3 0.9 %copy-done.21 = f32[3,128,128]{2,1,0:T(8,128)S(1)} copy-done((f32[3,128,128]{2,1,0:T(8,128)S(1)}, f32[3,128,128]{2,1,0:T(8,128)}, u32[]{:S(2)}) %copy-start.21) | copy-done | bytes 196632
  68.2 0.7 base.1.refs_2_
  69.0 1.0 %copy-done.3 = f32[16,128,128]{2,1,0:T(8,128)} copy-done((f32[16,128,128]{2,1,0:T(8,128)}, f32[16,128,128]{2,1,0:T(8,128)S(1)}, u32[]{:S(2)}) %copy-start.3) | copy-done | bytes 1048600
  69.9 3.3 %all-to-all-done = f32[16,8,128]{2,1,0:T(8,128)S(1)} async-done(((f32[16,8,128]{2,1,0:T(8,128)}), f32[16,8,128]{2,1,0:T(8,128)S(1)}, u32[]{:S(2)}, u32[]{:S(2)}) %all-to-all-start) | async-done | bytes 65568 | tf_op jit(solution)/shard_map/all_to_all | solution.py:490
  73.3 0.6 reduce_sum.29
  74.6 1.2 %copy-done.4 = f32[16,128,128]{2,1,0:T(8,128)S(1)} copy-done((f32[16,128,128]{2,1,0:T(8,128)S(1)}, f32[16,128,128]{2,1,0:T(8,128)}, u32[]{:S(2)}) %copy-start.4) | copy-done | bytes 1048600
  75.8 1.3 %final.1 = f32[16,128,128]{2,1,0:T(8,128)} custom-call(bf16[16,128,128]{2,1,0:T(8,128)(2,1)S(1)} %collective-permute-done.10.refs_0_, bf16[2,256,256]{2,1,0:T(8,128)(2,1)S(1)} %copy-done.7, f32[16,128,128]{2,1,0:T(8,128)S(1)} %copy-done.4), custom_call_target="tpu_custom_call" | custom-call | bytes 2883584 | tf_op jit(solution)/shard_map/final/pallas_call | solution.py:23
  (71 shorter events, 0.7 us)
Async XLA Ops:
  0.6 4.5 %copy-start.35 = (s32[32]{0:T(128)S(1)}, s32[32]{0:T(128)}, u32[]{:S(2)}) copy-start(s32[32]{0:T(128)} %param.17) | copy-start | bytes 388
  0.6 4.8 %copy-start.34 = (f32[32]{0:T(128)S(1)}, f32[32]{0:T(128)}, u32[]{:S(2)}) copy-start(f32[32]{0:T(128)} %param.18) | copy-start | bytes 388
  0.7 5.2 %copy-start = (bf16[16,3,128,128]{3,2,1,0:T(8,128)(2,1)S(1)}, bf16[16,3,128,128]{3,2,1,0:T(8,128)(2,1)}, u32[]{:S(2)}) copy-start(bf16[16,3,128,128]{3,2,1,0:T(8,128)(2,1)} %perturbations_ref.5) | copy-start | bytes 4718596
  2.1 15.0 %collective-permute-start = (bf16[16,128,128]{2,1,0:T(8,128)(2,1)S(1)}, bf16[16,128,128]{2,1,0:T(8,128)(2,1)S(1)}, u32[]{:S(2)}, u32[]{:S(2)}) collective-permute-start(bf16[16,128,128]{2,1,0:T(8,128)(2,1)S(1)} %convert_element_type.13), channel_id=1, source_target_pairs={{0,16},{16,0},{1,17},{17,1},{2,18},{18,2},{3,19},{19,3},{4,20},{20... | collective-permute-start | bytes 1572872 | tf_op jit(solution)/shard_map/ppermute | solution.py:349
  5.9 1.2 %copy-start.1 = (f32[16,128,128]{2,1,0:T(8,128)S(1)}, f32[16,128,128]{2,1,0:T(8,128)}, u32[]{:S(2)}) copy-start(f32[16,128,128]{2,1,0:T(8,128)} %alpha_ref.3) | copy-start | bytes 3145732
  8.0 12.6 %copy-start.5 = (bf16[2,256,256]{2,1,0:T(8,128)(2,1)}, bf16[2,256,256]{2,1,0:T(8,128)(2,1)S(1)}, u32[]{:S(2)}) copy-start(bf16[2,256,256]{2,1,0:T(8,128)(2,1)S(1)} %get-tuple-element.40.kron_ref.refs_1_) | copy-start | bytes 786436
  8.1 11.3 %copy-start.31 = (f32[1,1,6,512]{3,1,2,0:T(1,128)S(1)}, f32[1,1,6,512]{3,1,2,0:T(1,128)}, u32[]{:S(2)}) copy-start(f32[1,1,6,512]{3,1,2,0:T(1,128)} %param.21) | copy-start | bytes 36868
  8.1 11.3 %copy-start.32 = (f32[1,1,6,512]{3,1,2,0:T(1,128)S(1)}, f32[1,1,6,512]{3,1,2,0:T(1,128)}, u32[]{:S(2)}) copy-start(f32[1,1,6,512]{3,1,2,0:T(1,128)} %param.20) | copy-start | bytes 36868
  8.1 11.3 %copy-start.33 = (s32[1,1,6,512]{3,1,2,0:T(1,128)S(1)}, s32[1,1,6,512]{3,1,2,0:T(1,128)}, u32[]{:S(2)}) copy-start(s32[1,1,6,512]{3,1,2,0:T(1,128)} %param.19) | copy-start | bytes 36868
  8.1 11.3 %copy-start.10 = (f32[3,128,128]{2,1,0:T(8,128)S(1)}, f32[3,128,128]{2,1,0:T(8,128)}, u32[]{:S(2)}) copy-start(f32[3,128,128]{2,1,0:T(8,128)} %control_ref.5) | copy-start | bytes 589828
  17.1 3.6 %copy-start.14 = (f32[128,128]{1,0:T(8,128)S(1)}, f32[128,128]{1,0:T(8,128)}, u32[]{:S(2)}) copy-start(f32[128,128]{1,0:T(8,128)} %courant_ref.5) | copy-start | bytes 196612
  17.1 3.6 %copy-start.15 = (s32[128,128]{1,0:T(8,128)S(1)}, s32[128,128]{1,0:T(8,128)}, u32[]{:S(2)}) copy-start(s32[128,128]{1,0:T(8,128)} %mask_ref.5) | copy-start | bytes 196612
  17.5 12.5 %collective-permute-start.1 = (f32[4,128,128]{2,1,0:T(8,128)S(1)}, f32[4,128,128]{2,1,0:T(8,128)S(1)}, u32[]{:S(2)}, u32[]{:S(2)}) collective-permute-start(f32[4,128,128]{2,1,0:T(8,128)S(1)} %share.1.own_ref), channel_id=1, source_target_pairs={{0,16},{16,0},{1,17},{17,1},{2,18},{18,2},{3,19},{19,3},{4,20},{20... | collective-permute-start | bytes 786440 | tf_op jit(solution)/shard_map/ppermute | solution.py:349
  19.4 10.7 %copy-start.8 = (f32[3,128,128]{2,1,0:T(8,128)S(1)}, f32[3,128,128]{2,1,0:T(8,128)}, u32[]{:S(2)}) copy-start(f32[3,128,128]{2,1,0:T(8,128)} %std_ref.3) | copy-start | bytes 589828
  20.7 6.8 %collective-permute-start.6 = (f32[240,128]{1,0:T(8,128)S(1)}, f32[240,128]{1,0:T(8,128)S(1)}, u32[]{:S(2)}, u32[]{:S(2)}) collective-permute-start(f32[240,128]{1,0:T(8,128)S(1)} %get-tuple-element.33), channel_id=1, source_target_pairs={{4,0},{8,4},{12,8},{5,1},{9,5},{13,9},{6,2},{10,6},{14,10},{7,3},{... | collective-permute-start | bytes 368648 | tf_op jit(solution)/shard_map/ppermute | solution.py:397
  22.0 7.0 %collective-permute-start.7 = (f32[240,128]{1,0:T(8,128)S(1)}, f32[240,128]{1,0:T(8,128)S(1)}, u32[]{:S(2)}, u32[]{:S(2)}) collective-permute-start(f32[240,128]{1,0:T(8,128)S(1)} %get-tuple-element.34), channel_id=1, source_target_pairs={{0,4},{4,8},{8,12},{1,5},{5,9},{9,13},{2,6},{6,10},{10,14},{3,7},{... | collective-permute-start | bytes 368648 | tf_op jit(solution)/shard_map/ppermute | solution.py:396
  27.4 3.3 %copy-start.16 = (f32[240,128]{1,0:T(8,128)}, f32[240,128]{1,0:T(8,128)S(1)}, u32[]{:S(2)}) copy-start(f32[240,128]{1,0:T(8,128)S(1)} %collective-permute-done.6.below_ref.s_below_ref) | copy-start | bytes 368644
  28.9 1.2 %copy-start.18 = (f32[240,128]{1,0:T(8,128)}, f32[240,128]{1,0:T(8,128)S(1)}, u32[]{:S(2)}) copy-start(f32[240,128]{1,0:T(8,128)S(1)} %collective-permute-done.7.above_ref.s_above_ref) | copy-start | bytes 368644
  29.5 10.0 %collective-permute-start.8 = (f32[2,176,128]{2,1,0:T(8,128)S(1)}, f32[2,176,128]{2,1,0:T(8,128)S(1)}, u32[]{:S(2)}, u32[]{:S(2)}) collective-permute-start(f32[2,176,128]{2,1,0:T(8,128)S(1)} %get-tuple-element.35), channel_id=1, source_target_pairs={{1,0},{2,1},{3,2},{0,3},{5,4},{6,5},{7,6},{4,7},{9,8},{10,9},{11,1... | collective-permute-start | bytes 540680 | tf_op jit(solution)/shard_map/ppermute | solution.py:405
  29.6 10.6 %collective-permute-start.9 = (f32[2,176,128]{2,1,0:T(8,128)S(1)}, f32[2,176,128]{2,1,0:T(8,128)S(1)}, u32[]{:S(2)}, u32[]{:S(2)}) collective-permute-start(f32[2,176,128]{2,1,0:T(8,128)S(1)} %get-tuple-element.36), channel_id=1, source_target_pairs={{0,1},{1,2},{2,3},{3,0},{4,5},{5,6},{6,7},{7,4},{8,9},{9,10},{10,1... | collective-permute-start | bytes 540680 | tf_op jit(solution)/shard_map/ppermute | solution.py:404
  30.8 13.4 %copy-start.12 = (f32[3,128,128]{2,1,0:T(8,128)}, f32[3,128,128]{2,1,0:T(8,128)S(1)}, u32[]{:S(2)}) copy-start(f32[3,128,128]{2,1,0:T(8,128)S(1)} %get-tuple-element.27.inc_ref) | copy-start | bytes 589828
  30.8 6.5 %collective-permute-start.2 = (f32[3,24,128]{2,1,0:T(8,128)}, f32[3,24,128]{2,1,0:T(8,128)S(1)}, u32[]{:S(2)}, u32[]{:S(2)}) collective-permute-start(f32[3,24,128]{2,1,0:T(8,128)} %get-tuple-element.28), channel_id=1, source_target_pairs={{4,0},{8,4},{12,8},{5,1},{9,5},{13,9},{6,2},{10,6},{14,10},{7,3},{... | collective-permute-start | bytes 110600 | tf_op jit(solution)/shard_map/ppermute | solution.py:446
  32.1 6.6 %collective-permute-start.3 = (f32[3,24,128]{2,1,0:T(8,128)S(1)}, f32[3,24,128]{2,1,0:T(8,128)S(1)}, u32[]{:S(2)}, u32[]{:S(2)}) collective-permute-start(f32[3,24,128]{2,1,0:T(8,128)S(1)} %get-tuple-element.29), channel_id=1, source_target_pairs={{0,4},{4,8},{8,12},{1,5},{5,9},{9,13},{2,6},{6,10},{10,14},{3,7},{... | collective-permute-start | bytes 110600 | tf_op jit(solution)/shard_map/ppermute | solution.py:445
  37.2 6.9 %copy-start.26 = (f32[3,24,128]{2,1,0:T(8,128)}, f32[3,24,128]{2,1,0:T(8,128)S(1)}, u32[]{:S(2)}) copy-start(f32[3,24,128]{2,1,0:T(8,128)S(1)} %collective-permute-done.2.below_ref) | copy-start | bytes 110596
  38.7 5.5 %copy-start.28 = (f32[3,24,128]{2,1,0:T(8,128)}, f32[3,24,128]{2,1,0:T(8,128)S(1)}, u32[]{:S(2)}) copy-start(f32[3,24,128]{2,1,0:T(8,128)S(1)} %collective-permute-done.3.above_ref) | copy-start | bytes 110596
  38.9 2.6 %collective-permute-start.4 = (f32[176,128]{1,0:T(8,128)S(1)}, f32[176,128]{1,0:T(8,128)S(1)}, u32[]{:S(2)}, u32[]{:S(2)}) collective-permute-start(f32[176,128]{1,0:T(8,128)S(1)} %get-tuple-element.30), channel_id=1, source_target_pairs={{1,0},{2,1},{3,2},{0,3},{5,4},{6,5},{7,6},{4,7},{9,8},{10,9},{11,1... | collective-permute-start | bytes 270344 | tf_op jit(solution)/shard_map/ppermute | solution.py:454
  39.3 4.8 %collective-permute-start.5 = (f32[176,128]{1,0:T(8,128)S(1)}, f32[176,128]{1,0:T(8,128)S(1)}, u32[]{:S(2)}, u32[]{:S(2)}) collective-permute-start(f32[176,128]{1,0:T(8,128)S(1)} %get-tuple-element.31), channel_id=1, source_target_pairs={{0,1},{1,2},{2,3},{3,0},{4,5},{5,6},{6,7},{7,4},{8,9},{9,10},{10,1... | collective-permute-start | bytes 270344 | tf_op jit(solution)/shard_map/ppermute | solution.py:453
  39.5 0.7 copy-start.22
  40.2 0.7 copy-start.24
  44.2 0.9 %copy-start.9 = (f32[3,128,128]{2,1,0:T(8,128)S(1)}, f32[3,128,128]{2,1,0:T(8,128)}, u32[]{:S(2)}) copy-start(f32[3,128,128]{2,1,0:T(8,128)} %std_ref.3) | copy-start | bytes 589828
  45.1 0.9 %copy-start.11 = (f32[3,128,128]{2,1,0:T(8,128)S(1)}, f32[3,128,128]{2,1,0:T(8,128)}, u32[]{:S(2)}) copy-start(f32[3,128,128]{2,1,0:T(8,128)} %control_ref.5) | copy-start | bytes 589828
  46.0 0.9 %copy-start.13 = (f32[3,128,128]{2,1,0:T(8,128)S(1)}, f32[3,128,128]{2,1,0:T(8,128)}, u32[]{:S(2)}) copy-start(f32[3,128,128]{2,1,0:T(8,128)} %copy-done.12) | copy-start | bytes 589828
  46.9 0.9 %copy-start.17 = (f32[240,128]{1,0:T(8,128)S(1)}, f32[240,128]{1,0:T(8,128)}, u32[]{:S(2)}) copy-start(f32[240,128]{1,0:T(8,128)} %copy-done.16) | copy-start | bytes 368644
  47.8 0.9 %copy-start.19 = (f32[240,128]{1,0:T(8,128)S(1)}, f32[240,128]{1,0:T(8,128)}, u32[]{:S(2)}) copy-start(f32[240,128]{1,0:T(8,128)} %copy-done.18) | copy-start | bytes 368644
  48.7 0.9 %copy-start.23 = (f32[2,176,128]{2,1,0:T(8,128)S(1)}, f32[2,176,128]{2,1,0:T(8,128)}, u32[]{:S(2)}) copy-start(f32[2,176,128]{2,1,0:T(8,128)} %copy-done.22) | copy-start | bytes 540676
  49.7 0.9 %copy-start.25 = (f32[2,176,128]{2,1,0:T(8,128)S(1)}, f32[2,176,128]{2,1,0:T(8,128)}, u32[]{:S(2)}) copy-start(f32[2,176,128]{2,1,0:T(8,128)} %copy-done.24) | copy-start | bytes 540676
  50.6 0.8 copy-start.27
  51.4 0.8 copy-start.29
  52.1 14.2 %copy-start.2 = (f32[16,128,128]{2,1,0:T(8,128)S(1)}, f32[16,128,128]{2,1,0:T(8,128)}, u32[]{:S(2)}) copy-start(f32[16,128,128]{2,1,0:T(8,128)} %alpha_ref.3) | copy-start | bytes 3145732
  58.3 0.7 copy-start.20
  59.0 0.6 copy-start.30
  59.6 14.9 %collective-permute-start.10 = (bf16[16,128,128]{2,1,0:T(8,128)(2,1)}, bf16[16,128,128]{2,1,0:T(8,128)(2,1)S(1)}, u32[]{:S(2)}, u32[]{:S(2)}) collective-permute-start(bf16[16,128,128]{2,1,0:T(8,128)(2,1)} %get-tuple-element.39), channel_id=1, source_target_pairs={{0,16},{16,0},{1,17},{17,1},{2,18},{18,2},{3,19},{19,3},{4,20},{20... | collective-permute-start | bytes 1572872 | tf_op jit(solution)/shard_map/ppermute | solution.py:349
  59.8 13.5 %all-to-all-start = ((f32[16,8,128]{2,1,0:T(8,128)}), f32[16,8,128]{2,1,0:T(8,128)S(1)}, u32[]{:S(2)}, u32[]{:S(2)}) async-start(f32[16,8,128]{2,1,0:T(8,128)} %bitcast.11), calls=%async_computation | async-start | bytes 131072 | tf_op jit(solution)/shard_map/all_to_all | solution.py:490
  66.4 1.0 %copy-start.6 = (bf16[2,256,256]{2,1,0:T(8,128)(2,1)S(1)}, bf16[2,256,256]{2,1,0:T(8,128)(2,1)}, u32[]{:S(2)}) copy-start(bf16[2,256,256]{2,1,0:T(8,128)(2,1)} %copy-done.5) | copy-start | bytes 786436
  67.3 0.9 %copy-start.21 = (f32[3,128,128]{2,1,0:T(8,128)S(1)}, f32[3,128,128]{2,1,0:T(8,128)}, u32[]{:S(2)}) copy-start(f32[3,128,128]{2,1,0:T(8,128)} %copy-done.20) | copy-start | bytes 589828
  68.2 6.3 %copy-start.7 = (bf16[2,256,256]{2,1,0:T(8,128)(2,1)S(1)}, bf16[2,256,256]{2,1,0:T(8,128)(2,1)}, u32[]{:S(2)}) copy-start(bf16[2,256,256]{2,1,0:T(8,128)(2,1)} %copy-done.5) | copy-start | bytes 786436
  68.9 1.0 %copy-start.3 = (f32[16,128,128]{2,1,0:T(8,128)}, f32[16,128,128]{2,1,0:T(8,128)S(1)}, u32[]{:S(2)}) copy-start(f32[16,128,128]{2,1,0:T(8,128)S(1)} %base.1.refs_2_) | copy-start | bytes 3145732
  74.5 1.2 %copy-start.4 = (f32[16,128,128]{2,1,0:T(8,128)S(1)}, f32[16,128,128]{2,1,0:T(8,128)}, u32[]{:S(2)}) copy-start(f32[16,128,128]{2,1,0:T(8,128)} %copy-done.3) | copy-start | bytes 3145732
where the time goes:
time: 78.9 us; the launch traced here: 78.2 us
  starting transfers between devices  24.8 us (31%)
  waiting for transfers between devices  19.6 us (25%)
  local copies, waits for them, and re-layouts  16.1 us (20%)
  Pallas kernels  12.1 us (15%)
  between operations  2.78 us (4%)
  other arithmetic  2.69 us (3%)
    unnamed x74, local copies, waits for them, and re-layouts  16 us
    pallas_call x10, Pallas kernels, call(): pl.pallas_call(kernel, out_shape=out_shape, in_specs=[SMEM] * smem + [VME...  12.1 us
    ppermute x3, waiting for transfers between devices, to_others(): lax.ppermute(x, 'ens', [(i, (i - k) % groups) for i in range(groups)])  8.96 us
    all_to_all x1, starting transfers between devices, body(): terms = lax.all_to_all(cost_terms, ('ty', 'tx'), 0, 0, tiled=True)  6.59 us
    ppermute x3, starting transfers between devices, to_others(): lax.ppermute(x, 'ens', [(i, (i - k) % groups) for i in range(groups)])  5.01 us
    ppermute x1, starting transfers between devices, body(): above = lax.ppermute(bottom, 'ty', down)  4.97 us
    ppermute x1, starting transfers between devices, body(): s_above = lax.ppermute(s_bottom, 'ty', down)  4.55 us
    all_to_all x1, waiting for transfers between devices, body(): terms = lax.all_to_all(cost_terms, ('ty', 'tx'), 0, 0, tiled=True)  3.33 us
  transfers between devices with their start and end apart: 12, of which 8 were waited for; matrix products, arithmetic and copies ran while one was open for 2% of the time, Pallas kernels for 5%

commit v1 on v0

v1 whole, which is shorter than its diff:
```python
import functools
import math

import jax
import jax.numpy as jnp
from jax import lax
from jax.experimental import pallas as pl
from jax.experimental.pallas import tpu as pltpu
from jax.sharding import PartitionSpec as P

step_length = 0.25
SUB = 16
UNIT = 2 * SUB
PIECES = 3
F32 = jnp.float32
BF16 = jnp.bfloat16
VMEM = pl.BlockSpec(memory_space=pltpu.VMEM)
SMEM = pl.BlockSpec(memory_space=pltpu.SMEM)
HBM = pl.BlockSpec(memory_space=pltpu.HBM)


def call(kernel, outs, ins, scratch=(), smem=0, flops=0, name=None, mib=4, out_specs=None, in_specs=None, grid=()):
    out_shape = [jax.ShapeDtypeStruct(s, d) for s, d in outs]
    moved = sum(math.prod(s) * jnp.dtype(d).itemsize for s, d in outs)
    moved += sum(x.size * x.dtype.itemsize for x in ins)
    return pl.pallas_call(
        kernel,
        out_shape=out_shape,
        grid=grid,
        in_specs=in_specs or [SMEM] * smem + [VMEM] * (len(ins) - smem),
        out_specs=out_specs or [VMEM] * len(outs),
        scratch_shapes=list(scratch),
        compiler_params=pltpu.CompilerParams(vmem_limit_bytes=mib * 1024 * 1024),
        cost_estimate=pl.CostEstimate(flops=flops, bytes_accessed=moved, transcendentals=0),
        name=name,
    )(*ins)


def split(x):
    hi = x.astype(BF16)
    return hi, (x - hi.astype(F32)).astype(BF16)


def folded(x):
    cols = x.shape[-1]
    return jnp.sum(x.reshape(-1, 8, cols), axis=0)


def maps_kernel(steps, cells_ref, values_ref, weights_ref, control_ref, maps_ref, cost_ref):
    rows, cols = maps_ref.shape[1:]
    count = cells_ref.shape[1]
    shift = cols.bit_length() - 1
    row_iota = lax.broadcasted_iota(jnp.int32, (rows, count), 0)
    col_iota = lax.broadcasted_iota(jnp.int32, (cols, count), 0)
    for t in range(steps):
        cells = cells_ref[t : t + 1, :]
        weight = weights_ref[t : t + 1, :]
        product = weight * values_ref[t : t + 1, :]
        at_row = jnp.where(row_iota == (cells >> shift), 1.0, 0.0).astype(BF16)
        hit = col_iota == (cells & (cols - 1))
        parts = []
        for value in (weight, product):
            for piece in split(value):
                parts.append(jnp.where(hit, piece.astype(F32), 0.0).astype(BF16))
        sums = lax.dot_general(
            at_row,
            jnp.concatenate(parts, axis=0),
            (((1,), (1,)), ((), ())),
            preferred_element_type=F32,
        )
        maps_ref[t] = sums[:, :cols] + sums[:, cols : 2 * cols]
        maps_ref[steps + t] = sums[:, 2 * cols : 3 * cols] + sums[:, 3 * cols :]
    value = values_ref[...]
    fixed = jnp.sum(weights_ref[...] * value * value, axis=0, keepdims=True)
    line = sum(fixed[:, k : k + cols] for k in range(0, count, cols))
    first = lax.broadcasted_iota(jnp.int32, (8, cols), 0) == 0
    control = control_ref[...]
    cost_ref[...] = folded(control * control) + jnp.where(first, line, 0.0)


def send_kernel(chunk, alpha_ref, *refs):
    out_ref, rows_ref, sems = refs[-3:]
    copies = []
    for n, y in enumerate(chunk):
        at = slice(n * UNIT, (n + 1) * UNIT)
        copies.append(pltpu.make_async_copy(alpha_ref.at[:, y : y + UNIT, :], rows_ref.at[:, at, :], sems.at[n]))
        copies[-1].start()
    for n, copy in enumerate(copies):
        at = slice(n * UNIT, (n + 1) * UNIT)
        copy.wait()
        out_ref[:, at, :] = rows_ref[:, at, :].astype(BF16)


def expand(small):
    rows, cols = small.shape
    left = lax.broadcasted_iota(jnp.int32, (rows * SUB, rows), 0) // SUB
    left = (left == lax.broadcasted_iota(jnp.int32, (rows * SUB, rows), 1)).astype(F32).astype(BF16)
    right = lax.broadcasted_iota(jnp.int32, (cols, cols * SUB), 1) // SUB
    right = (right == lax.broadcasted_iota(jnp.int32, (cols, cols * SUB), 0)).astype(F32).astype(BF16)
    wide = jnp.dot(small, right, preferred_element_type=F32).astype(BF16)
    full = jnp.dot(left, wide, preferred_element_type=F32)
    row = lax.broadcasted_iota(jnp.int32, full.shape, 0) % SUB
    col = lax.broadcasted_iota(jnp.int32, full.shape, 1) % SUB
    return jnp.where(row == col, full, 0.0).astype(BF16)


def coefficients(own, members, axis, first_row, first_col, offsets_ref, weights_ref):
    shape = (own, own)
    row_place = lax.broadcasted_iota(jnp.int32, shape, axis)
    column = first_col + lax.broadcasted_iota(jnp.int32, shape, 1 - axis)
    shift = jnp.zeros(shape, jnp.int32)
    for j in range(own):
        shift = jnp.where(row_place == j, offsets_ref[first_row + j], shift)
    place = column - shift
    place = jnp.where(place < 0, place + members, place)
    value = jnp.zeros(shape, F32)
    for k in range(members):
        value = jnp.where(place == k, weights_ref[k], value)
    return value.astype(BF16)


def pair_of(ref, y):
    members, _, cols = ref.shape
    blocks = [ref[:, y + k * SUB : y + (k + 1) * SUB, :].reshape(members * SUB, cols) for k in (0, 1)]
    return jnp.concatenate(blocks, axis=1)


def shares(beta, perturbations_ref, y):
    members = perturbations_ref.shape[0]
    cols = perturbations_ref.shape[3]
    for k in (0, 1):
        part = beta[:, k * cols : (k + 1) * cols].reshape(members, SUB, cols)
        at = y + k * SUB
        for c in range(3):
            total = part[0] * perturbations_ref[0, c, at : at + SUB, :].astype(F32)
            for i in range(1, members):
                total = total + part[i] * perturbations_ref[i, c, at : at + SUB, :].astype(F32)
            yield k * SUB, c, total


def own_kernel(
    groups,
    place_ref,
    offsets_ref,
    weights_ref,
    alpha_hbm_ref,
    perturbations_ref,
    kron_beta_ref,
    kron_grad_ref,
    share_ref,
    square_ref,
    alpha_ref,
    sem,
):
    own, rows, cols = alpha_ref.shape
    load = pltpu.make_async_copy(alpha_hbm_ref, alpha_ref, sem)
    load.start()
    members = own * groups
    first = place_ref[2] * own
    for g in range(groups):
        other = lax.rem(place_ref[2] + g, groups) * own
        kron_beta_ref[g] = expand(coefficients(own, members, 1, other, first, offsets_ref, weights_ref))
        kron_grad_ref[g] = expand(coefficients(own, members, 0, first, other, offsets_ref, weights_ref))
    load.wait()
    matrix = kron_beta_ref[0]
    square = jnp.zeros((8, cols), F32)
    for y in range(0, rows, UNIT):
        alpha = pair_of(alpha_ref, y)
        square = square + folded(alpha[:, :cols] * alpha[:, :cols]) + folded(alpha[:, cols:] * alpha[:, cols:])
        hi, lo = split(alpha)
        beta = jnp.dot(matrix, hi, preferred_element_type=F32) + jnp.dot(matrix, lo, preferred_element_type=F32)
        for at, c, total in shares(beta, perturbations_ref, y):
            share_ref[c, y + at : y + at + SUB, :] = total
    for k in range(PIECES):
        piece = square.astype(BF16).astype(F32)
        square = square - piece
        square_ref[k * SUB : (k + 1) * SUB, :] = jnp.concatenate([piece, jnp.zeros_like(square)], axis=0).astype(BF16)


def share_kernel(groups, units, *refs):
    others = refs[: groups - 1]
    kron_ref, perturbations_ref, own_ref, out_ref = refs[groups - 1 :]
    height = len(units) * UNIT
    for n, y in enumerate(units):
        beta = None
        for g, other in enumerate(others):
            term = jnp.dot(kron_ref[g + 1], pair_of(other, n * UNIT), preferred_element_type=F32)
            beta = term if beta is None else beta + term
        for at, c, total in shares(beta, perturbations_ref, y):
            total = total + own_ref[c, y + at : y + at + SUB, :]
            to = c * height + n * UNIT + at
            out_ref[to : to + SUB, :] = total.astype(BF16)


def row_sizes(steps, halo):
    reach = [-(-2 * (t + 1) // 8) * 8 for t in range(steps)]
    return reach * 2 + [halo] * 8


def whole(rows):
    return -(-rows // SUB) * SUB


def strips_kernel(steps, halo, units, share_ref, std_ref, control_ref, maps_ref, courant_ref, mask_ref, top_ref, bottom_ref):
    rows, cols = courant_ref.shape
    height = len(units) * UNIT
    share = share_ref[...].astype(F32)
    sizes = row_sizes(steps, halo)
    for ref, low, share_low in ((top_ref, True, 0), (bottom_ref, False, height - halo)):

        def pick(size):
            return slice(0, size) if low else slice(rows - size, rows)

        fields = [maps_ref[k, pick(sizes[k]), :] for k in range(2 * steps)]
        fields += [courant_ref[pick(halo), :], mask_ref[pick(halo), :].astype(F32)]
        fields += [std_ref[c, pick(halo), :] * control_ref[c, pick(halo), :] for c in range(3)]
        fields += [share[c * height + share_low : c * height + share_low + halo] for c in range(3)]
        fill = ref.shape[0] - sum(sizes)
        if fill:
            fields.append(jnp.zeros((fill, cols), F32))
        ref[...] = jnp.concatenate(fields, axis=0).astype(BF16)


def merge_kernel(steps, halo, outer, inner, outer_ref, inner_ref, below_ref, above_ref, square_ref, out_ref):
    for units, ref in ((outer, outer_ref), (inner, inner_ref)):
        height = len(units) * UNIT
        rows = (len(outer) + len(inner)) * UNIT
        for c in range(3):
            for n, y in enumerate(units):
                at = c * height + n * UNIT
                out_ref[c * rows + y : c * rows + y + UNIT, :] = ref[at : at + UNIT, :]
    at = sum(row_sizes(steps, halo)) - 3 * halo
    beside = [ref[...].astype(F32)[at : at + 3 * halo] for ref in (below_ref, above_ref)]
    out_ref[3 * rows : 3 * rows + 6 * halo, :] = jnp.concatenate(beside, axis=0).astype(BF16)
    out_ref[3 * rows + 6 * halo :, :] = square_ref[...]


def lane_pack(fields, widths):
    cols = fields[0].shape[1]
    lane = lax.broadcasted_iota(jnp.int32, fields[0].shape, 1)
    left = right = None
    at = 0
    for field, width in zip(fields, widths):
        to_left = field if at == 0 else pltpu.roll(field, at, 1)
        to_right = field if at == 0 else pltpu.roll(field, cols - at, 1)
        left = to_left if left is None else jnp.where(lane >= at, to_left, left)
        right = to_right if right is None else jnp.where(lane < cols - at, to_right, right)
        at += width
    return left, right


def lane_unpack(from_right, from_left, at, width):
    cols = from_right.shape[1]
    lane = lax.broadcasted_iota(jnp.int32, from_right.shape, 1)
    if at:
        from_right = pltpu.roll(from_right, cols - at, 1)
        from_left = pltpu.roll(from_left, at, 1)
    return jnp.where(lane < width, from_right, jnp.where(lane >= cols - width, from_left, 0.0))


def lane_blocks(steps, halo):
    maps = [[(part * steps + t, 2 * (t + 1)) for t in range(steps)] for part in (0, 1)]
    at = 2 * steps
    return [maps[0] + [(at + 2 + c, halo) for c in range(3)], maps[1] + [(at, halo), (at + 1, halo)]]


def pack_kernel(
    steps,
    halo,
    scale,
    place_ref,
    own_ref,
    other_ref,
    std_ref,
    control_ref,
    early_ref,
    maps_ref,
    courant_ref,
    mask_ref,
    below_ref,
    above_ref,
    tall_ref,
    left_ref,
    right_ref,
    cost_ref,
):
    rows, cols = courant_ref.shape
    fields = 2 * steps + 2
    for k in range(2 * steps):
        tall_ref[k, :rows, :] = maps_ref[k]
    tall_ref[2 * steps, :rows, :] = courant_ref[...]
    tall_ref[2 * steps + 1, :rows, :] = mask_ref[...].astype(F32)
    for c in range(3):
        at = slice(c * rows, (c + 1) * rows)
        total = own_ref[at, :].astype(F32) + other_ref[at, :].astype(F32)
        tall_ref[fields + c, :rows, :] = std_ref[c] * control_ref[c] + scale * total
    at = slice(3 * rows, 3 * rows + 6 * halo)
    beside = scale * (own_ref[at, :].astype(F32) + other_ref[at, :].astype(F32))
    at = 3 * rows + 6 * halo
    squares = [
        sum(ref[at + k * SUB : at + (k + 1) * SUB, :].astype(F32) for k in range(PIECES)) for ref in (own_ref, other_ref)
    ]
    cost_ref[...] = early_ref[...] + (squares[0] + squares[1])[:8]
    sizes = row_sizes(steps, halo)
    below_outside, above_outside = place_ref[1] == 1, place_ref[0] == 1
    below, above = below_ref[...].astype(F32), above_ref[...].astype(F32)
    at = 0
    for k in range(fields + 3):
        size = sizes[k]
        lower, upper = below[at : at + size], above[at : at + size]
        if k >= fields:
            c = k - fields
            lower = lower + beside[c * halo : (c + 1) * halo]
            upper = upper + beside[(3 + c) * halo : (4 + c) * halo]
        at += size
        parts = [jnp.where(below_outside, 0.0, lower), jnp.where(above_outside, 0.0, upper)]
        if size < halo:
            parts.insert(1, jnp.zeros((2 * (halo - size), cols), F32))
        tall_ref[k, rows:, :] = jnp.concatenate(parts, axis=0)
    height = rows + 2 * halo
    for n, block in enumerate(lane_blocks(steps, halo)):
        values = [tall_ref[k] for k, _ in block]
        left, right = lane_pack(values, [w for _, w in block])
        left_ref[n * height : (n + 1) * height, :] = left.astype(BF16)
        right_ref[n * height : (n + 1) * height, :] = right.astype(BF16)


def model_kernel(
    steps,
    halo,
    place_ref,
    tall_ref,
    from_right_ref,
    from_left_ref,
    early_ref,
    std_ref,
    control_ref,
    perturbations_ref,
    control_new_ref,
    cost_out_ref,
    product_ref,
    source_ref,
    lam_ref,
    cost_ref,
    cost_sem,
):
    _, rows, cols = control_ref.shape
    members = perturbations_ref.shape[0]
    height_ext = rows + 2 * halo
    width_ext = 2 * cols

    def east(x):
        return pltpu.roll(x, width_ext - 1, 1) - pltpu.roll(x, 1, 1)

    def north(x):
        return pltpu.roll(x, height_ext - 1, 0) - pltpu.roll(x, 1, 0)

    fields = 2 * steps + 2
    sides = {}
    for n, block in enumerate(lane_blocks(steps, halo)):
        at = 0
        from_right = from_right_ref[n * height_ext : (n + 1) * height_ext, :].astype(F32)
        from_left = from_left_ref[n * height_ext : (n + 1) * height_ext, :].astype(F32)
        for k, size in block:
            sides[k] = lane_unpack(from_right, from_left, at, size)
            at += size
    full = [jnp.concatenate([tall_ref[k], sides[k]], axis=1) for k in range(fields + 3)]
    courant, wet = full[2 * steps : fields]
    row = lax.broadcasted_iota(jnp.int32, (height_ext, width_ext), 0)
    outside = ((row >= rows) & (row < rows + halo) & (place_ref[1] == 1)) | ((row >= rows + halo) & (place_ref[0] == 1))
    half_inside = jnp.where(outside, 0.0, 0.5)
    half_wet = 0.5 * wet
    half_both = half_wet * courant
    height, u, v = full[fields], wet * full[fields + 1], wet * full[fields + 2]
    total = early_ref[...]
    for t in range(steps):
        u = u - half_wet * east(height)
        v = v - half_wet * north(height)
        height = height - half_inside * (east(courant * u) + north(courant * v))
        offset = full[steps + t]
        source = full[t] * height - offset
        source_ref[t] = source
        total = total + folded(height[:rows, :cols] * (source[:rows, :cols] - offset[:rows, :cols]))
    cost_ref[...] = jnp.broadcast_to(total[None], (cost_ref.shape[0] // 8, 8, cols)).reshape(cost_ref.shape)
    cost_copy = pltpu.make_async_copy(cost_ref, cost_out_ref, cost_sem)
    cost_copy.start()
    adj = source_ref[steps - 1]
    adj_u = adj_v = None
    for t in range(steps - 1, -1, -1):
        if t < steps - 1:
            adj = adj + source_ref[t]
        du = half_both * east(adj)
        dv = half_both * north(adj)
        adj_u = du if adj_u is None else adj_u + du
        adj_v = dv if adj_v is None else adj_v + dv
        adj = adj + half_inside * (east(adj_u) + north(adj_v))
    lam = [x[:rows, :cols] for x in (adj, adj_u, adj_v)]
    for c in range(3):
        lam_ref[c] = lam[c]
        old = control_ref[c]
        control_new_ref[c] = old - step_length * (old + std_ref[c] * lam[c])
    for i in range(members):
        product_ref[i] = products(perturbations_ref, lam_ref, i).astype(BF16)
    cost_copy.wait()


def products(perturbations_ref, lam_ref, i):
    total = perturbations_ref[i, 0].astype(F32) * lam_ref[0]
    for c in (1, 2):
        total = total + perturbations_ref[i, c].astype(F32) * lam_ref[c]
    return total


def final_kernel(groups, scale, cost_scale, *refs):
    parts = refs[:groups]
    kron_ref, alpha_ref, terms_ref, out_ref, cost_ref = refs[groups:]
    members, rows, cols = alpha_ref.shape
    cost_ref[0, 0] = jnp.sum(terms_ref[...]) * cost_scale
    for y in range(0, rows, UNIT):
        grad = None
        for g, part in enumerate(parts):
            term = jnp.dot(kron_ref[g], pair_of(part, y), preferred_element_type=F32)
            grad = term if grad is None else grad + term
        for k in (0, 1):
            at = slice(y + k * SUB, y + (k + 1) * SUB)
            part = grad[:, k * cols : (k + 1) * cols].reshape(members, SUB, cols)
            old = alpha_ref[:, at, :]
            out_ref[:, at, :] = old - step_length * (old + scale * part)


def to_others(x, groups):
    return [lax.ppermute(x, "ens", [(i, (i - k) % groups) for i in range(groups)]) for k in range(1, groups)]


def sum_parts(share, groups):
    if groups == 2:
        return share, to_others(share, groups)[0]
    share = lax.psum(share.astype(F32), "ens")
    return share, jnp.zeros_like(share)


def body(
    perturbations,
    ens_weights,
    control,
    static_std,
    courant,
    land_mask,
    band_offsets,
    band_weights,
    obs_cells,
    obs_values,
    obs_weights,
):
    own, _, rows, cols = perturbations.shape
    groups = lax.axis_size("ens")
    n_ty, n_tx = lax.axis_size("ty"), lax.axis_size("tx")
    members = own * groups
    steps = obs_cells.shape[2]
    halo = 4 * steps
    scale = 1.0 / math.sqrt(members)
    down = [(i, (i + 1) % n_ty) for i in range(n_ty)]
    up = [(j, i) for i, j in down]
    right = [(i, (i + 1) % n_tx) for i in range(n_tx)]
    left = [(j, i) for i, j in right]
    ty_index = lax.axis_index("ty")
    place = jnp.stack(
        [
            (ty_index == 0).astype(jnp.int32),
            (ty_index == n_ty - 1).astype(jnp.int32),
            lax.axis_index("ens").astype(jnp.int32),
        ]
    )
    units = list(range(0, rows, UNIT))
    at_edge = -(-halo // UNIT)
    outer = units[:at_edge] + units[len(units) - at_edge :]
    inner = units[at_edge : len(units) - at_edge]

    def rows_of(chunk, mib, *before):
        shape = (own, len(chunk) * UNIT, cols)
        (sent,) = call(
            functools.partial(send_kernel, chunk),
            [(shape, BF16)],
            [ens_weights, *before],
            in_specs=[HBM] * (1 + len(before)),
            scratch=[pltpu.VMEM(shape, F32), pltpu.SemaphoreType.DMA((len(chunk),))],
            name="send",
            mib=mib,
        )
        return sent

    outer_sent = rows_of(outer, 56)
    outer_others = to_others(outer_sent, groups)
    inner_others = to_others(rows_of(inner, 4, outer_sent), groups)

    cells, values, weights = (x.reshape(steps, x.shape[-1]) for x in (obs_cells, obs_values, obs_weights))
    maps, early = call(
        functools.partial(maps_kernel, steps),
        [((2 * steps, rows, cols), F32), ((8, cols), F32)],
        [cells, values, weights, control],
        flops=2 * steps * 4 * rows * cols * cells.shape[1],
        name="maps",
    )
    wide = own * SUB
    kron_beta, kron_grad, own_share, square = call(
        functools.partial(own_kernel, groups),
        [((groups, wide, wide), BF16)] * 2 + [((3, rows, cols), F32), ((PIECES * SUB, cols), BF16)],
        [place, band_offsets, band_weights, ens_weights, perturbations],
        in_specs=[SMEM, SMEM, SMEM, HBM, VMEM],
        scratch=[pltpu.VMEM((own, rows, cols), F32), pltpu.SemaphoreType.DMA],
        name="own",
    )

    def share_of(units, others, name):
        (share,) = call(
            functools.partial(share_kernel, groups, units),
            [((3 * len(units) * UNIT, cols), BF16)],
            [*others, kron_beta, perturbations, own_share],
            name=name,
        )
        return share

    outer_share = share_of(outer, outer_others, "outer_share")
    edge_rows = whole(sum(row_sizes(steps, halo)))
    top, bottom = call(
        functools.partial(strips_kernel, steps, halo, outer),
        [((edge_rows, cols), BF16)] * 2,
        [outer_share, static_std, control, maps, courant, land_mask],
        name="strips",
    )
    above = lax.ppermute(bottom, "ty", down)
    below = lax.ppermute(top, "ty", up)

    inner_share = share_of(inner, inner_others, "inner_share")
    (share,) = call(
        functools.partial(merge_kernel, steps, halo, outer, inner),
        [((3 * rows + 6 * halo + PIECES * SUB, cols), BF16)],
        [outer_share, inner_share, below, above, square],
        name="merge",
    )
    share, share_other = sum_parts(share, groups)
    high = rows + 2 * halo
    tall, to_left, to_right, early = call(
        functools.partial(pack_kernel, steps, halo, scale),
        [((2 * steps + 5, high, cols), F32), ((2 * high, cols), BF16), ((2 * high, cols), BF16), ((8, cols), F32)],
        [place, share, share_other, static_std, control, early, maps, courant, land_mask, below, above],
        smem=1,
        name="pack",
    )
    from_left = lax.ppermute(to_right, "tx", right)
    from_right = lax.ppermute(to_left, "tx", left)

    control_new, cost_terms, product = call(
        functools.partial(model_kernel, steps, halo),
        [
            ((3, rows, cols), F32),
            ((n_ty * n_tx * 8, cols), F32),
            ((own, rows, cols), BF16),
        ],
        [place, tall, from_right, from_left, early, static_std, control, perturbations],
        scratch=[
            pltpu.VMEM((steps, high, 2 * cols), F32),
            pltpu.VMEM((3, rows, cols), F32),
            pltpu.VMEM((n_ty * n_tx * 8, cols), F32),
            pltpu.SemaphoreType.DMA,
        ],
        out_specs=[VMEM, HBM, VMEM],
        smem=1,
        mib=16,
        name="model",
    )
    product_others = to_others(product, groups)
    terms = lax.all_to_all(cost_terms, ("ty", "tx"), 0, 0, tiled=True)
    cost_scale = 0.5 / ((3 + members) * rows * cols * n_ty * n_tx)

    weights_new, cost = call(
        functools.partial(final_kernel, groups, scale, cost_scale),
        [((own, rows, cols), F32), ((1, 1), F32)],
        [product, *product_others, kron_grad, ens_weights, terms],
        out_specs=[VMEM, SMEM],
        name="final",
    )
    return (control_new, weights_new, cost.reshape(()))


def solution(mesh):
    return jax.shard_map(
        body,
        mesh=mesh,
        in_specs=(
            P("ens", None, "ty", "tx"),
            P("ens", "ty", "tx"),
            P(None, "ty", "tx"),
            P(None, "ty", "tx"),
            P("ty", "tx"),
            P("ty", "tx"),
            P(),
            P(),
            P("ty", "tx", None, None),
            P("ty", "tx", None, None),
            P("ty", "tx", None, None),
        ),
        out_specs=(P(None, "ty", "tx"), P("ens", "ty", "tx"), P()),
        check_vma=False,
    )
```

time: 78.9 us -> 56.4 us (0.71)
  local copies, waits for them, and re-layouts: 16.1 us -> 1.05 us
  starting transfers between devices: 24.8 us -> 11 us
  blocking collectives: 0 us -> 9.47 us
  other arithmetic: 2.69 us -> 0.08 us
  Pallas kernels: 12.1 us -> 14.5 us
  between operations: 2.78 us -> 0.88 us
    unnamed x74 -> x26, local copies, waits for them, and re-layouts: 16 us -> 1.05 us
    all_to_all x0 -> x1, blocking collectives: none -> 9.47 us  [body(): terms = lax.all_to_all(cost_terms, ('ty', 'tx'), 0, 0, tiled=True)]
    all_to_all x1 -> x0, starting transfers between devices: 6.59 us -> none  [body(): terms = lax.all_to_all(cost_terms, ('ty', 'tx'), 0, 0, tiled=True)]
    ppermute x4 -> x0, starting transfers between devices: 6.4 us -> none  [the longest x1 4.55 us: body(): s_above = lax.ppermute(s_bottom, 'ty', down)]
    ppermute x1, starting transfers between devices: 4.97 us -> 0.01 us  [body(): above = lax.ppermute(bottom, 'ty', down)]
    all_to_all x1 -> x0, waiting for transfers between devices: 3.33 us -> none  [body(): terms = lax.all_to_all(cost_terms, ('ty', 'tx'), 0, 0, tiled=True)]
    ppermute x1, starting transfers between devices: 1.28 us -> 4.19 us  [body(): below = lax.ppermute(top, 'ty', up)]
    ppermute x1, waiting for transfers between devices: 1.45 us -> 4.18 us  [body(): above = lax.ppermute(bottom, 'ty', down)]
  transfers between devices with their start and end apart: 12 -> 8, of which waited for: 8 -> 8; matrix products, arithmetic and copies ran while one was open for 2% -> 0% of each run, Pallas kernels for 5% -> 7%
where the time goes in v1:
time: 56.4 us; the launch traced here: 56.2 us
  waiting for transfers between devices  19.1 us (34%)
  Pallas kernels  14.5 us (26%)
  starting transfers between devices  11 us (20%)
  blocking collectives  9.47 us (17%)
  local copies, waits for them, and re-layouts  1.05 us (2%)
  between operations  0.88 us (2%)
    pallas_call x11, Pallas kernels, call(): pl.pallas_call(kernel, out_shape=out_shape, grid=grid, in_specs=in_specs...  14.5 us
    all_to_all x1, blocking collectives, body(): terms = lax.all_to_all(cost_terms, ('ty', 'tx'), 0, 0, tiled=True)  9.47 us
    ppermute x4, waiting for transfers between devices, to_others(): lax.ppermute(x, 'ens', [(i, (i - k) % groups) for i in range(groups)])  8.98 us
    ppermute x4, starting transfers between devices, to_others(): lax.ppermute(x, 'ens', [(i, (i - k) % groups) for i in range(groups)])  6.27 us
    ppermute x1, starting transfers between devices, body(): below = lax.ppermute(top, 'ty', up)  4.19 us
    ppermute x1, waiting for transfers between devices, body(): above = lax.ppermute(bottom, 'ty', down)  4.18 us
    ppermute x1, waiting for transfers between devices, body(): from_left = lax.ppermute(to_right, 'tx', right)  2.82 us
    ppermute x1, waiting for transfers between devices, body(): from_right = lax.ppermute(to_left, 'tx', left)  1.63 us
  transfers between devices with their start and end apart: 8, of which 8 were waited for; matrix products, arithmetic and copies ran while one was open for 0% of the time, Pallas kernels for 7%

profile of v1, /device:TPU:0, one launch (start us, length us, event | category | flops | bytes accessed | tf_op | source)
XLA Modules:
  0.0 56.2 jit_solution(9718279376775863598)
XLA Ops:
  0.6 0.0 copy-start.1
  0.6 0.0 copy-start
  0.6 1.9 %send.2.refs_0_ = bf16[16,64,128]{2,1,0:T(8,128)(2,1)} custom-call(f32[16,128,128]{2,1,0:T(8,128)} %refs_3_.1), custom_call_target="tpu_custom_call" | custom-call | bytes 1310720 | tf_op jit(solution)/shard_map/send/pallas_call | solution.py:26
  2.6 3.0 %collective-permute-start = (bf16[16,64,128]{2,1,0:T(8,128)(2,1)}, bf16[16,64,128]{2,1,0:T(8,128)(2,1)S(1)}, u32[]{:S(2)}, u32[]{:S(2)}) collective-permute-start(bf16[16,64,128]{2,1,0:T(8,128)(2,1)} %send.2.refs_0_), channel_id=1, source_target_pairs={{0,16},{16,0},{1,17},{17,1},{2,18},{18,2},{3,19},{19,3},{4,20},{20... | collective-permute-start | bytes 786440 | tf_op jit(solution)/shard_map/ppermute | solution.py:432
  5.6 0.0 copy-done.1
  5.6 0.0 copy-start.4
  5.6 1.0 %copy-done.4 = bf16[16,64,128]{2,1,0:T(8,128)(2,1)S(1)} copy-done((bf16[16,64,128]{2,1,0:T(8,128)(2,1)S(1)}, bf16[16,64,128]{2,1,0:T(8,128)(2,1)}, u32[]{:S(2)}) %copy-start.4) | copy-done | bytes 262168
  6.6 0.8 %send.3 = bf16[16,64,128]{2,1,0:T(8,128)(2,1)} custom-call(f32[16,128,128]{2,1,0:T(8,128)S(1)} %copy-done.1, bf16[16,64,128]{2,1,0:T(8,128)(2,1)S(1)} %copy-done.4), custom_call_target="tpu_custom_call" | custom-call | bytes 1572864 | tf_op jit(solution)/shard_map/send/pallas_call | solution.py:26
  7.4 0.0 copy-start.10
  7.4 0.0 copy-start.11
  7.4 0.0 copy-start.3
  7.4 0.1 collective-permute-start.1
  7.5 0.0 copy-done.9
  7.5 0.1 pad_add_fusion.place_ref
  7.6 0.0 copy-done
  7.6 0.0 copy-done.7
  7.6 0.0 copy-done.8
  7.6 1.8 %own.1 = (bf16[2,256,256]{2,1,0:T(8,128)(2,1)S(1)}, bf16[2,256,256]{2,1,0:T(8,128)(2,1)S(1)}, f32[3,128,128]{2,1,0:T(8,128)S(1)}, bf16[48,128]{1,0:T(8,128)(2,1)S(1)}) custom-call(s32[3]{0:T(128)S(1)} %pad_add_fusion.place_ref, s32[32]{0:T(128)S(1)} %copy-done.7, f32[32]{0:T(128)S(1)} %copy-done.8, f32[16,128,128]{2,1,0:T(8,128)S(1)} %copy-done.1, ...), custom_call_target="tpu_custom_call" | custom-call | bytes 3354892 | tf_op jit(solution)/shard_map/own/pallas_call | solution.py:26
  9.5 0.0 copy-done.10
  9.5 0.0 copy-done.11
  9.5 0.0 copy-done.3
  9.5 0.0 copy-start.2
  9.5 0.0 copy-start.5
  9.5 0.0 copy-start.6
  9.6 1.2 %maps.1 = (f32[12,128,128]{2,1,0:T(8,128)S(1)}, f32[8,128]{1,0:T(8,128)S(1)}) custom-call(s32[6,512]{1,0:T(8,128)S(1)} %bitcast.15, f32[6,512]{1,0:T(8,128)S(1)} %get-tuple-element.38.values_ref, f32[6,512]{1,0:T(8,128)S(1)} %get-tuple-element.37.weights_ref, f32[3,128,128]{2,1,0:T(8,128)S(1)} %copy-done.3), custom_call_target="tpu_custom_call" | custom-call | flops 402653184 | bytes 1024000 | tf_op jit(solution)/shard_map/maps/pallas_call | solution.py:26
  10.7 2.2 %collective-permute-done.refs_0_ = bf16[16,64,128]{2,1,0:T(8,128)(2,1)S(1)} collective-permute-done((bf16[16,64,128]{2,1,0:T(8,128)(2,1)}, bf16[16,64,128]{2,1,0:T(8,128)(2,1)S(1)}, u32[]{:S(2)}, u32[]{:S(2)}) %collective-permute-start) | collective-permute-done | bytes 262176 | tf_op jit(solution)/shard_map/ppermute | solution.py:432
  12.9 0.3 outer_share.1.share_ref.outer_ref
  13.3 0.0 copy-done.2
  13.3 0.0 copy-done.5
  13.3 0.0 copy-done.6
  13.3 4.2 %collective-permute-start.2 = (bf16[320,128]{1,0:T(8,128)(2,1)S(1)}, bf16[320,128]{1,0:T(8,128)(2,1)S(1)}, u32[]{:S(2)}, u32[]{:S(2)}) collective-permute-start(bf16[320,128]{1,0:T(8,128)(2,1)S(1)} %get-tuple-element.23), channel_id=1, source_target_pairs={{4,0},{8,4},{12,8},{0,12},{5,1},{9,5},{13,9},{1,13},{6,2},{10,6},{... | collective-permute-start | bytes 245768 | tf_op jit(solution)/shard_map/ppermute | solution.py:532
  17.5 0.0 collective-permute-start.3
  17.5 0.2 collective-permute-done.1.refs_0_
  17.7 0.3 inner_share.1.inner_ref
  18.0 1.5 %collective-permute-done.2.below_ref = bf16[320,128]{1,0:T(8,128)(2,1)S(1)} collective-permute-done((bf16[320,128]{1,0:T(8,128)(2,1)S(1)}, bf16[320,128]{1,0:T(8,128)(2,1)S(1)}, u32[]{:S(2)}, u32[]{:S(2)}) %collective-permute-start.2) | collective-permute-done | bytes 81952 | tf_op jit(solution)/shard_map/ppermute | solution.py:532
  19.6 4.2 %collective-permute-done.3.above_ref = bf16[320,128]{1,0:T(8,128)(2,1)S(1)} collective-permute-done((bf16[320,128]{1,0:T(8,128)(2,1)S(1)}, bf16[320,128]{1,0:T(8,128)(2,1)S(1)}, u32[]{:S(2)}, u32[]{:S(2)}) %collective-permute-start.3) | collective-permute-done | bytes 81952 | tf_op jit(solution)/shard_map/ppermute | solution.py:531
  23.8 1.6 %collective-permute-start.4 = (bf16[576,128]{1,0:T(8,128)(2,1)S(1)}, bf16[576,128]{1,0:T(8,128)(2,1)S(1)}, u32[]{:S(2)}, u32[]{:S(2)}) collective-permute-start(bf16[576,128]{1,0:T(8,128)(2,1)S(1)} %merge.1.own_ref), channel_id=1, source_target_pairs={{0,16},{16,0},{1,17},{17,1},{2,18},{18,2},{3,19},{19,3},{4,20},{20... | collective-permute-start | bytes 442376 | tf_op jit(solution)/shard_map/ppermute | solution.py:432
  25.4 3.6 %collective-permute-done.4.other_ref = bf16[576,128]{1,0:T(8,128)(2,1)S(1)} collective-permute-done((bf16[576,128]{1,0:T(8,128)(2,1)S(1)}, bf16[576,128]{1,0:T(8,128)(2,1)S(1)}, u32[]{:S(2)}, u32[]{:S(2)}) %collective-permute-start.4) | collective-permute-done | bytes 147488 | tf_op jit(solution)/shard_map/ppermute | solution.py:432
  29.0 1.0 %pack.1 = (f32[17,176,128]{2,1,0:T(8,128)S(1)}, bf16[352,128]{1,0:T(8,128)(2,1)S(1)}, bf16[352,128]{1,0:T(8,128)(2,1)S(1)}, f32[8,128]{1,0:T(8,128)S(1)}) custom-call(s32[3]{0:T(128)S(1)} %pad_add_fusion.place_ref, bf16[576,128]{1,0:T(8,128)(2,1)S(1)} %merge.1.own_ref, bf16[576,128]{1,0:T(8,128)(2,1)S(1)} %collective-permute-done.4.other_ref, ...), custom_call_target="tpu_custom_call" | custom-call | bytes 3489804 | tf_op jit(solution)/shard_map/pack/pallas_call | solution.py:26
  30.0 0.1 collective-permute-start.5
  30.0 0.5 collective-permute-start.6
  30.5 1.6 %collective-permute-done.5.from_right_ref = bf16[352,128]{1,0:T(8,128)(2,1)S(1)} collective-permute-done((bf16[352,128]{1,0:T(8,128)(2,1)S(1)}, bf16[352,128]{1,0:T(8,128)(2,1)S(1)}, u32[]{:S(2)}, u32[]{:S(2)}) %collective-permute-start.5) | collective-permute-done | bytes 90144 | tf_op jit(solution)/shard_map/ppermute | solution.py:551
  32.2 2.8 %collective-permute-done.6.from_left_ref = bf16[352,128]{1,0:T(8,128)(2,1)S(1)} collective-permute-done((bf16[352,128]{1,0:T(8,128)(2,1)S(1)}, bf16[352,128]{1,0:T(8,128)(2,1)S(1)}, u32[]{:S(2)}, u32[]{:S(2)}) %collective-permute-start.6) | collective-permute-done | bytes 90144 | tf_op jit(solution)/shard_map/ppermute | solution.py:550
  35.0 5.7 %model.1 = (f32[3,128,128]{2,1,0:T(8,128)}, f32[128,128]{1,0:T(8,128)S(1)}, bf16[16,128,128]{2,1,0:T(8,128)(2,1)S(1)}) custom-call(s32[3]{0:T(128)S(1)} %pad_add_fusion.place_ref, f32[17,176,128]{2,1,0:T(8,128)S(1)} %get-tuple-element.27.tall_ref, bf16[352,128]{1,0:T(8,128)(2,1)S(1)} %collective-permute-done.5.from_right_ref, ...), custom_call_target="tpu_custom_call" | custom-call | bytes 4468748 | tf_op jit(solution)/shard_map/model/pallas_call | solution.py:26
  40.7 1.6 %collective-permute-start.7 = (bf16[16,128,128]{2,1,0:T(8,128)(2,1)S(1)}, bf16[16,128,128]{2,1,0:T(8,128)(2,1)S(1)}, u32[]{:S(2)}, u32[]{:S(2)}) collective-permute-start(bf16[16,128,128]{2,1,0:T(8,128)(2,1)S(1)} %get-tuple-element.32.refs_0_), channel_id=1, source_target_pairs={{0,16},{16,0},{1,17},{17,1},{2,18},{18,2},{3,19},{19,3},{4,20},{20... | collective-permute-start | bytes 1572872 | tf_op jit(solution)/shard_map/ppermute | solution.py:432
  42.3 9.5 %all_to_all.11 = f32[16,8,128]{2,1,0:T(8,128)S(1)} all-to-all(f32[16,8,128]{2,1,0:T(8,128)S(1)} %bitcast.14), channel_id=1, replica_groups=mesh['ens'=2,'ty'=4,'tx'=4] {'ty','tx'}, dimensions={0} | all-to-all | bytes 131072 | tf_op jit(solution)/shard_map/all_to_all | solution.py:573
  51.8 2.9 %collective-permute-done.7.refs_1_ = bf16[16,128,128]{2,1,0:T(8,128)(2,1)S(1)} collective-permute-done((bf16[16,128,128]{2,1,0:T(8,128)(2,1)S(1)}, bf16[16,128,128]{2,1,0:T(8,128)(2,1)S(1)}, u32[]{:S(2)}, u32[]{:S(2)}) %collective-permute-start.7) | collective-permute-done | bytes 524320 | tf_op jit(solution)/shard_map/ppermute | solution.py:432
  54.7 1.4 %final.1 = (f32[16,128,128]{2,1,0:T(8,128)}, f32[1,1]{1,0:T(1,128)}) custom-call(bf16[16,128,128]{2,1,0:T(8,128)(2,1)S(1)} %get-tuple-element.32.refs_0_, bf16[16,128,128]{2,1,0:T(8,128)(2,1)S(1)} %collective-permute-done.7.refs_1_, bf16[2,256,256]{2,1,0:T(8,128)(2,1)S(1)} %get-tuple-element.33.refs_2_, f32[16,128,128]{2,1,0:T(8,128)S(1)} %copy-done.1, ...), custom_call_target="tpu_custom_call" | custom-call | bytes 3473412 | tf_op jit(solution)/shard_map/final/pallas_call | solution.py:26
  (7 shorter events, 0.1 us)
Async XLA Ops:
  0.6 5.0 %copy-start.1 = (f32[16,128,128]{2,1,0:T(8,128)S(1)}, f32[16,128,128]{2,1,0:T(8,128)}, u32[]{:S(2)}) copy-start(f32[16,128,128]{2,1,0:T(8,128)} %refs_3_.1) | copy-start | bytes 3145732
  0.6 7.0 %copy-start = (bf16[16,3,128,128]{3,2,1,0:T(8,128)(2,1)S(1)}, bf16[16,3,128,128]{3,2,1,0:T(8,128)(2,1)}, u32[]{:S(2)}) copy-start(bf16[16,3,128,128]{3,2,1,0:T(8,128)(2,1)} %perturbations_ref.3) | copy-start | bytes 4718596
  2.6 10.4 %collective-permute-start = (bf16[16,64,128]{2,1,0:T(8,128)(2,1)}, bf16[16,64,128]{2,1,0:T(8,128)(2,1)S(1)}, u32[]{:S(2)}, u32[]{:S(2)}) collective-permute-start(bf16[16,64,128]{2,1,0:T(8,128)(2,1)} %send.2.refs_0_), channel_id=1, source_target_pairs={{0,16},{16,0},{1,17},{17,1},{2,18},{18,2},{3,19},{19,3},{4,20},{20... | collective-permute-start | bytes 786440 | tf_op jit(solution)/shard_map/ppermute | solution.py:432
  5.6 1.0 %copy-start.4 = (bf16[16,64,128]{2,1,0:T(8,128)(2,1)S(1)}, bf16[16,64,128]{2,1,0:T(8,128)(2,1)}, u32[]{:S(2)}) copy-start(bf16[16,64,128]{2,1,0:T(8,128)(2,1)} %send.2.refs_0_) | copy-start | bytes 786436
  6.6 0.9 %copy-start.9 = (s32[1,1,6,512]{3,1,2,0:T(1,128)S(1)}, s32[1,1,6,512]{3,1,2,0:T(1,128)}, u32[]{:S(2)}) copy-start(s32[1,1,6,512]{3,1,2,0:T(1,128)} %param.19) | copy-start | bytes 36868
  6.6 1.0 %copy-start.7 = (s32[32]{0:T(128)S(1)}, s32[32]{0:T(128)}, u32[]{:S(2)}) copy-start(s32[32]{0:T(128)} %offsets_ref.1) | copy-start | bytes 388
  6.6 1.0 %copy-start.8 = (f32[32]{0:T(128)S(1)}, f32[32]{0:T(128)}, u32[]{:S(2)}) copy-start(f32[32]{0:T(128)} %weights_ref.1) | copy-start | bytes 388
  7.4 2.1 %copy-start.10 = (f32[1,1,6,512]{3,1,2,0:T(1,128)S(1)}, f32[1,1,6,512]{3,1,2,0:T(1,128)}, u32[]{:S(2)}) copy-start(f32[1,1,6,512]{3,1,2,0:T(1,128)} %param.21) | copy-start | bytes 36868
  7.4 2.1 %copy-start.11 = (f32[1,1,6,512]{3,1,2,0:T(1,128)S(1)}, f32[1,1,6,512]{3,1,2,0:T(1,128)}, u32[]{:S(2)}) copy-start(f32[1,1,6,512]{3,1,2,0:T(1,128)} %param.20) | copy-start | bytes 36868
  7.4 2.1 %copy-start.3 = (f32[3,128,128]{2,1,0:T(8,128)S(1)}, f32[3,128,128]{2,1,0:T(8,128)}, u32[]{:S(2)}) copy-start(f32[3,128,128]{2,1,0:T(8,128)} %control_ref.7) | copy-start | bytes 589828
  7.4 10.3 %collective-permute-start.1 = (bf16[16,64,128]{2,1,0:T(8,128)(2,1)}, bf16[16,64,128]{2,1,0:T(8,128)(2,1)S(1)}, u32[]{:S(2)}, u32[]{:S(2)}) collective-permute-start(bf16[16,64,128]{2,1,0:T(8,128)(2,1)} %send.3), channel_id=1, source_target_pairs={{0,16},{16,0},{1,17},{17,1},{2,18},{18,2},{3,19},{19,3},{4,20},{20... | collective-permute-start | bytes 786440 | tf_op jit(solution)/shard_map/ppermute | solution.py:432
  9.5 3.7 %copy-start.2 = (f32[3,128,128]{2,1,0:T(8,128)S(1)}, f32[3,128,128]{2,1,0:T(8,128)}, u32[]{:S(2)}) copy-start(f32[3,128,128]{2,1,0:T(8,128)} %std_ref.5) | copy-start | bytes 589828
  9.5 3.7 %copy-start.5 = (f32[128,128]{1,0:T(8,128)S(1)}, f32[128,128]{1,0:T(8,128)}, u32[]{:S(2)}) copy-start(f32[128,128]{1,0:T(8,128)} %courant_ref.3) | copy-start | bytes 196612
  9.5 3.7 %copy-start.6 = (s32[128,128]{1,0:T(8,128)S(1)}, s32[128,128]{1,0:T(8,128)}, u32[]{:S(2)}) copy-start(s32[128,128]{1,0:T(8,128)} %mask_ref.3) | copy-start | bytes 196612
  13.3 6.3 %collective-permute-start.2 = (bf16[320,128]{1,0:T(8,128)(2,1)S(1)}, bf16[320,128]{1,0:T(8,128)(2,1)S(1)}, u32[]{:S(2)}, u32[]{:S(2)}) collective-permute-start(bf16[320,128]{1,0:T(8,128)(2,1)S(1)} %get-tuple-element.23), channel_id=1, source_target_pairs={{4,0},{8,4},{12,8},{0,12},{5,1},{9,5},{13,9},{1,13},{6,2},{10,6},{... | collective-permute-start | bytes 245768 | tf_op jit(solution)/shard_map/ppermute | solution.py:532
  17.5 6.2 %collective-permute-start.3 = (bf16[320,128]{1,0:T(8,128)(2,1)S(1)}, bf16[320,128]{1,0:T(8,128)(2,1)S(1)}, u32[]{:S(2)}, u32[]{:S(2)}) collective-permute-start(bf16[320,128]{1,0:T(8,128)(2,1)S(1)} %get-tuple-element.24), channel_id=1, source_target_pairs={{0,4},{4,8},{8,12},{12,0},{1,5},{5,9},{9,13},{13,1},{2,6},{6,10},{... | collective-permute-start | bytes 245768 | tf_op jit(solution)/shard_map/ppermute | solution.py:531
  23.8 5.2 %collective-permute-start.4 = (bf16[576,128]{1,0:T(8,128)(2,1)S(1)}, bf16[576,128]{1,0:T(8,128)(2,1)S(1)}, u32[]{:S(2)}, u32[]{:S(2)}) collective-permute-start(bf16[576,128]{1,0:T(8,128)(2,1)S(1)} %merge.1.own_ref), channel_id=1, source_target_pairs={{0,16},{16,0},{1,17},{17,1},{2,18},{18,2},{3,19},{19,3},{4,20},{20... | collective-permute-start | bytes 442376 | tf_op jit(solution)/shard_map/ppermute | solution.py:432
  30.0 2.2 %collective-permute-start.5 = (bf16[352,128]{1,0:T(8,128)(2,1)S(1)}, bf16[352,128]{1,0:T(8,128)(2,1)S(1)}, u32[]{:S(2)}, u32[]{:S(2)}) collective-permute-start(bf16[352,128]{1,0:T(8,128)(2,1)S(1)} %get-tuple-element.28), channel_id=1, source_target_pairs={{1,0},{2,1},{3,2},{0,3},{5,4},{6,5},{7,6},{4,7},{9,8},{10,9},{11,1... | collective-permute-start | bytes 270344 | tf_op jit(solution)/shard_map/ppermute | solution.py:551
  30.0 5.0 %collective-permute-start.6 = (bf16[352,128]{1,0:T(8,128)(2,1)S(1)}, bf16[352,128]{1,0:T(8,128)(2,1)S(1)}, u32[]{:S(2)}, u32[]{:S(2)}) collective-permute-start(bf16[352,128]{1,0:T(8,128)(2,1)S(1)} %get-tuple-element.29), channel_id=1, source_target_pairs={{0,1},{1,2},{2,3},{3,0},{4,5},{5,6},{6,7},{7,4},{8,9},{9,10},{10,1... | collective-permute-start | bytes 270344 | tf_op jit(solution)/shard_map/ppermute | solution.py:550
  40.7 14.0 %collective-permute-start.7 = (bf16[16,128,128]{2,1,0:T(8,128)(2,1)S(1)}, bf16[16,128,128]{2,1,0:T(8,128)(2,1)S(1)}, u32[]{:S(2)}, u32[]{:S(2)}) collective-permute-start(bf16[16,128,128]{2,1,0:T(8,128)(2,1)S(1)} %get-tuple-element.32.refs_0_), channel_id=1, source_target_pairs={{0,16},{16,0},{1,17},{17,1},{2,18},{18,2},{3,19},{19,3},{4,20},{20... | collective-permute-start | bytes 1572872 | tf_op jit(solution)/shard_map/ppermute | solution.py:432

commit v2 on v1

--- a/solution.py
+++ b/solution.py
@@ -12,6 +12,8 @@
 SUB = 16
 UNIT = 2 * SUB
 PIECES = 3
+ROW = 8
+GROUP = 24
 F32 = jnp.float32
 BF16 = jnp.bfloat16
 VMEM = pl.BlockSpec(memory_space=pltpu.VMEM)
@@ -335,97 +337,213 @@
     early_ref,
     std_ref,
     control_ref,
-    perturbations_ref,
     control_new_ref,
     cost_out_ref,
-    product_ref,
+    lam_ref,
     source_ref,
-    lam_ref,
     cost_ref,
     cost_sem,
+    sides_ref,
+    courant_ref,
+    half_wet_ref,
+    half_both_ref,
+    *state_refs,
 ):
     _, rows, cols = control_ref.shape
-    members = perturbations_ref.shape[0]
     height_ext = rows + 2 * halo
-    width_ext = 2 * cols
+    fields = 2 * steps + 2
+    tile, extra, total_blocks = rows // ROW, halo // ROW, height_ext // ROW
+    states = state_refs[:3], state_refs[3:]
+    left, right = slice(0, cols), slice(cols, 2 * cols)
+    row = lax.broadcasted_iota(jnp.int32, (ROW, 2 * cols), 0)
+    top, last = row == 0, row == ROW - 1
+    half = [jnp.where(place_ref[k] == 1, 0.0, 0.5) for k in (0, 1)]
+
+    def at(k):
+        k = k % total_blocks
+        return slice(k * ROW, (k + 1) * ROW)
+
+    def half_inside(k):
+        return half[0] if k < 0 else half[1] if k >= tile else 0.5
+
+    def around(reach):
+        n = min(extra, -(-reach // ROW))
+        return range(-n, tile + n)
 
     def east(x):
-        return pltpu.roll(x, width_ext - 1, 1) - pltpu.roll(x, 1, 1)
-
-    def north(x):
-        return pltpu.roll(x, height_ext - 1, 0) - pltpu.roll(x, 1, 0)
-
-    fields = 2 * steps + 2
-    sides = {}
+        return pltpu.roll(x, 2 * cols - 1, 1) - pltpu.roll(x, 1, 1)
+
+    class Column:
+        def __init__(self):
+            self.value, self.up, self.down = {}, {}, {}
+
+        def put(self, k, x):
+            self.value[k], self.up[k], self.down[k] = x, pltpu.roll(x, ROW - 1, 0), pltpu.roll(x, 1, 0)
+
+        def north(self, k):
+            up = jnp.where(last, self.up.get(k + 1, self.up[k]), self.up[k])
+            return up - jnp.where(top, self.down.get(k - 1, self.down[k]), self.down[k])
+
     for n, block in enumerate(lane_blocks(steps, halo)):
-        at = 0
+        place = 0
         from_right = from_right_ref[n * height_ext : (n + 1) * height_ext, :].astype(F32)
         from_left = from_left_ref[n * height_ext : (n + 1) * height_ext, :].astype(F32)
         for k, size in block:
-            sides[k] = lane_unpack(from_right, from_left, at, size)
-            at += size
-    full = [jnp.concatenate([tall_ref[k], sides[k]], axis=1) for k in range(fields + 3)]
-    courant, wet = full[2 * steps : fields]
-    row = lax.broadcasted_iota(jnp.int32, (height_ext, width_ext), 0)
-    outside = ((row >= rows) & (row < rows + halo) & (place_ref[1] == 1)) | ((row >= rows + halo) & (place_ref[0] == 1))
-    half_inside = jnp.where(outside, 0.0, 0.5)
-    half_wet = 0.5 * wet
-    half_both = half_wet * courant
-    height, u, v = full[fields], wet * full[fields + 1], wet * full[fields + 2]
+            sides_ref[k] = lane_unpack(from_right, from_left, place, size)
+            place += size
+
+    def joined(k, rows_at):
+        return jnp.concatenate([tall_ref[k, rows_at, :], sides_ref[k, rows_at, :]], axis=1)
+
+    for k in around(halo):
+        wet, courant = joined(2 * steps + 1, at(k)), joined(2 * steps, at(k))
+        half_wet_ref[at(k), :] = 0.5 * wet
+        courant_ref[at(k), :] = courant
+        half_both_ref[at(k), :] = 0.5 * wet * courant
+        states[0][0][at(k), :] = joined(fields, at(k))
+        states[0][1][at(k), :] = wet * joined(fields + 1, at(k))
+        states[0][2][at(k), :] = wet * joined(fields + 2, at(k))
+
     total = early_ref[...]
     for t in range(steps):
-        u = u - half_wet * east(height)
-        v = v - half_wet * north(height)
-        height = height - half_inside * (east(courant * u) + north(courant * v))
-        offset = full[steps + t]
-        source = full[t] * height - offset
-        source_ref[t] = source
-        total = total + folded(height[:rows, :cols] * (source[:rows, :cols] - offset[:rows, :cols]))
+        out = halo - 2 * (t + 1)
+        src, dst = states[t % 2], states[1 - t % 2]
+        flow, result, seen = around(out + 1), around(out), around(2 * (t + 1))
+        height, flux, spread = Column(), Column(), {}
+        for k in (flow[0] - 1, flow[0]):
+            if k >= -extra:
+                height.put(k, src[0][at(k), :])
+        for first in range(flow[0], flow[-1] + 2, GROUP):
+            group = [k for k in range(first, first + GROUP) if k in flow]
+            for k in group:
+                if k + 1 < tile + extra:
+                    height.put(k + 1, src[0][at(k + 1), :])
+            slopes = [(east(height.value[k]), height.north(k)) for k in group]
+            moved = []
+            for k, (x, y) in zip(group, slopes):
+                half_wet = half_wet_ref[at(k), :]
+                moved.append((src[1][at(k), :] - half_wet * x, src[2][at(k), :] - half_wet * y))
+            for k, (u, v) in zip(group, moved):
+                dst[1][at(k), :] = u
+                dst[2][at(k), :] = v
+            flows = []
+            for k, (u, v) in zip(group, moved):
+                courant = courant_ref[at(k), :]
+                flows.append((courant * u, courant * v))
+            for k, (u, v) in zip(group, flows):
+                spread[k] = east(u)
+                flux.put(k, v)
+            ready = [k for k in range(first - 1, first + GROUP - 1) if k in result]
+            new = [height.value[k] - half_inside(k) * (spread[k] + flux.north(k)) for k in ready]
+            for k, x in zip(ready, new):
+                dst[0][at(k), :] = x
+            for k, x in zip(ready, new):
+                if k in seen:
+                    offset = joined(steps + t, at(k))
+                    source = joined(t, at(k)) * x - offset
+                    source_ref[t, at(k), :] = source
+                    if 0 <= k < tile:
+                        total = total + x[:, left] * (source[:, left] - offset[:, left])
     cost_ref[...] = jnp.broadcast_to(total[None], (cost_ref.shape[0] // 8, 8, cols)).reshape(cost_ref.shape)
     cost_copy = pltpu.make_async_copy(cost_ref, cost_out_ref, cost_sem)
     cost_copy.start()
-    adj = source_ref[steps - 1]
-    adj_u = adj_v = None
+
     for t in range(steps - 1, -1, -1):
-        if t < steps - 1:
-            adj = adj + source_ref[t]
-        du = half_both * east(adj)
-        dv = half_both * north(adj)
-        adj_u = du if adj_u is None else adj_u + du
-        adj_v = dv if adj_v is None else adj_v + dv
-        adj = adj + half_inside * (east(adj_u) + north(adj_v))
-    lam = [x[:rows, :cols] for x in (adj, adj_u, adj_v)]
+        given, flow, result = around(2 * (t + 1)), around(2 * t + 1), around(2 * t)
+        src, dst = states[t % 2], states[1 - t % 2]
+        adj, flux, spread, east_flow = Column(), Column(), {}, {}
+
+        def load(k):
+            x = source_ref[t, at(k), :]
+            adj.put(k, x if t == steps - 1 else x + src[0][at(k), :])
+
+        for k in (flow[0] - 1, flow[0]):
+            if k in given:
+                load(k)
+        for first in range(flow[0], flow[-1] + 2, GROUP):
+            group = [k for k in range(first, first + GROUP) if k in flow]
+            for k in group:
+                if k + 1 in given:
+                    load(k + 1)
+            slopes = [(east(adj.value[k]), adj.north(k)) for k in group]
+            moved = []
+            for k, (x, y) in zip(group, slopes):
+                half_both = half_both_ref[at(k), :]
+                u, v = half_both * x, half_both * y
+                if t < steps - 1:
+                    u = u + src[1][at(k), :]
+                    v = v + src[2][at(k), :]
+                moved.append((u, v))
+            for k, (u, v) in zip(group, moved):
+                spread[k] = east(u)
+                flux.put(k, v)
+            for k, (u, v) in zip(group, moved):
+                if t:
+                    dst[1][at(k), :] = u
+                    dst[2][at(k), :] = v
+                elif 0 <= k < tile:
+                    lam_ref[1, at(k), :] = u[:, left]
+                    lam_ref[2, at(k), :] = v[:, left]
+            ready = [k for k in range(first - 1, first + GROUP - 1) if k in result]
+            new = [adj.value[k] + half_inside(k) * (spread[k] + flux.north(k)) for k in ready]
+            for k, x in zip(ready, new):
+                if t:
+                    dst[0][at(k), :] = x
+                else:
+                    lam_ref[0, at(k), :] = x[:, left]
     for c in range(3):
-        lam_ref[c] = lam[c]
         old = control_ref[c]
-        control_new_ref[c] = old - step_length * (old + std_ref[c] * lam[c])
-    for i in range(members):
-        product_ref[i] = products(perturbations_ref, lam_ref, i).astype(BF16)
+        control_new_ref[c] = old - step_length * (old + std_ref[c] * lam_ref[c])
     cost_copy.wait()
 
 
-def products(perturbations_ref, lam_ref, i):
-    total = perturbations_ref[i, 0].astype(F32) * lam_ref[0]
-    for c in (1, 2):
-        total = total + perturbations_ref[i, c].astype(F32) * lam_ref[c]
-    return total
-
-
-def final_kernel(groups, scale, cost_scale, *refs):
-    parts = refs[:groups]
-    kron_ref, alpha_ref, terms_ref, out_ref, cost_ref = refs[groups:]
+def model_scratch(steps, halo, rows, cols, terms):
+    high = rows + 2 * halo
+    return [
+        pltpu.VMEM((steps, high, 2 * cols), F32),
+        pltpu.VMEM((terms, cols), F32),
+        pltpu.SemaphoreType.DMA,
+        pltpu.VMEM((2 * steps + 5, high, cols), F32),
+    ] + [pltpu.VMEM((high, 2 * cols), F32)] * 9
+
+
+def products_kernel(units, ahead, lam_ref, perturbations_ref, *refs):
+    count = (len(refs) - 2) // 2
+    others, sent_ref, ahead_refs = refs[:count], refs[count], refs[count + 1 :]
+
+    def products(ref, i, at, rows):
+        total = ref[i, 0, at, :].astype(F32) * lam_ref[0, rows, :]
+        for c in (1, 2):
+            total = total + ref[i, c, at, :].astype(F32) * lam_ref[c, rows, :]
+        return total.astype(BF16)
+
+    for i in range(perturbations_ref.shape[0]):
+        for n, y in enumerate(units):
+            rows = slice(y, y + UNIT)
+            sent_ref[i, n * UNIT : (n + 1) * UNIT, :] = products(perturbations_ref, i, rows, rows)
+        for n, y in enumerate(ahead):
+            rows, at = slice(y, y + UNIT), slice(n * UNIT, (n + 1) * UNIT)
+            ahead_refs[0][i, at, :] = products(perturbations_ref, i, rows, rows)
+            for ref, out_ref in zip(others, ahead_refs[1:]):
+                out_ref[i, at, :] = products(ref, i, at, rows)
+
+
+def final_kernel(groups, scale, cost_scale, units, ahead, *refs):
+    late, early = refs[:groups], refs[groups : 2 * groups]
+    kron_ref, alpha_ref, terms_ref, out_ref, cost_ref = refs[2 * groups :]
     members, rows, cols = alpha_ref.shape
     cost_ref[0, 0] = jnp.sum(terms_ref[...]) * cost_scale
-    for y in range(0, rows, UNIT):
-        grad = None
-        for g, part in enumerate(parts):
-            term = jnp.dot(kron_ref[g], pair_of(part, y), preferred_element_type=F32)
-            grad = term if grad is None else grad + term
-        for k in (0, 1):
-            at = slice(y + k * SUB, y + (k + 1) * SUB)
-            part = grad[:, k * cols : (k + 1) * cols].reshape(members, SUB, cols)
-            old = alpha_ref[:, at, :]
-            out_ref[:, at, :] = old - step_length * (old + scale * part)
+    for parts, chunk in ((early, ahead), (late, units)):
+        for n, y in enumerate(chunk):
+            grad = None
+            for g, part in enumerate(parts):
+                term = jnp.dot(kron_ref[g], pair_of(part, n * UNIT), preferred_element_type=F32)
+                grad = term if grad is None else grad + term
+            for k in (0, 1):
+                at = slice(y + k * SUB, y + (k + 1) * SUB)
+                part = grad[:, k * cols : (k + 1) * cols].reshape(members, SUB, cols)
+                old = alpha_ref[:, at, :]
+                out_ref[:, at, :] = old - step_length * (old + scale * part)
 
 
 def to_others(x, groups):
@@ -475,6 +593,8 @@
     at_edge = -(-halo // UNIT)
     outer = units[:at_edge] + units[len(units) - at_edge :]
     inner = units[at_edge : len(units) - at_edge]
+    ahead = inner[: len(units) // 4]
+    behind = [y for y in units if y not in ahead]
 
     def rows_of(chunk, mib, *before):
         shape = (own, len(chunk) * UNIT, cols)
@@ -550,33 +670,33 @@
     from_left = lax.ppermute(to_right, "tx", right)
     from_right = lax.ppermute(to_left, "tx", left)
 
-    control_new, cost_terms, product = call(
+    rows_ahead = jnp.concatenate([perturbations[:, :, y : y + UNIT] for y in ahead], axis=2)
+    rows_ahead, tall = lax.optimization_barrier((rows_ahead, tall))
+    ahead_others = to_others(rows_ahead, groups)
+
+    control_new, cost_terms, lam = call(
         functools.partial(model_kernel, steps, halo),
-        [
-            ((3, rows, cols), F32),
-            ((n_ty * n_tx * 8, cols), F32),
-            ((own, rows, cols), BF16),
-        ],
-        [place, tall, from_right, from_left, early, static_std, control, perturbations],
-        scratch=[
-            pltpu.VMEM((steps, high, 2 * cols), F32),
-            pltpu.VMEM((3, rows, cols), F32),
-            pltpu.VMEM((n_ty * n_tx * 8, cols), F32),
-            pltpu.SemaphoreType.DMA,
-        ],
+        [((3, rows, cols), F32), ((n_ty * n_tx * 8, cols), F32), ((3, rows, cols), F32)],
+        [place, tall, from_right, from_left, early, static_std, control],
+        scratch=model_scratch(steps, halo, rows, cols, n_ty * n_tx * 8),
         out_specs=[VMEM, HBM, VMEM],
         smem=1,
         mib=16,
         name="model",
     )
-    product_others = to_others(product, groups)
+    sent, *products_ahead = call(
+        functools.partial(products_kernel, behind, ahead),
+        [((own, len(behind) * UNIT, cols), BF16)] + [((own, len(ahead) * UNIT, cols), BF16)] * groups,
+        [lam, perturbations, *ahead_others],
+        name="products",
+    )
+    sent_others = to_others(sent, groups)
     terms = lax.all_to_all(cost_terms, ("ty", "tx"), 0, 0, tiled=True)
     cost_scale = 0.5 / ((3 + members) * rows * cols * n_ty * n_tx)
-
     weights_new, cost = call(
-        functools.partial(final_kernel, groups, scale, cost_scale),
+        functools.partial(final_kernel, groups, scale, cost_scale, behind, ahead),
         [((own, rows, cols), F32), ((1, 1), F32)],
-        [product, *product_others, kron_grad, ens_weights, terms],
+        [sent, *sent_others, *products_ahead, kron_grad, ens_weights, terms],
         out_specs=[VMEM, SMEM],
         name="final",
     )

time: 56.4 us -> 54 us (0.957)
  waiting for transfers between devices: 19.1 us -> 17.5 us
  Pallas kernels: 14.5 us -> 13.2 us
    ppermute x4 -> x5, waiting for transfers between devices: 8.98 us -> 7.45 us  [to_others(): lax.ppermute(x, 'ens', [(i, (i - k) % groups) for i in range(groups)])]
    pallas_call x11 -> x12, Pallas kernels: 14.5 us -> 13.2 us  [call(): pl.pallas_call(kernel, out_shape=out_shape, grid=grid, in_specs=in_specs...]
    ppermute x4 -> x5, starting transfers between devices: 6.27 us -> 6.84 us  [to_others(): lax.ppermute(x, 'ens', [(i, (i - k) % groups) for i in range(groups)])]
  transfers between devices with their start and end apart: 8 -> 9, of which waited for: 8 -> 8; matrix products, arithmetic and copies ran while one was open for 0% -> 0% of each run, Pallas kernels for 7% -> 14%
where the time goes in v2:
time: 54 us; the launch traced here: 53.8 us
  waiting for transfers between devices  17.5 us (32%)
  Pallas kernels  13.2 us (24%)
  starting transfers between devices  11.5 us (21%)
  blocking collectives  9.47 us (18%)
  local copies, waits for them, and re-layouts  1.07 us (2%)
  between operations  0.88 us (2%)
    pallas_call x12, Pallas kernels, call(): pl.pallas_call(kernel, out_shape=out_shape, grid=grid, in_specs=in_specs...  13.2 us
    all_to_all x1, blocking collectives, body(): terms = lax.all_to_all(cost_terms, ('ty', 'tx'), 0, 0, tiled=True)  9.47 us
    ppermute x5, waiting for transfers between devices, to_others(): lax.ppermute(x, 'ens', [(i, (i - k) % groups) for i in range(groups)])  7.45 us
    ppermute x5, starting transfers between devices, to_others(): lax.ppermute(x, 'ens', [(i, (i - k) % groups) for i in range(groups)])  6.84 us
    ppermute x1, starting transfers between devices, body(): below = lax.ppermute(top, 'ty', up)  4.19 us
    ppermute x1, waiting for transfers between devices, body(): above = lax.ppermute(bottom, 'ty', down)  4.18 us
    ppermute x1, waiting for transfers between devices, body(): from_left = lax.ppermute(to_right, 'tx', right)  2.74 us
    ppermute x1, waiting for transfers between devices, body(): from_right = lax.ppermute(to_left, 'tx', left)  1.63 us
  transfers between devices with their start and end apart: 9, of which 8 were waited for; matrix products, arithmetic and copies ran while one was open for 0% of the time, Pallas kernels for 14%

profile of v2, /device:TPU:0, one launch (start us, length us, event | category | flops | bytes accessed | tf_op | source)
XLA Modules:
  0.0 53.8 jit_solution(548734537774472182)
XLA Ops:
  0.6 0.0 copy-start.1
  0.6 0.0 copy-start
  0.6 1.9 %send.2.refs_0_ = bf16[16,64,128]{2,1,0:T(8,128)(2,1)} custom-call(f32[16,128,128]{2,1,0:T(8,128)} %refs_5_.1), custom_call_target="tpu_custom_call" | custom-call | bytes 1310720 | tf_op jit(solution)/shard_map/send/pallas_call | solution.py:28
  2.6 3.0 %collective-permute-start = (bf16[16,64,128]{2,1,0:T(8,128)(2,1)}, bf16[16,64,128]{2,1,0:T(8,128)(2,1)S(1)}, u32[]{:S(2)}, u32[]{:S(2)}) collective-permute-start(bf16[16,64,128]{2,1,0:T(8,128)(2,1)} %send.2.refs_0_), channel_id=1, source_target_pairs={{0,16},{16,0},{1,17},{17,1},{2,18},{18,2},{3,19},{19,3},{4,20},{20... | collective-permute-start | bytes 786440 | tf_op jit(solution)/shard_map/ppermute | solution.py:550
  5.6 0.0 copy-done.1
  5.6 1.0 %copy-done.4 = bf16[16,64,128]{2,1,0:T(8,128)(2,1)S(1)} copy-done((bf16[16,64,128]{2,1,0:T(8,128)(2,1)S(1)}, bf16[16,64,128]{2,1,0:T(8,128)(2,1)}, u32[]{:S(2)}) %copy-start.4) | copy-done | bytes 262168
  6.6 0.8 %send.3 = bf16[16,64,128]{2,1,0:T(8,128)(2,1)} custom-call(f32[16,128,128]{2,1,0:T(8,128)S(1)} %copy-done.1, bf16[16,64,128]{2,1,0:T(8,128)(2,1)S(1)} %copy-done.4), custom_call_target="tpu_custom_call" | custom-call | bytes 1572864 | tf_op jit(solution)/shard_map/send/pallas_call | solution.py:28
  7.4 0.0 copy-start.10
  7.4 0.0 copy-start.11
  7.4 0.0 copy-start.3
  7.4 0.1 collective-permute-start.1
  7.5 0.0 copy-done.9
  7.5 0.1 pad_add_fusion.place_ref
  7.6 0.0 copy-done
  7.6 0.0 copy-done.7
  7.6 0.0 copy-done.8
  7.6 1.9 %own.1 = (bf16[2,256,256]{2,1,0:T(8,128)(2,1)S(1)}, bf16[2,256,256]{2,1,0:T(8,128)(2,1)S(1)}, f32[3,128,128]{2,1,0:T(8,128)S(1)}, bf16[48,128]{1,0:T(8,128)(2,1)S(1)}) custom-call(s32[3]{0:T(128)S(1)} %pad_add_fusion.place_ref, s32[32]{0:T(128)S(1)} %copy-done.7, f32[32]{0:T(128)S(1)} %copy-done.8, f32[16,128,128]{2,1,0:T(8,128)S(1)} %copy-done.1, ...), custom_call_target="tpu_custom_call" | custom-call | bytes 3354892 | tf_op jit(solution)/shard_map/own/pallas_call | solution.py:28
  9.5 0.0 copy-done.10
  9.5 0.0 copy-done.11
  9.5 0.0 copy-done.3
  9.5 0.0 copy-start.2
  9.6 0.0 copy-start.5
  9.6 0.0 copy-start.6
  9.6 1.2 %maps.1 = (f32[12,128,128]{2,1,0:T(8,128)S(1)}, f32[8,128]{1,0:T(8,128)S(1)}) custom-call(s32[6,512]{1,0:T(8,128)S(1)} %bitcast.15, f32[6,512]{1,0:T(8,128)S(1)} %get-tuple-element.48.values_ref, f32[6,512]{1,0:T(8,128)S(1)} %get-tuple-element.47.weights_ref, f32[3,128,128]{2,1,0:T(8,128)S(1)} %copy-done.3), custom_call_target="tpu_custom_call" | custom-call | flops 402653184 | bytes 1024000 | tf_op jit(solution)/shard_map/maps/pallas_call | solution.py:28
  10.8 2.2 %collective-permute-done.refs_0_ = bf16[16,64,128]{2,1,0:T(8,128)(2,1)S(1)} collective-permute-done((bf16[16,64,128]{2,1,0:T(8,128)(2,1)}, bf16[16,64,128]{2,1,0:T(8,128)(2,1)S(1)}, u32[]{:S(2)}, u32[]{:S(2)}) %collective-permute-start) | collective-permute-done | bytes 262176 | tf_op jit(solution)/shard_map/ppermute | solution.py:550
  12.9 0.3 outer_share.1.share_ref.outer_ref
  13.3 0.0 copy-done.2
  13.3 4.2 %collective-permute-start.2 = (bf16[320,128]{1,0:T(8,128)(2,1)S(1)}, bf16[320,128]{1,0:T(8,128)(2,1)S(1)}, u32[]{:S(2)}, u32[]{:S(2)}) collective-permute-start(bf16[320,128]{1,0:T(8,128)(2,1)S(1)} %get-tuple-element.28), channel_id=1, source_target_pairs={{4,0},{8,4},{12,8},{0,12},{5,1},{9,5},{13,9},{1,13},{6,2},{10,6},{... | collective-permute-start | bytes 245768 | tf_op jit(solution)/shard_map/ppermute | solution.py:652
  17.5 0.0 collective-permute-start.3
  17.5 0.2 collective-permute-done.1.refs_0_
  17.7 0.3 inner_share.1.inner_ref
  18.0 1.5 %collective-permute-done.2.below_ref = bf16[320,128]{1,0:T(8,128)(2,1)S(1)} collective-permute-done((bf16[320,128]{1,0:T(8,128)(2,1)S(1)}, bf16[320,128]{1,0:T(8,128)(2,1)S(1)}, u32[]{:S(2)}, u32[]{:S(2)}) %collective-permute-start.2) | collective-permute-done | bytes 81952 | tf_op jit(solution)/shard_map/ppermute | solution.py:652
  19.6 4.2 %collective-permute-done.3.above_ref = bf16[320,128]{1,0:T(8,128)(2,1)S(1)} collective-permute-done((bf16[320,128]{1,0:T(8,128)(2,1)S(1)}, bf16[320,128]{1,0:T(8,128)(2,1)S(1)}, u32[]{:S(2)}, u32[]{:S(2)}) %collective-permute-start.3) | collective-permute-done | bytes 81952 | tf_op jit(solution)/shard_map/ppermute | solution.py:651
  23.8 1.6 %collective-permute-start.4 = (bf16[576,128]{1,0:T(8,128)(2,1)S(1)}, bf16[576,128]{1,0:T(8,128)(2,1)S(1)}, u32[]{:S(2)}, u32[]{:S(2)}) collective-permute-start(bf16[576,128]{1,0:T(8,128)(2,1)S(1)} %merge.1.own_ref), channel_id=1, source_target_pairs={{0,16},{16,0},{1,17},{17,1},{2,18},{18,2},{3,19},{19,3},{4,20},{20... | collective-permute-start | bytes 442376 | tf_op jit(solution)/shard_map/ppermute | solution.py:550
  25.4 3.8 %collective-permute-done.4.other_ref = bf16[576,128]{1,0:T(8,128)(2,1)S(1)} collective-permute-done((bf16[576,128]{1,0:T(8,128)(2,1)S(1)}, bf16[576,128]{1,0:T(8,128)(2,1)S(1)}, u32[]{:S(2)}, u32[]{:S(2)}) %collective-permute-start.4) | collective-permute-done | bytes 147488 | tf_op jit(solution)/shard_map/ppermute | solution.py:550
  29.2 1.0 %pack.1 = (f32[17,176,128]{2,1,0:T(8,128)S(1)}, bf16[352,128]{1,0:T(8,128)(2,1)S(1)}, bf16[352,128]{1,0:T(8,128)(2,1)S(1)}, f32[8,128]{1,0:T(8,128)S(1)}) custom-call(s32[3]{0:T(128)S(1)} %pad_add_fusion.place_ref, bf16[576,128]{1,0:T(8,128)(2,1)S(1)} %merge.1.own_ref, bf16[576,128]{1,0:T(8,128)(2,1)S(1)} %collective-permute-done.4.other_ref, ...), custom_call_target="tpu_custom_call" | custom-call | bytes 3489804 | tf_op jit(solution)/shard_map/pack/pallas_call | solution.py:28
  30.2 1.6 %collective-permute-start.7 = (bf16[16,3,32,128]{3,2,1,0:T(8,128)(2,1)S(1)}, bf16[16,3,32,128]{3,2,1,0:T(8,128)(2,1)S(1)}, u32[]{:S(2)}, u32[]{:S(2)}) collective-permute-start(bf16[16,3,32,128]{3,2,1,0:T(8,128)(2,1)S(1)} %slice.3), channel_id=1, source_target_pairs={{0,16},{16,0},{1,17},{17,1},{2,18},{18,2},{3,19},{19,3},{4,20},{20... | collective-permute-start | bytes 1179656 | tf_op jit(solution)/shard_map/ppermute | solution.py:550
  31.8 0.0 collective-permute-start.5
  31.8 0.5 collective-permute-start.6
  32.3 1.6 %collective-permute-done.5.from_right_ref = bf16[352,128]{1,0:T(8,128)(2,1)S(1)} collective-permute-done((bf16[352,128]{1,0:T(8,128)(2,1)S(1)}, bf16[352,128]{1,0:T(8,128)(2,1)S(1)}, u32[]{:S(2)}, u32[]{:S(2)}) %collective-permute-start.5) | collective-permute-done | bytes 90144 | tf_op jit(solution)/shard_map/ppermute | solution.py:671
  34.0 2.7 %collective-permute-done.6.from_left_ref = bf16[352,128]{1,0:T(8,128)(2,1)S(1)} collective-permute-done((bf16[352,128]{1,0:T(8,128)(2,1)S(1)}, bf16[352,128]{1,0:T(8,128)(2,1)S(1)}, u32[]{:S(2)}, u32[]{:S(2)}) %collective-permute-start.6) | collective-permute-done | bytes 90144 | tf_op jit(solution)/shard_map/ppermute | solution.py:670
  36.7 4.0 %model.1 = (f32[3,128,128]{2,1,0:T(8,128)}, f32[128,128]{1,0:T(8,128)S(1)}, f32[3,128,128]{2,1,0:T(8,128)S(1)}) custom-call(s32[3]{0:T(128)S(1)} %pad_add_fusion.place_ref, f32[17,176,128]{2,1,0:T(8,128)S(1)} %get-tuple-element.33.tall_ref, bf16[352,128]{1,0:T(8,128)(2,1)S(1)} %collective-permute-done.5.from_right_ref, ...), custom_call_target="tpu_custom_call" | custom-call | bytes 2568204 | tf_op jit(solution)/shard_map/model/pallas_call | solution.py:28
  40.7 0.0 collective-permute-done.7.refs_0_
  40.7 0.4 products.1
  41.1 0.6 %collective-permute-start.8 = (bf16[16,96,128]{2,1,0:T(8,128)(2,1)S(1)}, bf16[16,96,128]{2,1,0:T(8,128)(2,1)S(1)}, u32[]{:S(2)}, u32[]{:S(2)}) collective-permute-start(bf16[16,96,128]{2,1,0:T(8,128)(2,1)S(1)} %get-tuple-element.40.refs_0_), channel_id=1, source_target_pairs={{0,16},{16,0},{1,17},{17,1},{2,18},{18,2},{3,19},{19,3},{4,20},{20... | collective-permute-start | bytes 1179656 | tf_op jit(solution)/shard_map/ppermute | solution.py:550
  41.7 9.5 %all_to_all.11 = f32[16,8,128]{2,1,0:T(8,128)S(1)} all-to-all(f32[16,8,128]{2,1,0:T(8,128)S(1)} %bitcast.14), channel_id=1, replica_groups=mesh['ens'=2,'ty'=4,'tx'=4] {'ty','tx'}, dimensions={0} | all-to-all | bytes 131072 | tf_op jit(solution)/shard_map/all_to_all | solution.py:694
  51.2 1.2 %collective-permute-done.8.refs_1_ = bf16[16,96,128]{2,1,0:T(8,128)(2,1)S(1)} collective-permute-done((bf16[16,96,128]{2,1,0:T(8,128)(2,1)S(1)}, bf16[16,96,128]{2,1,0:T(8,128)(2,1)S(1)}, u32[]{:S(2)}, u32[]{:S(2)}) %collective-permute-start.8) | collective-permute-done | bytes 393248 | tf_op jit(solution)/shard_map/ppermute | solution.py:550
  52.4 1.4 %final.1 = (f32[16,128,128]{2,1,0:T(8,128)}, f32[1,1]{1,0:T(1,128)}) custom-call(bf16[16,96,128]{2,1,0:T(8,128)(2,1)S(1)} %get-tuple-element.40.refs_0_, bf16[16,96,128]{2,1,0:T(8,128)(2,1)S(1)} %collective-permute-done.8.refs_1_, bf16[16,32,128]{2,1,0:T(8,128)(2,1)S(1)} %get-tuple-element.41.refs_2_, bf16[16,32,128]{2,1,0:T(8,128)(2,1)S(1)} %get-tuple-element.42.refs_3_, ...), custom_call_target="tpu_custom_call" | custom-call | bytes 3473412 | tf_op jit(solution)/shard_map/final/pallas_call | solution.py:28
  (11 shorter events, 0.1 us)
Async XLA Ops:
  0.6 5.0 %copy-start.1 = (f32[16,128,128]{2,1,0:T(8,128)S(1)}, f32[16,128,128]{2,1,0:T(8,128)}, u32[]{:S(2)}) copy-start(f32[16,128,128]{2,1,0:T(8,128)} %refs_5_.1) | copy-start | bytes 3145732
  0.6 7.0 %copy-start = (bf16[16,3,128,128]{3,2,1,0:T(8,128)(2,1)S(1)}, bf16[16,3,128,128]{3,2,1,0:T(8,128)(2,1)}, u32[]{:S(2)}) copy-start(bf16[16,3,128,128]{3,2,1,0:T(8,128)(2,1)} %perturbations_ref.3) | copy-start | bytes 4718596
  2.6 10.4 %collective-permute-start = (bf16[16,64,128]{2,1,0:T(8,128)(2,1)}, bf16[16,64,128]{2,1,0:T(8,128)(2,1)S(1)}, u32[]{:S(2)}, u32[]{:S(2)}) collective-permute-start(bf16[16,64,128]{2,1,0:T(8,128)(2,1)} %send.2.refs_0_), channel_id=1, source_target_pairs={{0,16},{16,0},{1,17},{17,1},{2,18},{18,2},{3,19},{19,3},{4,20},{20... | collective-permute-start | bytes 786440 | tf_op jit(solution)/shard_map/ppermute | solution.py:550
  5.6 1.0 %copy-start.4 = (bf16[16,64,128]{2,1,0:T(8,128)(2,1)S(1)}, bf16[16,64,128]{2,1,0:T(8,128)(2,1)}, u32[]{:S(2)}) copy-start(bf16[16,64,128]{2,1,0:T(8,128)(2,1)} %send.2.refs_0_) | copy-start | bytes 786436
  6.6 0.9 %copy-start.9 = (s32[1,1,6,512]{3,1,2,0:T(1,128)S(1)}, s32[1,1,6,512]{3,1,2,0:T(1,128)}, u32[]{:S(2)}) copy-start(s32[1,1,6,512]{3,1,2,0:T(1,128)} %param.19) | copy-start | bytes 36868
  6.6 1.0 %copy-start.7 = (s32[32]{0:T(128)S(1)}, s32[32]{0:T(128)}, u32[]{:S(2)}) copy-start(s32[32]{0:T(128)} %offsets_ref.1) | copy-start | bytes 388
  6.6 1.0 %copy-start.8 = (f32[32]{0:T(128)S(1)}, f32[32]{0:T(128)}, u32[]{:S(2)}) copy-start(f32[32]{0:T(128)} %weights_ref.1) | copy-start | bytes 388
  7.4 2.1 %copy-start.10 = (f32[1,1,6,512]{3,1,2,0:T(1,128)S(1)}, f32[1,1,6,512]{3,1,2,0:T(1,128)}, u32[]{:S(2)}) copy-start(f32[1,1,6,512]{3,1,2,0:T(1,128)} %param.21) | copy-start | bytes 36868
  7.4 2.1 %copy-start.11 = (f32[1,1,6,512]{3,1,2,0:T(1,128)S(1)}, f32[1,1,6,512]{3,1,2,0:T(1,128)}, u32[]{:S(2)}) copy-start(f32[1,1,6,512]{3,1,2,0:T(1,128)} %param.20) | copy-start | bytes 36868
  7.4 2.1 %copy-start.3 = (f32[3,128,128]{2,1,0:T(8,128)S(1)}, f32[3,128,128]{2,1,0:T(8,128)}, u32[]{:S(2)}) copy-start(f32[3,128,128]{2,1,0:T(8,128)} %control_ref.7) | copy-start | bytes 589828
  7.4 10.3 %collective-permute-start.1 = (bf16[16,64,128]{2,1,0:T(8,128)(2,1)}, bf16[16,64,128]{2,1,0:T(8,128)(2,1)S(1)}, u32[]{:S(2)}, u32[]{:S(2)}) collective-permute-start(bf16[16,64,128]{2,1,0:T(8,128)(2,1)} %send.3), channel_id=1, source_target_pairs={{0,16},{16,0},{1,17},{17,1},{2,18},{18,2},{3,19},{19,3},{4,20},{20... | collective-permute-start | bytes 786440 | tf_op jit(solution)/shard_map/ppermute | solution.py:550
  9.5 3.7 %copy-start.2 = (f32[3,128,128]{2,1,0:T(8,128)S(1)}, f32[3,128,128]{2,1,0:T(8,128)}, u32[]{:S(2)}) copy-start(f32[3,128,128]{2,1,0:T(8,128)} %std_ref.5) | copy-start | bytes 589828
  9.6 3.7 %copy-start.5 = (f32[128,128]{1,0:T(8,128)S(1)}, f32[128,128]{1,0:T(8,128)}, u32[]{:S(2)}) copy-start(f32[128,128]{1,0:T(8,128)} %courant_ref.3) | copy-start | bytes 196612
  9.6 3.7 %copy-start.6 = (s32[128,128]{1,0:T(8,128)S(1)}, s32[128,128]{1,0:T(8,128)}, u32[]{:S(2)}) copy-start(s32[128,128]{1,0:T(8,128)} %mask_ref.3) | copy-start | bytes 196612
  13.3 6.3 %collective-permute-start.2 = (bf16[320,128]{1,0:T(8,128)(2,1)S(1)}, bf16[320,128]{1,0:T(8,128)(2,1)S(1)}, u32[]{:S(2)}, u32[]{:S(2)}) collective-permute-start(bf16[320,128]{1,0:T(8,128)(2,1)S(1)} %get-tuple-element.28), channel_id=1, source_target_pairs={{4,0},{8,4},{12,8},{0,12},{5,1},{9,5},{13,9},{1,13},{6,2},{10,6},{... | collective-permute-start | bytes 245768 | tf_op jit(solution)/shard_map/ppermute | solution.py:652
  17.5 6.2 %collective-permute-start.3 = (bf16[320,128]{1,0:T(8,128)(2,1)S(1)}, bf16[320,128]{1,0:T(8,128)(2,1)S(1)}, u32[]{:S(2)}, u32[]{:S(2)}) collective-permute-start(bf16[320,128]{1,0:T(8,128)(2,1)S(1)} %get-tuple-element.29), channel_id=1, source_target_pairs={{0,4},{4,8},{8,12},{12,0},{1,5},{5,9},{9,13},{13,1},{2,6},{6,10},{... | collective-permute-start | bytes 245768 | tf_op jit(solution)/shard_map/ppermute | solution.py:651
  23.8 5.5 %collective-permute-start.4 = (bf16[576,128]{1,0:T(8,128)(2,1)S(1)}, bf16[576,128]{1,0:T(8,128)(2,1)S(1)}, u32[]{:S(2)}, u32[]{:S(2)}) collective-permute-start(bf16[576,128]{1,0:T(8,128)(2,1)S(1)} %merge.1.own_ref), channel_id=1, source_target_pairs={{0,16},{16,0},{1,17},{17,1},{2,18},{18,2},{3,19},{19,3},{4,20},{20... | collective-permute-start | bytes 442376 | tf_op jit(solution)/shard_map/ppermute | solution.py:550
  30.2 10.5 %collective-permute-start.7 = (bf16[16,3,32,128]{3,2,1,0:T(8,128)(2,1)S(1)}, bf16[16,3,32,128]{3,2,1,0:T(8,128)(2,1)S(1)}, u32[]{:S(2)}, u32[]{:S(2)}) collective-permute-start(bf16[16,3,32,128]{3,2,1,0:T(8,128)(2,1)S(1)} %slice.3), channel_id=1, source_target_pairs={{0,16},{16,0},{1,17},{17,1},{2,18},{18,2},{3,19},{19,3},{4,20},{20... | collective-permute-start | bytes 1179656 | tf_op jit(solution)/shard_map/ppermute | solution.py:550
  31.8 2.1 %collective-permute-start.5 = (bf16[352,128]{1,0:T(8,128)(2,1)S(1)}, bf16[352,128]{1,0:T(8,128)(2,1)S(1)}, u32[]{:S(2)}, u32[]{:S(2)}) collective-permute-start(bf16[352,128]{1,0:T(8,128)(2,1)S(1)} %get-tuple-element.34), channel_id=1, source_target_pairs={{1,0},{2,1},{3,2},{0,3},{5,4},{6,5},{7,6},{4,7},{9,8},{10,9},{11,1... | collective-permute-start | bytes 270344 | tf_op jit(solution)/shard_map/ppermute | solution.py:671
  31.8 4.9 %collective-permute-start.6 = (bf16[352,128]{1,0:T(8,128)(2,1)S(1)}, bf16[352,128]{1,0:T(8,128)(2,1)S(1)}, u32[]{:S(2)}, u32[]{:S(2)}) collective-permute-start(bf16[352,128]{1,0:T(8,128)(2,1)S(1)} %get-tuple-element.35), channel_id=1, source_target_pairs={{0,1},{1,2},{2,3},{3,0},{4,5},{5,6},{6,7},{7,4},{8,9},{9,10},{10,1... | collective-permute-start | bytes 270344 | tf_op jit(solution)/shard_map/ppermute | solution.py:670
  41.1 11.2 %collective-permute-start.8 = (bf16[16,96,128]{2,1,0:T(8,128)(2,1)S(1)}, bf16[16,96,128]{2,1,0:T(8,128)(2,1)S(1)}, u32[]{:S(2)}, u32[]{:S(2)}) collective-permute-start(bf16[16,96,128]{2,1,0:T(8,128)(2,1)S(1)} %get-tuple-element.40.refs_0_), channel_id=1, source_target_pairs={{0,16},{16,0},{1,17},{17,1},{2,18},{18,2},{3,19},{19,3},{4,20},{20... | collective-permute-start | bytes 1179656 | tf_op jit(solution)/shard_map/ppermute | solution.py:550

commit v3 on v2

--- a/solution.py
+++ b/solution.py
@@ -173,10 +173,13 @@
         beta = jnp.dot(matrix, hi, preferred_element_type=F32) + jnp.dot(matrix, lo, preferred_element_type=F32)
         for at, c, total in shares(beta, perturbations_ref, y):
             share_ref[c, y + at : y + at + SUB, :] = total
-    for k in range(PIECES):
-        piece = square.astype(BF16).astype(F32)
-        square = square - piece
-        square_ref[k * SUB : (k + 1) * SUB, :] = jnp.concatenate([piece, jnp.zeros_like(square)], axis=0).astype(BF16)
+    rest = jnp.sum(square, axis=0, keepdims=True)
+    pieces = []
+    for _ in range(PIECES):
+        pieces.append(rest.astype(BF16).astype(F32))
+        rest = rest - pieces[-1]
+    pieces.append(jnp.zeros((SUB - PIECES, cols), F32))
+    square_ref[...] = jnp.concatenate(pieces, axis=0).astype(BF16)
 
 
 def share_kernel(groups, units, *refs):
@@ -237,11 +240,9 @@
     out_ref[3 * rows + 6 * halo :, :] = square_ref[...]
 
 
-def lane_pack(fields, widths):
+def lane_pack(fields, widths, at=0, left=None, right=None):
     cols = fields[0].shape[1]
     lane = lax.broadcasted_iota(jnp.int32, fields[0].shape, 1)
-    left = right = None
-    at = 0
     for field, width in zip(fields, widths):
         to_left = field if at == 0 else pltpu.roll(field, at, 1)
         to_right = field if at == 0 else pltpu.roll(field, cols - at, 1)
@@ -264,6 +265,36 @@
     maps = [[(part * steps + t, 2 * (t + 1)) for t in range(steps)] for part in (0, 1)]
     at = 2 * steps
     return [maps[0] + [(at + 2 + c, halo) for c in range(3)], maps[1] + [(at, halo), (at + 1, halo)]]
+
+
+def tall_rows(place_ref, tile, lower, upper, halo, out_ref):
+    rows, cols = tile.shape
+    size = lower.shape[0]
+    parts = [jnp.where(place_ref[1] == 1, 0.0, lower), jnp.where(place_ref[0] == 1, 0.0, upper)]
+    if size < halo:
+        parts.insert(1, jnp.zeros((2 * (halo - size), cols), F32))
+    out_ref[:rows, :] = tile
+    out_ref[rows:, :] = jnp.concatenate(parts, axis=0)
+
+
+def static_pack_kernel(
+    steps, halo, place_ref, maps_ref, courant_ref, mask_ref, below_ref, above_ref, tall_ref, left_ref, right_ref
+):
+    sizes = row_sizes(steps, halo)
+    fields = 2 * steps + 2
+    below, above = below_ref[...].astype(F32), above_ref[...].astype(F32)
+    at = 0
+    for k in range(fields):
+        tile = maps_ref[k] if k < 2 * steps else courant_ref[...] if k == 2 * steps else mask_ref[...].astype(F32)
+        end = at + sizes[k]
+        tall_rows(place_ref, tile, below[at:end], above[at:end], halo, tall_ref.at[k])
+        at = end
+    high = tall_ref.shape[1]
+    for n, block in enumerate(lane_blocks(steps, halo)):
+        kept = [(k, w) for k, w in block if k < fields]
+        left, right = lane_pack([tall_ref[k] for k, _ in kept], [w for _, w in kept])
+        left_ref[n * high : (n + 1) * high, :] = left.astype(BF16)
+        right_ref[n * high : (n + 1) * high, :] = right.astype(BF16)
 
 
 def pack_kernel(
@@ -276,55 +307,43 @@
     std_ref,
     control_ref,
     early_ref,
-    maps_ref,
-    courant_ref,
-    mask_ref,
     below_ref,
     above_ref,
-    tall_ref,
+    static_left_ref,
+    static_right_ref,
+    inc_ref,
     left_ref,
     right_ref,
     cost_ref,
 ):
-    rows, cols = courant_ref.shape
-    fields = 2 * steps + 2
-    for k in range(2 * steps):
-        tall_ref[k, :rows, :] = maps_ref[k]
-    tall_ref[2 * steps, :rows, :] = courant_ref[...]
-    tall_ref[2 * steps + 1, :rows, :] = mask_ref[...].astype(F32)
+    _, rows, cols = control_ref.shape
+    at = slice(3 * rows, 3 * rows + 6 * halo)
+    beside = scale * (own_ref[at, :].astype(F32) + other_ref[at, :].astype(F32))
+    at = 3 * rows + 6 * halo
+    squares = own_ref[at : at + SUB, :].astype(F32) + other_ref[at : at + SUB, :].astype(F32)
+    cost_ref[...] = early_ref[...] + squares[:8]
+    below, above = below_ref[...].astype(F32), above_ref[...].astype(F32)
+    first = sum(row_sizes(steps, halo)[: 2 * steps + 2])
     for c in range(3):
         at = slice(c * rows, (c + 1) * rows)
         total = own_ref[at, :].astype(F32) + other_ref[at, :].astype(F32)
-        tall_ref[fields + c, :rows, :] = std_ref[c] * control_ref[c] + scale * total
-    at = slice(3 * rows, 3 * rows + 6 * halo)
-    beside = scale * (own_ref[at, :].astype(F32) + other_ref[at, :].astype(F32))
-    at = 3 * rows + 6 * halo
-    squares = [
-        sum(ref[at + k * SUB : at + (k + 1) * SUB, :].astype(F32) for k in range(PIECES)) for ref in (own_ref, other_ref)
-    ]
-    cost_ref[...] = early_ref[...] + (squares[0] + squares[1])[:8]
-    sizes = row_sizes(steps, halo)
-    below_outside, above_outside = place_ref[1] == 1, place_ref[0] == 1
-    below, above = below_ref[...].astype(F32), above_ref[...].astype(F32)
-    at = 0
-    for k in range(fields + 3):
-        size = sizes[k]
-        lower, upper = below[at : at + size], above[at : at + size]
-        if k >= fields:
-            c = k - fields
-            lower = lower + beside[c * halo : (c + 1) * halo]
-            upper = upper + beside[(3 + c) * halo : (4 + c) * halo]
-        at += size
-        parts = [jnp.where(below_outside, 0.0, lower), jnp.where(above_outside, 0.0, upper)]
-        if size < halo:
-            parts.insert(1, jnp.zeros((2 * (halo - size), cols), F32))
-        tall_ref[k, rows:, :] = jnp.concatenate(parts, axis=0)
-    height = rows + 2 * halo
-    for n, block in enumerate(lane_blocks(steps, halo)):
-        values = [tall_ref[k] for k, _ in block]
-        left, right = lane_pack(values, [w for _, w in block])
-        left_ref[n * height : (n + 1) * height, :] = left.astype(BF16)
-        right_ref[n * height : (n + 1) * height, :] = right.astype(BF16)
+        at = slice(first + c * halo, first + (c + 1) * halo)
+        lower = below[at] + beside[c * halo : (c + 1) * halo]
+        upper = above[at] + beside[(3 + c) * halo : (4 + c) * halo]
+        tall_rows(place_ref, std_ref[c] * control_ref[c] + scale * total, lower, upper, halo, inc_ref.at[c])
+    high = rows + 2 * halo
+    taken = sum(2 * (t + 1) for t in range(steps))
+    left, right = lane_pack(
+        [inc_ref[c] for c in range(3)],
+        [halo] * 3,
+        taken,
+        static_left_ref[:high, :].astype(F32),
+        static_right_ref[:high, :].astype(F32),
+    )
+    left_ref[:high, :] = left.astype(BF16)
+    right_ref[:high, :] = right.astype(BF16)
+    left_ref[high:, :] = static_left_ref[high:, :]
+    right_ref[high:, :] = static_right_ref[high:, :]
 
 
 def model_kernel(
@@ -332,6 +351,7 @@
     halo,
     place_ref,
     tall_ref,
+    inc_ref,
     from_right_ref,
     from_left_ref,
     early_ref,
@@ -393,7 +413,8 @@
             place += size
 
     def joined(k, rows_at):
-        return jnp.concatenate([tall_ref[k, rows_at, :], sides_ref[k, rows_at, :]], axis=1)
+        main = tall_ref[k, rows_at, :] if k < fields else inc_ref[k - fields, rows_at, :]
+        return jnp.concatenate([main, sides_ref[k, rows_at, :]], axis=1)
 
     for k in around(halo):
         wet, courant = joined(2 * steps + 1, at(k)), joined(2 * steps, at(k))
@@ -444,7 +465,7 @@
                     source_ref[t, at(k), :] = source
                     if 0 <= k < tile:
                         total = total + x[:, left] * (source[:, left] - offset[:, left])
-    cost_ref[...] = jnp.broadcast_to(total[None], (cost_ref.shape[0] // 8, 8, cols)).reshape(cost_ref.shape)
+    cost_ref[...] = jnp.broadcast_to(jnp.sum(total, axis=0, keepdims=True), cost_ref.shape)
     cost_copy = pltpu.make_async_copy(cost_ref, cost_out_ref, cost_sem)
     cost_copy.start()
 
@@ -507,6 +528,11 @@
     ] + [pltpu.VMEM((high, 2 * cols), F32)] * 9
 
 
+def ahead_kernel(ahead, perturbations_ref, early_ref, out_ref):
+    for n, y in enumerate(ahead):
+        out_ref[:, :, n * UNIT : (n + 1) * UNIT, :] = perturbations_ref[:, :, y : y + UNIT, :]
+
+
 def products_kernel(units, ahead, lam_ref, perturbations_ref, *refs):
     count = (len(refs) - 2) // 2
     others, sent_ref, ahead_refs = refs[:count], refs[count], refs[count + 1 :]
@@ -611,7 +637,6 @@
 
     outer_sent = rows_of(outer, 56)
     outer_others = to_others(outer_sent, groups)
-    inner_others = to_others(rows_of(inner, 4, outer_sent), groups)
 
     cells, values, weights = (x.reshape(steps, x.shape[-1]) for x in (obs_cells, obs_values, obs_weights))
     maps, early = call(
@@ -624,12 +649,14 @@
     wide = own * SUB
     kron_beta, kron_grad, own_share, square = call(
         functools.partial(own_kernel, groups),
-        [((groups, wide, wide), BF16)] * 2 + [((3, rows, cols), F32), ((PIECES * SUB, cols), BF16)],
+        [((groups, wide, wide), BF16)] * 2 + [((3, rows, cols), F32), ((SUB, cols), BF16)],
         [place, band_offsets, band_weights, ens_weights, perturbations],
         in_specs=[SMEM, SMEM, SMEM, HBM, VMEM],
         scratch=[pltpu.VMEM((own, rows, cols), F32), pltpu.SemaphoreType.DMA],
         name="own",
     )
+
+    inner_others = to_others(rows_of(inner, 4, square), groups)
 
     def share_of(units, others, name):
         (share,) = call(
@@ -654,31 +681,43 @@
     inner_share = share_of(inner, inner_others, "inner_share")
     (share,) = call(
         functools.partial(merge_kernel, steps, halo, outer, inner),
-        [((3 * rows + 6 * halo + PIECES * SUB, cols), BF16)],
+        [((3 * rows + 6 * halo + SUB, cols), BF16)],
         [outer_share, inner_share, below, above, square],
         name="merge",
     )
     share, share_other = sum_parts(share, groups)
     high = rows + 2 * halo
-    tall, to_left, to_right, early = call(
+    packed = [((2 * high, cols), BF16)] * 2
+    tall, static_left, static_right = call(
+        functools.partial(static_pack_kernel, steps, halo),
+        [((2 * steps + 2, high, cols), F32)] + packed,
+        [place, maps, courant, land_mask, below, above],
+        smem=1,
+        name="static_pack",
+    )
+    inc, to_left, to_right, early = call(
         functools.partial(pack_kernel, steps, halo, scale),
-        [((2 * steps + 5, high, cols), F32), ((2 * high, cols), BF16), ((2 * high, cols), BF16), ((8, cols), F32)],
-        [place, share, share_other, static_std, control, early, maps, courant, land_mask, below, above],
+        [((3, high, cols), F32)] + packed + [((8, cols), F32)],
+        [place, share, share_other, static_std, control, early, below, above, static_left, static_right],
         smem=1,
         name="pack",
     )
     from_left = lax.ppermute(to_right, "tx", right)
     from_right = lax.ppermute(to_left, "tx", left)
 
-    rows_ahead = jnp.concatenate([perturbations[:, :, y : y + UNIT] for y in ahead], axis=2)
-    rows_ahead, tall = lax.optimization_barrier((rows_ahead, tall))
+    (rows_ahead,) = call(
+        functools.partial(ahead_kernel, ahead),
+        [((own, 3, len(ahead) * UNIT, cols), BF16)],
+        [perturbations, early],
+        name="ahead",
+    )
     ahead_others = to_others(rows_ahead, groups)
 
     control_new, cost_terms, lam = call(
         functools.partial(model_kernel, steps, halo),
-        [((3, rows, cols), F32), ((n_ty * n_tx * 8, cols), F32), ((3, rows, cols), F32)],
-        [place, tall, from_right, from_left, early, static_std, control],
-        scratch=model_scratch(steps, halo, rows, cols, n_ty * n_tx * 8),
+        [((3, rows, cols), F32), ((n_ty * n_tx, cols), F32), ((3, rows, cols), F32)],
+        [place, tall, inc, from_right, from_left, early, static_std, control],
+        scratch=model_scratch(steps, halo, rows, cols, n_ty * n_tx),
         out_specs=[VMEM, HBM, VMEM],
         smem=1,
         mib=16,

time: 54 us -> 53.3 us (0.987)
  waiting for transfers between devices: 17.5 us -> 15.2 us
  local copies, waits for them, and re-layouts: 1.07 us -> 2.77 us
  starting transfers between devices: 11.5 us -> 12.1 us
    unnamed x26, local copies, waits for them, and re-layouts: 1.05 us -> 2.77 us
    ppermute x1, waiting for transfers between devices: 1.53 us -> 0.01 us  [body(): below = lax.ppermute(top, 'ty', up)]
    ppermute x5, starting transfers between devices: 6.84 us -> 8.02 us  [to_others(): lax.ppermute(x, 'ens', [(i, (i - k) % groups) for i in range(groups)])]
    ppermute x5, waiting for transfers between devices: 7.45 us -> 6.76 us  [to_others(): lax.ppermute(x, 'ens', [(i, (i - k) % groups) for i in range(groups)])]
    ppermute x1, starting transfers between devices: 4.19 us -> 3.62 us  [body(): below = lax.ppermute(top, 'ty', up)]
    pallas_call x12 -> x14, Pallas kernels: 13.2 us -> 13.1 us  [call(): pl.pallas_call(kernel, out_shape=out_shape, grid=grid, in_specs=in_specs...]
  transfers between devices with their start and end apart: 9 -> 9, of which waited for: 8 -> 7; matrix products, arithmetic and copies ran while one was open for 0% -> 0% of each run, Pallas kernels for 14% -> 16%
where the time goes in v3:
time: 53.3 us; the launch traced here: 53.1 us
  waiting for transfers between devices  15.2 us (29%)
  Pallas kernels  13.1 us (25%)
  starting transfers between devices  12.1 us (23%)
  blocking collectives  8.97 us (17%)
  local copies, waits for them, and re-layouts  2.77 us (5%)
  between operations  0.85 us (2%)
    pallas_call x14, Pallas kernels, call(): pl.pallas_call(kernel, out_shape=out_shape, grid=grid, in_specs=in_specs...  13.1 us
    all_to_all x1, blocking collectives, body(): terms = lax.all_to_all(cost_terms, ('ty', 'tx'), 0, 0, tiled=True)  8.97 us
    ppermute x5, starting transfers between devices, to_others(): lax.ppermute(x, 'ens', [(i, (i - k) % groups) for i in range(groups)])  8.02 us
    ppermute x5, waiting for transfers between devices, to_others(): lax.ppermute(x, 'ens', [(i, (i - k) % groups) for i in range(groups)])  6.76 us
    ppermute x1, waiting for transfers between devices, body(): above = lax.ppermute(bottom, 'ty', down)  4.08 us
    ppermute x1, starting transfers between devices, body(): below = lax.ppermute(top, 'ty', up)  3.62 us
    unnamed x26, local copies, waits for them, and re-layouts  2.77 us
    ppermute x1, waiting for transfers between devices, body(): from_left = lax.ppermute(to_right, 'tx', right)  2.74 us
  transfers between devices with their start and end apart: 9, of which 7 were waited for; matrix products, arithmetic and copies ran while one was open for 0% of the time, Pallas kernels for 16%

profile of v3, /device:TPU:0, one launch (start us, length us, event | category | flops | bytes accessed | tf_op | source)
XLA Modules:
  0.0 53.1 jit_solution(1005650331391332152)
XLA Ops:
  0.6 0.0 copy-start.2
  0.6 1.9 %send.2 = bf16[16,64,128]{2,1,0:T(8,128)(2,1)} custom-call(f32[16,128,128]{2,1,0:T(8,128)} %refs_5_.1), custom_call_target="tpu_custom_call" | custom-call | bytes 1310720 | tf_op jit(solution)/shard_map/send/pallas_call | solution.py:28
  2.5 3.0 %collective-permute-start = (bf16[16,64,128]{2,1,0:T(8,128)(2,1)}, bf16[16,64,128]{2,1,0:T(8,128)(2,1)S(1)}, u32[]{:S(2)}, u32[]{:S(2)}) collective-permute-start(bf16[16,64,128]{2,1,0:T(8,128)(2,1)} %send.2), channel_id=1, source_target_pairs={{0,16},{16,0},{1,17},{17,1},{2,18},{18,2},{3,19},{19,3},{4,20},{20... | collective-permute-start | bytes 786440 | tf_op jit(solution)/shard_map/ppermute | solution.py:576
  5.5 0.1 pad_add_fusion.place_ref
  5.6 0.0 copy-done.2
  5.6 1.4 %copy-done = bf16[16,3,128,128]{3,2,1,0:T(8,128)(2,1)S(1)} copy-done((bf16[16,3,128,128]{3,2,1,0:T(8,128)(2,1)S(1)}, bf16[16,3,128,128]{3,2,1,0:T(8,128)(2,1)}, u32[]{:S(2)}) %copy-start) | copy-done | bytes 1572888
  7.0 0.7 %copy-done.7 = s32[32]{0:T(128)S(1)} copy-done((s32[32]{0:T(128)S(1)}, s32[32]{0:T(128)}, u32[]{:S(2)}) %copy-start.7) | copy-done | bytes 152
  7.7 0.7 %copy-done.8 = f32[32]{0:T(128)S(1)} copy-done((f32[32]{0:T(128)S(1)}, f32[32]{0:T(128)}, u32[]{:S(2)}) %copy-start.8) | copy-done | bytes 152
  8.3 1.8 %own.1 = (bf16[2,256,256]{2,1,0:T(8,128)(2,1)S(1)}, bf16[2,256,256]{2,1,0:T(8,128)(2,1)S(1)}, f32[3,128,128]{2,1,0:T(8,128)S(1)}, bf16[16,128]{1,0:T(8,128)(2,1)S(1)}) custom-call(s32[3]{0:T(128)S(1)} %pad_add_fusion.place_ref, s32[32]{0:T(128)S(1)} %copy-done.7, f32[32]{0:T(128)S(1)} %copy-done.8, f32[16,128,128]{2,1,0:T(8,128)S(1)} %copy-done.2, ...), custom_call_target="tpu_custom_call" | custom-call | bytes 3346700 | tf_op jit(solution)/shard_map/own/pallas_call | solution.py:28
  10.2 0.0 copy-start.1
  10.2 0.1 send.3
  10.3 0.1 collective-permute-start.3
  10.4 0.0 copy-done.9
  10.4 0.0 copy-done.10
  10.4 0.0 copy-done.11
  10.4 0.0 copy-done.3
  10.4 0.0 copy-start.4
  10.5 0.0 copy-start.5
  10.5 0.0 copy-start.6
  10.5 1.2 %maps.1 = (f32[12,128,128]{2,1,0:T(8,128)S(1)}, f32[8,128]{1,0:T(8,128)S(1)}) custom-call(s32[6,512]{1,0:T(8,128)S(1)} %bitcast.16, f32[6,512]{1,0:T(8,128)S(1)} %get-tuple-element.50.values_ref, f32[6,512]{1,0:T(8,128)S(1)} %get-tuple-element.49.weights_ref, f32[3,128,128]{2,1,0:T(8,128)S(1)} %copy-done.3), custom_call_target="tpu_custom_call" | custom-call | flops 402653184 | bytes 1024000 | tf_op jit(solution)/shard_map/maps/pallas_call | solution.py:28
  11.7 0.6 %collective-permute-done.refs_0_ = bf16[16,64,128]{2,1,0:T(8,128)(2,1)S(1)} collective-permute-done((bf16[16,64,128]{2,1,0:T(8,128)(2,1)}, bf16[16,64,128]{2,1,0:T(8,128)(2,1)S(1)}, u32[]{:S(2)}, u32[]{:S(2)}) %collective-permute-start) | collective-permute-done | bytes 262176 | tf_op jit(solution)/shard_map/ppermute | solution.py:576
  12.3 0.0 copy-done.1
  12.3 0.3 outer_share.1.share_ref.outer_ref
  12.6 0.0 copy-done.4
  12.6 0.0 copy-done.5
  12.6 0.0 copy-done.6
  12.7 3.6 %collective-permute-start.1 = (bf16[320,128]{1,0:T(8,128)(2,1)S(1)}, bf16[320,128]{1,0:T(8,128)(2,1)S(1)}, u32[]{:S(2)}, u32[]{:S(2)}) collective-permute-start(bf16[320,128]{1,0:T(8,128)(2,1)S(1)} %get-tuple-element.29), channel_id=1, source_target_pairs={{4,0},{8,4},{12,8},{0,12},{5,1},{9,5},{13,9},{1,13},{6,2},{10,6},{... | collective-permute-start | bytes 245768 | tf_op jit(solution)/shard_map/ppermute | solution.py:679
  16.3 0.0 collective-permute-start.2
  16.3 1.8 %collective-permute-done.3.refs_0_ = bf16[16,64,128]{2,1,0:T(8,128)(2,1)S(1)} collective-permute-done((bf16[16,64,128]{2,1,0:T(8,128)(2,1)S(1)}, bf16[16,64,128]{2,1,0:T(8,128)(2,1)S(1)}, u32[]{:S(2)}, u32[]{:S(2)}) %collective-permute-start.3) | collective-permute-done | bytes 262176 | tf_op jit(solution)/shard_map/ppermute | solution.py:576
  18.1 0.3 inner_share.1.inner_ref
  18.4 0.0 collective-permute-done.1.below_ref
  18.5 4.1 %collective-permute-done.2.above_ref = bf16[320,128]{1,0:T(8,128)(2,1)S(1)} collective-permute-done((bf16[320,128]{1,0:T(8,128)(2,1)S(1)}, bf16[320,128]{1,0:T(8,128)(2,1)S(1)}, u32[]{:S(2)}, u32[]{:S(2)}) %collective-permute-start.2) | collective-permute-done | bytes 81952 | tf_op jit(solution)/shard_map/ppermute | solution.py:678
  22.6 2.3 %collective-permute-start.4 = (bf16[544,128]{1,0:T(8,128)(2,1)S(1)}, bf16[544,128]{1,0:T(8,128)(2,1)S(1)}, u32[]{:S(2)}, u32[]{:S(2)}) collective-permute-start(bf16[544,128]{1,0:T(8,128)(2,1)S(1)} %merge.1.own_ref), channel_id=1, source_target_pairs={{0,16},{16,0},{1,17},{17,1},{2,18},{18,2},{3,19},{19,3},{4,20},{20... | collective-permute-start | bytes 417800 | tf_op jit(solution)/shard_map/ppermute | solution.py:576
  24.8 0.9 %static_pack.1 = (f32[14,176,128]{2,1,0:T(8,128)S(1)}, bf16[352,128]{1,0:T(8,128)(2,1)S(1)}, bf16[352,128]{1,0:T(8,128)(2,1)S(1)}) custom-call(s32[3]{0:T(128)S(1)} %pad_add_fusion.place_ref, f32[12,128,128]{2,1,0:T(8,128)S(1)} %get-tuple-element.26.maps_ref, f32[128,128]{1,0:T(8,128)S(1)} %copy-done.5, s32[128,128]{1,0:T(8,128)S(1)} %copy-done.6, ...), custom_call_target="tpu_custom_call" | custom-call | bytes 2523148 | tf_op jit(solution)/shard_map/static_pack/pallas_call | solution.py:28
  25.8 2.2 %collective-permute-done.4.other_ref = bf16[544,128]{1,0:T(8,128)(2,1)S(1)} collective-permute-done((bf16[544,128]{1,0:T(8,128)(2,1)S(1)}, bf16[544,128]{1,0:T(8,128)(2,1)S(1)}, u32[]{:S(2)}, u32[]{:S(2)}) %collective-permute-start.4) | collective-permute-done | bytes 139296 | tf_op jit(solution)/shard_map/ppermute | solution.py:576
  28.0 0.7 %pack.1 = (f32[3,176,128]{2,1,0:T(8,128)S(1)}, bf16[352,128]{1,0:T(8,128)(2,1)S(1)}, bf16[352,128]{1,0:T(8,128)(2,1)S(1)}, f32[8,128]{1,0:T(8,128)S(1)}) custom-call(s32[3]{0:T(128)S(1)} %pad_add_fusion.place_ref, bf16[544,128]{1,0:T(8,128)(2,1)S(1)} %merge.1.own_ref, bf16[544,128]{1,0:T(8,128)(2,1)S(1)} %collective-permute-done.4.other_ref, ...), custom_call_target="tpu_custom_call" | custom-call | bytes 1474572 | tf_op jit(solution)/shard_map/pack/pallas_call | solution.py:28
  28.7 2.4 %collective-permute-start.7 = (bf16[16,3,32,128]{3,2,1,0:T(8,128)(2,1)S(1)}, bf16[16,3,32,128]{3,2,1,0:T(8,128)(2,1)S(1)}, u32[]{:S(2)}, u32[]{:S(2)}) collective-permute-start(bf16[16,3,32,128]{3,2,1,0:T(8,128)(2,1)S(1)} %ahead.1), channel_id=1, source_target_pairs={{0,16},{16,0},{1,17},{17,1},{2,18},{18,2},{3,19},{19,3},{4,20},{20... | collective-permute-start | bytes 1179656 | tf_op jit(solution)/shard_map/ppermute | solution.py:576
  31.1 0.0 collective-permute-start.5
  31.1 0.5 collective-permute-start.6
  31.6 1.6 %collective-permute-done.5.from_right_ref = bf16[352,128]{1,0:T(8,128)(2,1)S(1)} collective-permute-done((bf16[352,128]{1,0:T(8,128)(2,1)S(1)}, bf16[352,128]{1,0:T(8,128)(2,1)S(1)}, u32[]{:S(2)}, u32[]{:S(2)}) %collective-permute-start.5) | collective-permute-done | bytes 90144 | tf_op jit(solution)/shard_map/ppermute | solution.py:706
  33.3 2.7 %collective-permute-done.6.from_left_ref = bf16[352,128]{1,0:T(8,128)(2,1)S(1)} collective-permute-done((bf16[352,128]{1,0:T(8,128)(2,1)S(1)}, bf16[352,128]{1,0:T(8,128)(2,1)S(1)}, u32[]{:S(2)}, u32[]{:S(2)}) %collective-permute-start.6) | collective-permute-done | bytes 90144 | tf_op jit(solution)/shard_map/ppermute | solution.py:705
  36.0 4.0 %model.1 = (f32[3,128,128]{2,1,0:T(8,128)}, f32[16,128]{1,0:T(8,128)S(1)}, f32[3,128,128]{2,1,0:T(8,128)S(1)}) custom-call(s32[3]{0:T(128)S(1)} %pad_add_fusion.place_ref, f32[14,176,128]{2,1,0:T(8,128)S(1)} %get-tuple-element.31.tall_ref, f32[3,176,128]{2,1,0:T(8,128)S(1)} %get-tuple-element.36.inc_ref, ...), custom_call_target="tpu_custom_call" | custom-call | bytes 2510860 | tf_op jit(solution)/shard_map/model/pallas_call | solution.py:28
  40.0 0.0 collective-permute-done.7.refs_0_
  40.0 0.4 products.1
  40.4 0.2 collective-permute-start.8
  40.6 9.0 %all_to_all.11 = f32[16,1,128]{2,1,0:T(1,128)S(1)} all-to-all(f32[16,1,128]{2,1,0:T(1,128)S(1)} %bitcast.17), channel_id=1, replica_groups=mesh['ens'=2,'ty'=4,'tx'=4] {'ty','tx'}, dimensions={0} | all-to-all | bytes 16384 | tf_op jit(solution)/shard_map/all_to_all | solution.py:733
  49.6 2.1 %collective-permute-done.8.refs_1_ = bf16[16,96,128]{2,1,0:T(8,128)(2,1)S(1)} collective-permute-done((bf16[16,96,128]{2,1,0:T(8,128)(2,1)S(1)}, bf16[16,96,128]{2,1,0:T(8,128)(2,1)S(1)}, u32[]{:S(2)}, u32[]{:S(2)}) %collective-permute-start.8) | collective-permute-done | bytes 393248 | tf_op jit(solution)/shard_map/ppermute | solution.py:576
  51.7 1.4 %final.1 = (f32[16,128,128]{2,1,0:T(8,128)}, f32[1,1]{1,0:T(1,128)}) custom-call(bf16[16,96,128]{2,1,0:T(8,128)(2,1)S(1)} %get-tuple-element.42.refs_0_, bf16[16,96,128]{2,1,0:T(8,128)(2,1)S(1)} %collective-permute-done.8.refs_1_, bf16[16,32,128]{2,1,0:T(8,128)(2,1)S(1)} %get-tuple-element.43.refs_2_, bf16[16,32,128]{2,1,0:T(8,128)(2,1)S(1)} %get-tuple-element.44.refs_3_, ...), custom_call_target="tpu_custom_call" | custom-call | bytes 3416068 | tf_op jit(solution)/shard_map/final/pallas_call | solution.py:28
  (12 shorter events, 0.1 us)
Async XLA Ops:
  0.6 5.0 %copy-start.2 = (f32[16,128,128]{2,1,0:T(8,128)S(1)}, f32[16,128,128]{2,1,0:T(8,128)}, u32[]{:S(2)}) copy-start(f32[16,128,128]{2,1,0:T(8,128)} %refs_5_.1) | copy-start | bytes 3145732
  2.5 9.8 %collective-permute-start = (bf16[16,64,128]{2,1,0:T(8,128)(2,1)}, bf16[16,64,128]{2,1,0:T(8,128)(2,1)S(1)}, u32[]{:S(2)}, u32[]{:S(2)}) collective-permute-start(bf16[16,64,128]{2,1,0:T(8,128)(2,1)} %send.2), channel_id=1, source_target_pairs={{0,16},{16,0},{1,17},{17,1},{2,18},{18,2},{3,19},{19,3},{4,20},{20... | collective-permute-start | bytes 786440 | tf_op jit(solution)/shard_map/ppermute | solution.py:576
  5.6 1.4 %copy-start = (bf16[16,3,128,128]{3,2,1,0:T(8,128)(2,1)S(1)}, bf16[16,3,128,128]{3,2,1,0:T(8,128)(2,1)}, u32[]{:S(2)}) copy-start(bf16[16,3,128,128]{3,2,1,0:T(8,128)(2,1)} %perturbations_ref.5) | copy-start | bytes 4718596
  7.0 0.7 %copy-start.7 = (s32[32]{0:T(128)S(1)}, s32[32]{0:T(128)}, u32[]{:S(2)}) copy-start(s32[32]{0:T(128)} %offsets_ref.1) | copy-start | bytes 388
  7.7 0.7 %copy-start.8 = (f32[32]{0:T(128)S(1)}, f32[32]{0:T(128)}, u32[]{:S(2)}) copy-start(f32[32]{0:T(128)} %weights_ref.1) | copy-start | bytes 388
  8.3 2.1 %copy-start.9 = (s32[1,1,6,512]{3,1,2,0:T(1,128)S(1)}, s32[1,1,6,512]{3,1,2,0:T(1,128)}, u32[]{:S(2)}) copy-start(s32[1,1,6,512]{3,1,2,0:T(1,128)} %param.19) | copy-start | bytes 36868
  8.3 2.1 %copy-start.10 = (f32[1,1,6,512]{3,1,2,0:T(1,128)S(1)}, f32[1,1,6,512]{3,1,2,0:T(1,128)}, u32[]{:S(2)}) copy-start(f32[1,1,6,512]{3,1,2,0:T(1,128)} %param.21) | copy-start | bytes 36868
  8.3 2.1 %copy-start.11 = (f32[1,1,6,512]{3,1,2,0:T(1,128)S(1)}, f32[1,1,6,512]{3,1,2,0:T(1,128)}, u32[]{:S(2)}) copy-start(f32[1,1,6,512]{3,1,2,0:T(1,128)} %param.20) | copy-start | bytes 36868
  8.3 2.1 %copy-start.3 = (f32[3,128,128]{2,1,0:T(8,128)S(1)}, f32[3,128,128]{2,1,0:T(8,128)}, u32[]{:S(2)}) copy-start(f32[3,128,128]{2,1,0:T(8,128)} %control_ref.7) | copy-start | bytes 589828
  10.2 2.1 %copy-start.1 = (bf16[16,3,128,128]{3,2,1,0:T(8,128)(2,1)S(1)}, bf16[16,3,128,128]{3,2,1,0:T(8,128)(2,1)}, u32[]{:S(2)}) copy-start(bf16[16,3,128,128]{3,2,1,0:T(8,128)(2,1)} %perturbations_ref.5) | copy-start | bytes 4718596
  10.3 7.8 %collective-permute-start.3 = (bf16[16,64,128]{2,1,0:T(8,128)(2,1)S(1)}, bf16[16,64,128]{2,1,0:T(8,128)(2,1)S(1)}, u32[]{:S(2)}, u32[]{:S(2)}) collective-permute-start(bf16[16,64,128]{2,1,0:T(8,128)(2,1)S(1)} %send.3), channel_id=1, source_target_pairs={{0,16},{16,0},{1,17},{17,1},{2,18},{18,2},{3,19},{19,3},{4,20},{20... | collective-permute-start | bytes 786440 | tf_op jit(solution)/shard_map/ppermute | solution.py:576
  10.4 2.2 %copy-start.4 = (f32[3,128,128]{2,1,0:T(8,128)S(1)}, f32[3,128,128]{2,1,0:T(8,128)}, u32[]{:S(2)}) copy-start(f32[3,128,128]{2,1,0:T(8,128)} %std_ref.5) | copy-start | bytes 589828
  10.5 2.2 %copy-start.5 = (f32[128,128]{1,0:T(8,128)S(1)}, f32[128,128]{1,0:T(8,128)}, u32[]{:S(2)}) copy-start(f32[128,128]{1,0:T(8,128)} %courant_ref.3) | copy-start | bytes 196612
  10.5 2.2 %copy-start.6 = (s32[128,128]{1,0:T(8,128)S(1)}, s32[128,128]{1,0:T(8,128)}, u32[]{:S(2)}) copy-start(s32[128,128]{1,0:T(8,128)} %mask_ref.3) | copy-start | bytes 196612
  12.7 5.8 %collective-permute-start.1 = (bf16[320,128]{1,0:T(8,128)(2,1)S(1)}, bf16[320,128]{1,0:T(8,128)(2,1)S(1)}, u32[]{:S(2)}, u32[]{:S(2)}) collective-permute-start(bf16[320,128]{1,0:T(8,128)(2,1)S(1)} %get-tuple-element.29), channel_id=1, source_target_pairs={{4,0},{8,4},{12,8},{0,12},{5,1},{9,5},{13,9},{1,13},{6,2},{10,6},{... | collective-permute-start | bytes 245768 | tf_op jit(solution)/shard_map/ppermute | solution.py:679
  16.3 6.2 %collective-permute-start.2 = (bf16[320,128]{1,0:T(8,128)(2,1)S(1)}, bf16[320,128]{1,0:T(8,128)(2,1)S(1)}, u32[]{:S(2)}, u32[]{:S(2)}) collective-permute-start(bf16[320,128]{1,0:T(8,128)(2,1)S(1)} %get-tuple-element.30), channel_id=1, source_target_pairs={{0,4},{4,8},{8,12},{12,0},{1,5},{5,9},{9,13},{13,1},{2,6},{6,10},{... | collective-permute-start | bytes 245768 | tf_op jit(solution)/shard_map/ppermute | solution.py:678
  22.6 5.4 %collective-permute-start.4 = (bf16[544,128]{1,0:T(8,128)(2,1)S(1)}, bf16[544,128]{1,0:T(8,128)(2,1)S(1)}, u32[]{:S(2)}, u32[]{:S(2)}) collective-permute-start(bf16[544,128]{1,0:T(8,128)(2,1)S(1)} %merge.1.own_ref), channel_id=1, source_target_pairs={{0,16},{16,0},{1,17},{17,1},{2,18},{18,2},{3,19},{19,3},{4,20},{20... | collective-permute-start | bytes 417800 | tf_op jit(solution)/shard_map/ppermute | solution.py:576
  28.7 11.3 %collective-permute-start.7 = (bf16[16,3,32,128]{3,2,1,0:T(8,128)(2,1)S(1)}, bf16[16,3,32,128]{3,2,1,0:T(8,128)(2,1)S(1)}, u32[]{:S(2)}, u32[]{:S(2)}) collective-permute-start(bf16[16,3,32,128]{3,2,1,0:T(8,128)(2,1)S(1)} %ahead.1), channel_id=1, source_target_pairs={{0,16},{16,0},{1,17},{17,1},{2,18},{18,2},{3,19},{19,3},{4,20},{20... | collective-permute-start | bytes 1179656 | tf_op jit(solution)/shard_map/ppermute | solution.py:576
  31.1 2.1 %collective-permute-start.5 = (bf16[352,128]{1,0:T(8,128)(2,1)S(1)}, bf16[352,128]{1,0:T(8,128)(2,1)S(1)}, u32[]{:S(2)}, u32[]{:S(2)}) collective-permute-start(bf16[352,128]{1,0:T(8,128)(2,1)S(1)} %get-tuple-element.37), channel_id=1, source_target_pairs={{1,0},{2,1},{3,2},{0,3},{5,4},{6,5},{7,6},{4,7},{9,8},{10,9},{11,1... | collective-permute-start | bytes 270344 | tf_op jit(solution)/shard_map/ppermute | solution.py:706
  31.1 4.9 %collective-permute-start.6 = (bf16[352,128]{1,0:T(8,128)(2,1)S(1)}, bf16[352,128]{1,0:T(8,128)(2,1)S(1)}, u32[]{:S(2)}, u32[]{:S(2)}) collective-permute-start(bf16[352,128]{1,0:T(8,128)(2,1)S(1)} %get-tuple-element.38), channel_id=1, source_target_pairs={{0,1},{1,2},{2,3},{3,0},{4,5},{5,6},{6,7},{7,4},{8,9},{9,10},{10,1... | collective-permute-start | bytes 270344 | tf_op jit(solution)/shard_map/ppermute | solution.py:705
  40.4 11.2 %collective-permute-start.8 = (bf16[16,96,128]{2,1,0:T(8,128)(2,1)S(1)}, bf16[16,96,128]{2,1,0:T(8,128)(2,1)S(1)}, u32[]{:S(2)}, u32[]{:S(2)}) collective-permute-start(bf16[16,96,128]{2,1,0:T(8,128)(2,1)S(1)} %get-tuple-element.42.refs_0_), channel_id=1, source_target_pairs={{0,16},{16,0},{1,17},{17,1},{2,18},{18,2},{3,19},{19,3},{4,20},{20... | collective-permute-start | bytes 1179656 | tf_op jit(solution)/shard_map/ppermute | solution.py:576

commit v4 on v3

--- a/solution.py
+++ b/solution.py
@@ -226,20 +226,6 @@
         ref[...] = jnp.concatenate(fields, axis=0).astype(BF16)
 
 
-def merge_kernel(steps, halo, outer, inner, outer_ref, inner_ref, below_ref, above_ref, square_ref, out_ref):
-    for units, ref in ((outer, outer_ref), (inner, inner_ref)):
-        height = len(units) * UNIT
-        rows = (len(outer) + len(inner)) * UNIT
-        for c in range(3):
-            for n, y in enumerate(units):
-                at = c * height + n * UNIT
-                out_ref[c * rows + y : c * rows + y + UNIT, :] = ref[at : at + UNIT, :]
-    at = sum(row_sizes(steps, halo)) - 3 * halo
-    beside = [ref[...].astype(F32)[at : at + 3 * halo] for ref in (below_ref, above_ref)]
-    out_ref[3 * rows : 3 * rows + 6 * halo, :] = jnp.concatenate(beside, axis=0).astype(BF16)
-    out_ref[3 * rows + 6 * halo :, :] = square_ref[...]
-
-
 def lane_pack(fields, widths, at=0, left=None, right=None):
     cols = fields[0].shape[1]
     lane = lax.broadcasted_iota(jnp.int32, fields[0].shape, 1)
@@ -267,93 +253,119 @@
     return [maps[0] + [(at + 2 + c, halo) for c in range(3)], maps[1] + [(at, halo), (at + 1, halo)]]
 
 
-def tall_rows(place_ref, tile, lower, upper, halo, out_ref):
-    rows, cols = tile.shape
-    size = lower.shape[0]
-    parts = [jnp.where(place_ref[1] == 1, 0.0, lower), jnp.where(place_ref[0] == 1, 0.0, upper)]
-    if size < halo:
-        parts.insert(1, jnp.zeros((2 * (halo - size), cols), F32))
-    out_ref[:rows, :] = tile
-    out_ref[rows:, :] = jnp.concatenate(parts, axis=0)
-
-
-def static_pack_kernel(
-    steps, halo, place_ref, maps_ref, courant_ref, mask_ref, below_ref, above_ref, tall_ref, left_ref, right_ref
+def packed_blocks(steps, halo, field, left_ref, right_ref, first, place):
+    for n, block in enumerate(lane_blocks(steps, halo)):
+        left, right = lane_pack([field(k) for k, _ in block], [w for _, w in block])
+        at = slice(n * first + place, n * first + place + left.shape[0])
+        left_ref[at, :] = left.astype(BF16)
+        right_ref[at, :] = right.astype(BF16)
+
+
+def static_tile(steps, maps_ref, courant_ref, mask_ref, std_ref, control_ref):
+    def field(k):
+        if k < 2 * steps:
+            return maps_ref[k]
+        if k == 2 * steps:
+            return courant_ref[...]
+        if k == 2 * steps + 1:
+            return mask_ref[...].astype(F32)
+        return std_ref[k - 2 * steps - 2] * control_ref[k - 2 * steps - 2]
+
+    return field
+
+
+def tile_pack_kernel(steps, halo, maps_ref, courant_ref, mask_ref, std_ref, control_ref, left_ref, right_ref):
+    field = static_tile(steps, maps_ref, courant_ref, mask_ref, std_ref, control_ref)
+    packed_blocks(steps, halo, field, left_ref, right_ref, courant_ref.shape[0], 0)
+
+
+def beside_rows(steps, halo, place_ref, below_ref, above_ref):
+    sizes = row_sizes(steps, halo)
+    cols = below_ref.shape[1]
+    below = jnp.where(place_ref[1] == 1, 0.0, below_ref[...].astype(F32))
+    above = jnp.where(place_ref[0] == 1, 0.0, above_ref[...].astype(F32))
+
+    def field(k):
+        at, size = sum(sizes[:k]), sizes[k]
+        parts = [below[at : at + size], above[at : at + size]]
+        if size < halo:
+            parts.insert(1, jnp.zeros((2 * (halo - size), cols), F32))
+        return jnp.concatenate(parts, axis=0)
+
+    return field
+
+
+def merge_kernel(
+    steps,
+    halo,
+    outer,
+    inner,
+    place_ref,
+    outer_ref,
+    inner_ref,
+    below_ref,
+    above_ref,
+    square_ref,
+    tile_left_ref,
+    tile_right_ref,
+    out_ref,
+    left_ref,
+    right_ref,
+    part_left_ref,
+    part_right_ref,
 ):
-    sizes = row_sizes(steps, halo)
-    fields = 2 * steps + 2
-    below, above = below_ref[...].astype(F32), above_ref[...].astype(F32)
-    at = 0
-    for k in range(fields):
-        tile = maps_ref[k] if k < 2 * steps else courant_ref[...] if k == 2 * steps else mask_ref[...].astype(F32)
-        end = at + sizes[k]
-        tall_rows(place_ref, tile, below[at:end], above[at:end], halo, tall_ref.at[k])
-        at = end
-    high = tall_ref.shape[1]
+    rows = (len(outer) + len(inner)) * UNIT
+    high = rows + 2 * halo
+    for units, ref in ((outer, outer_ref), (inner, inner_ref)):
+        height = len(units) * UNIT
+        for c in range(3):
+            for n, y in enumerate(units):
+                at = c * height + n * UNIT
+                out_ref[c * rows + y : c * rows + y + UNIT, :] = ref[at : at + UNIT, :]
+    field = beside_rows(steps, halo, place_ref, below_ref, above_ref)
+    beside = [field(2 * steps + 5 + c) for c in range(3)]
+    out_ref[3 * rows : 3 * rows + 6 * halo, :] = jnp.concatenate(beside, axis=0).astype(BF16)
+    out_ref[3 * rows + 6 * halo :, :] = square_ref[...]
+    for ref, tile_ref in ((left_ref, tile_left_ref), (right_ref, tile_right_ref)):
+        for n in (0, 1):
+            ref[n * high : n * high + rows, :] = tile_ref[n * rows : (n + 1) * rows, :]
     for n, block in enumerate(lane_blocks(steps, halo)):
-        kept = [(k, w) for k, w in block if k < fields]
-        left, right = lane_pack([tall_ref[k] for k, _ in kept], [w for _, w in kept])
-        left_ref[n * high : (n + 1) * high, :] = left.astype(BF16)
-        right_ref[n * high : (n + 1) * high, :] = right.astype(BF16)
-
-
-def pack_kernel(
+        left, right = lane_pack([field(k) for k, _ in block], [w for _, w in block])
+        left_ref[n * high + rows : (n + 1) * high, :] = left.astype(BF16)
+        right_ref[n * high + rows : (n + 1) * high, :] = right.astype(BF16)
+    shares_tall = [
+        jnp.concatenate([out_ref[c * rows : (c + 1) * rows, :].astype(F32), beside[c]], axis=0) for c in range(3)
+    ]
+    left, right = lane_pack(shares_tall, [halo] * 3)
+    part_left_ref[...] = left.astype(BF16)
+    part_right_ref[...] = right.astype(BF16)
+
+
+def tall_kernel(
+    steps, halo, place_ref, maps_ref, courant_ref, mask_ref, std_ref, control_ref, below_ref, above_ref, tall_ref
+):
+    rows = courant_ref.shape[0]
+    tile = static_tile(steps, maps_ref, courant_ref, mask_ref, std_ref, control_ref)
+    beside = beside_rows(steps, halo, place_ref, below_ref, above_ref)
+    for k in range(2 * steps + 5):
+        tall_ref[k, :rows, :] = tile(k)
+        tall_ref[k, rows:, :] = beside(k)
+
+
+def model_kernel(
     steps,
     halo,
     scale,
     place_ref,
+    tall_ref,
     own_ref,
     other_ref,
-    std_ref,
-    control_ref,
-    early_ref,
-    below_ref,
-    above_ref,
-    static_left_ref,
-    static_right_ref,
-    inc_ref,
-    left_ref,
-    right_ref,
-    cost_ref,
-):
-    _, rows, cols = control_ref.shape
-    at = slice(3 * rows, 3 * rows + 6 * halo)
-    beside = scale * (own_ref[at, :].astype(F32) + other_ref[at, :].astype(F32))
-    at = 3 * rows + 6 * halo
-    squares = own_ref[at : at + SUB, :].astype(F32) + other_ref[at : at + SUB, :].astype(F32)
-    cost_ref[...] = early_ref[...] + squares[:8]
-    below, above = below_ref[...].astype(F32), above_ref[...].astype(F32)
-    first = sum(row_sizes(steps, halo)[: 2 * steps + 2])
-    for c in range(3):
-        at = slice(c * rows, (c + 1) * rows)
-        total = own_ref[at, :].astype(F32) + other_ref[at, :].astype(F32)
-        at = slice(first + c * halo, first + (c + 1) * halo)
-        lower = below[at] + beside[c * halo : (c + 1) * halo]
-        upper = above[at] + beside[(3 + c) * halo : (4 + c) * halo]
-        tall_rows(place_ref, std_ref[c] * control_ref[c] + scale * total, lower, upper, halo, inc_ref.at[c])
-    high = rows + 2 * halo
-    taken = sum(2 * (t + 1) for t in range(steps))
-    left, right = lane_pack(
-        [inc_ref[c] for c in range(3)],
-        [halo] * 3,
-        taken,
-        static_left_ref[:high, :].astype(F32),
-        static_right_ref[:high, :].astype(F32),
-    )
-    left_ref[:high, :] = left.astype(BF16)
-    right_ref[:high, :] = right.astype(BF16)
-    left_ref[high:, :] = static_left_ref[high:, :]
-    right_ref[high:, :] = static_right_ref[high:, :]
-
-
-def model_kernel(
-    steps,
-    halo,
-    place_ref,
-    tall_ref,
-    inc_ref,
     from_right_ref,
     from_left_ref,
+    part_right_ref,
+    part_left_ref,
+    far_right_ref,
+    far_left_ref,
     early_ref,
     std_ref,
     control_ref,
@@ -363,6 +375,7 @@
     source_ref,
     cost_ref,
     cost_sem,
+    inc_ref,
     sides_ref,
     courant_ref,
     half_wet_ref,
@@ -404,12 +417,28 @@
             up = jnp.where(last, self.up.get(k + 1, self.up[k]), self.up[k])
             return up - jnp.where(top, self.down.get(k - 1, self.down[k]), self.down[k])
 
+    part_right = part_right_ref[...].astype(F32) + far_right_ref[...].astype(F32)
+    part_left = part_left_ref[...].astype(F32) + far_left_ref[...].astype(F32)
+    for c in range(3):
+        here = slice(c * rows, (c + 1) * rows)
+        total = own_ref[here, :].astype(F32) + other_ref[here, :].astype(F32)
+        inc_ref[c, :rows, :] = tall_ref[fields + c, :rows, :] + scale * total
+    here = slice(3 * rows, 3 * rows + 6 * halo)
+    total = own_ref[here, :].astype(F32) + other_ref[here, :].astype(F32)
+    for c in range(3):
+        beside = total[2 * c * halo : 2 * (c + 1) * halo]
+        inc_ref[c, rows:, :] = tall_ref[fields + c, rows:, :] + scale * beside
+    here = slice(3 * rows + 6 * halo, 3 * rows + 6 * halo + SUB)
+    squares = own_ref[here, :].astype(F32) + other_ref[here, :].astype(F32)
     for n, block in enumerate(lane_blocks(steps, halo)):
         place = 0
         from_right = from_right_ref[n * height_ext : (n + 1) * height_ext, :].astype(F32)
         from_left = from_left_ref[n * height_ext : (n + 1) * height_ext, :].astype(F32)
         for k, size in block:
-            sides_ref[k] = lane_unpack(from_right, from_left, place, size)
+            side = lane_unpack(from_right, from_left, place, size)
+            if k >= fields:
+                side = side + scale * lane_unpack(part_right, part_left, (k - fields) * halo, halo)
+            sides_ref[k] = side
             place += size
 
     def joined(k, rows_at):
@@ -425,7 +454,7 @@
         states[0][1][at(k), :] = wet * joined(fields + 1, at(k))
         states[0][2][at(k), :] = wet * joined(fields + 2, at(k))
 
-    total = early_ref[...]
+    total = early_ref[...] + squares[:8]
     for t in range(steps):
         out = halo - 2 * (t + 1)
         src, dst = states[t % 2], states[1 - t % 2]
@@ -524,6 +553,7 @@
         pltpu.VMEM((steps, high, 2 * cols), F32),
         pltpu.VMEM((terms, cols), F32),
         pltpu.SemaphoreType.DMA,
+        pltpu.VMEM((3, high, cols), F32),
         pltpu.VMEM((2 * steps + 5, high, cols), F32),
     ] + [pltpu.VMEM((high, 2 * cols), F32)] * 9
 
@@ -534,7 +564,7 @@
 
 
 def products_kernel(units, ahead, lam_ref, perturbations_ref, *refs):
-    count = (len(refs) - 2) // 2
+    count = 0
     others, sent_ref, ahead_refs = refs[:count], refs[count], refs[count + 1 :]
 
     def products(ref, i, at, rows):
@@ -555,8 +585,8 @@
 
 
 def final_kernel(groups, scale, cost_scale, units, ahead, *refs):
-    late, early = refs[:groups], refs[groups : 2 * groups]
-    kron_ref, alpha_ref, terms_ref, out_ref, cost_ref = refs[2 * groups :]
+    late, early = refs[:groups], ()
+    kron_ref, alpha_ref, terms_ref, out_ref, cost_ref = refs[groups:]
     members, rows, cols = alpha_ref.shape
     cost_ref[0, 0] = jnp.sum(terms_ref[...]) * cost_scale
     for parts, chunk in ((early, ahead), (late, units)):
@@ -619,7 +649,7 @@
     at_edge = -(-halo // UNIT)
     outer = units[:at_edge] + units[len(units) - at_edge :]
     inner = units[at_edge : len(units) - at_edge]
-    ahead = inner[: len(units) // 4]
+    ahead = []
     behind = [y for y in units if y not in ahead]
 
     def rows_of(chunk, mib, *before):
@@ -679,44 +709,59 @@
     below = lax.ppermute(top, "ty", up)
 
     inner_share = share_of(inner, inner_others, "inner_share")
-    (share,) = call(
+    high = rows + 2 * halo
+    static = [maps, courant, land_mask, static_std, control]
+    tile_left, tile_right = call(
+        functools.partial(tile_pack_kernel, steps, halo),
+        [((2 * rows, cols), BF16)] * 2,
+        static,
+        name="tile_pack",
+    )
+    share, to_left, to_right, part_left, part_right = call(
         functools.partial(merge_kernel, steps, halo, outer, inner),
-        [((3 * rows + 6 * halo + SUB, cols), BF16)],
-        [outer_share, inner_share, below, above, square],
+        [((3 * rows + 6 * halo + SUB, cols), BF16)] + [((2 * high, cols), BF16)] * 2 + [((high, cols), BF16)] * 2,
+        [place, outer_share, inner_share, below, above, square, tile_left, tile_right],
+        smem=1,
         name="merge",
     )
     share, share_other = sum_parts(share, groups)
-    high = rows + 2 * halo
-    packed = [((2 * high, cols), BF16)] * 2
-    tall, static_left, static_right = call(
-        functools.partial(static_pack_kernel, steps, halo),
-        [((2 * steps + 2, high, cols), F32)] + packed,
-        [place, maps, courant, land_mask, below, above],
+
+    def across(to, part, perm):
+        if groups != 2:
+            part = lax.psum(part.astype(F32), "ens")
+            return lax.ppermute(to, "tx", perm), lax.ppermute(part, "tx", perm), jnp.zeros_like(part)
+        got = lax.ppermute(jnp.concatenate([to, part], axis=0), "tx", perm)
+        far = [(e * n_tx + i, (1 - e) * n_tx + j) for e in (0, 1) for i, j in perm]
+        return got[: 2 * high], got[2 * high :], lax.ppermute(part, ("ens", "tx"), far)
+
+    from_left, near_left, far_left = across(to_right, part_right, right)
+    from_right, near_right, far_right = across(to_left, part_left, left)
+    (tall,) = call(
+        functools.partial(tall_kernel, steps, halo),
+        [((2 * steps + 5, high, cols), F32)],
+        [place, *static, below, above],
         smem=1,
-        name="static_pack",
-    )
-    inc, to_left, to_right, early = call(
-        functools.partial(pack_kernel, steps, halo, scale),
-        [((3, high, cols), F32)] + packed + [((8, cols), F32)],
-        [place, share, share_other, static_std, control, early, below, above, static_left, static_right],
-        smem=1,
-        name="pack",
-    )
-    from_left = lax.ppermute(to_right, "tx", right)
-    from_right = lax.ppermute(to_left, "tx", left)
-
-    (rows_ahead,) = call(
-        functools.partial(ahead_kernel, ahead),
-        [((own, 3, len(ahead) * UNIT, cols), BF16)],
-        [perturbations, early],
-        name="ahead",
-    )
-    ahead_others = to_others(rows_ahead, groups)
-
+        name="tall",
+    )
+    ahead_others = []
     control_new, cost_terms, lam = call(
-        functools.partial(model_kernel, steps, halo),
+        functools.partial(model_kernel, steps, halo, scale),
         [((3, rows, cols), F32), ((n_ty * n_tx, cols), F32), ((3, rows, cols), F32)],
-        [place, tall, inc, from_right, from_left, early, static_std, control],
+        [
+            place,
+            tall,
+            share,
+            share_other,
+            from_right,
+            from_left,
+            near_right,
+            near_left,
+            far_right,
+            far_left,
+            early,
+            static_std,
+            control,
+        ],
         scratch=model_scratch(steps, halo, rows, cols, n_ty * n_tx),
         out_specs=[VMEM, HBM, VMEM],
         smem=1,
@@ -725,7 +770,7 @@
     )
     sent, *products_ahead = call(
         functools.partial(products_kernel, behind, ahead),
-        [((own, len(behind) * UNIT, cols), BF16)] + [((own, len(ahead) * UNIT, cols), BF16)] * groups,
+        [((own, len(behind) * UNIT, cols), BF16)],
         [lam, perturbations, *ahead_others],
         name="products",
     )

time: 53.3 us -> 52.1 us (0.977)
  waiting for transfers between devices: 15.2 us -> 12 us
  starting transfers between devices: 12.1 us -> 14.1 us
    ppermute x2 -> x4, starting transfers between devices: 0.51 us -> 3.24 us  [the longest x2 1.75 us: across(): lax.ppermute(part, ('ens', 'tx'), far)]
    ppermute x2 -> x4, waiting for transfers between devices: 4.37 us -> 2.46 us  [the longest x2 2.33 us: across(): lax.ppermute(part, ('ens', 'tx'), far)]
    ppermute x5 -> x4, waiting for transfers between devices: 6.76 us -> 5.47 us  [to_others(): lax.ppermute(x, 'ens', [(i, (i - k) % groups) for i in range(groups)])]
    ppermute x5 -> x4, starting transfers between devices: 8.02 us -> 7.2 us  [to_others(): lax.ppermute(x, 'ens', [(i, (i - k) % groups) for i in range(groups)])]
    pallas_call x14 -> x13, Pallas kernels: 13.1 us -> 13.1 us  [call(): pl.pallas_call(kernel, out_shape=out_shape, grid=grid, in_specs=in_specs...]
  transfers between devices with their start and end apart: 9 -> 10, of which waited for: 7 -> 7; matrix products, arithmetic and copies ran while one was open for 0% -> 0% of each run, Pallas kernels for 16% -> 9%
where the time goes in v4:
time: 52.1 us; the launch traced here: 51.9 us
  starting transfers between devices  14.1 us (27%)
  Pallas kernels  13.1 us (25%)
  waiting for transfers between devices  12 us (23%)
  blocking collectives  8.97 us (17%)
  local copies, waits for them, and re-layouts  2.8 us (5%)
  between operations  0.88 us (2%)
    pallas_call x13, Pallas kernels, call(): pl.pallas_call(kernel, out_shape=out_shape, grid=grid, in_specs=in_specs...  13.1 us
    all_to_all x1, blocking collectives, body(): terms = lax.all_to_all(cost_terms, ('ty', 'tx'), 0, 0, tiled=True)  8.97 us
    ppermute x4, starting transfers between devices, to_others(): lax.ppermute(x, 'ens', [(i, (i - k) % groups) for i in range(groups)])  7.2 us
    ppermute x4, waiting for transfers between devices, to_others(): lax.ppermute(x, 'ens', [(i, (i - k) % groups) for i in range(groups)])  5.47 us
    ppermute x1, waiting for transfers between devices, body(): above = lax.ppermute(bottom, 'ty', down)  4.07 us
    ppermute x1, starting transfers between devices, body(): below = lax.ppermute(top, 'ty', up)  3.62 us
    unnamed x26, local copies, waits for them, and re-layouts  2.77 us
    ppermute x2, waiting for transfers between devices, across(): lax.ppermute(part, ('ens', 'tx'), far)  2.33 us
  transfers between devices with their start and end apart: 10, of which 7 were waited for; matrix products, arithmetic and copies ran while one was open for 0% of the time, Pallas kernels for 9%

profile of v4, /device:TPU:0, one launch (start us, length us, event | category | flops | bytes accessed | tf_op | source)
XLA Modules:
  0.0 51.9 jit_solution(11598261285824106728)
XLA Ops:
  0.6 0.0 copy-start.2
  0.6 1.9 %send.2 = bf16[16,64,128]{2,1,0:T(8,128)(2,1)} custom-call(f32[16,128,128]{2,1,0:T(8,128)} %refs_3_.1), custom_call_target="tpu_custom_call" | custom-call | bytes 1310720 | tf_op jit(solution)/shard_map/send/pallas_call | solution.py:28
  2.5 3.0 %collective-permute-start = (bf16[16,64,128]{2,1,0:T(8,128)(2,1)}, bf16[16,64,128]{2,1,0:T(8,128)(2,1)S(1)}, u32[]{:S(2)}, u32[]{:S(2)}) collective-permute-start(bf16[16,64,128]{2,1,0:T(8,128)(2,1)} %send.2), channel_id=1, source_target_pairs={{0,16},{16,0},{1,17},{17,1},{2,18},{18,2},{3,19},{19,3},{4,20},{20... | collective-permute-start | bytes 786440 | tf_op jit(solution)/shard_map/ppermute | solution.py:606
  5.5 0.1 pad_add_fusion.place_ref
  5.6 0.0 copy-done.2
  5.6 1.4 %copy-done = bf16[16,3,128,128]{3,2,1,0:T(8,128)(2,1)S(1)} copy-done((bf16[16,3,128,128]{3,2,1,0:T(8,128)(2,1)S(1)}, bf16[16,3,128,128]{3,2,1,0:T(8,128)(2,1)}, u32[]{:S(2)}) %copy-start) | copy-done | bytes 1572888
  7.0 0.7 %copy-done.7 = s32[32]{0:T(128)S(1)} copy-done((s32[32]{0:T(128)S(1)}, s32[32]{0:T(128)}, u32[]{:S(2)}) %copy-start.7) | copy-done | bytes 152
  7.7 0.7 %copy-done.8 = f32[32]{0:T(128)S(1)} copy-done((f32[32]{0:T(128)S(1)}, f32[32]{0:T(128)}, u32[]{:S(2)}) %copy-start.8) | copy-done | bytes 152
  8.3 1.9 %own.1 = (bf16[2,256,256]{2,1,0:T(8,128)(2,1)S(1)}, bf16[2,256,256]{2,1,0:T(8,128)(2,1)S(1)}, f32[3,128,128]{2,1,0:T(8,128)S(1)}, bf16[16,128]{1,0:T(8,128)(2,1)S(1)}) custom-call(s32[3]{0:T(128)S(1)} %pad_add_fusion.place_ref, s32[32]{0:T(128)S(1)} %copy-done.7, f32[32]{0:T(128)S(1)} %copy-done.8, f32[16,128,128]{2,1,0:T(8,128)S(1)} %copy-done.2, ...), custom_call_target="tpu_custom_call" | custom-call | bytes 3346700 | tf_op jit(solution)/shard_map/own/pallas_call | solution.py:28
  10.2 0.0 copy-start.1
  10.2 0.1 send.3
  10.3 0.1 collective-permute-start.3
  10.4 0.0 copy-done.9
  10.4 0.0 copy-done.10
  10.4 0.0 copy-done.11
  10.4 0.0 copy-done.3
  10.5 0.0 copy-start.4
  10.5 0.0 copy-start.5
  10.5 0.0 copy-start.6
  10.5 1.2 %maps.1 = (f32[12,128,128]{2,1,0:T(8,128)S(1)}, f32[8,128]{1,0:T(8,128)S(1)}) custom-call(s32[6,512]{1,0:T(8,128)S(1)} %bitcast.16, f32[6,512]{1,0:T(8,128)S(1)} %get-tuple-element.44.values_ref, f32[6,512]{1,0:T(8,128)S(1)} %get-tuple-element.43.weights_ref, f32[3,128,128]{2,1,0:T(8,128)S(1)} %copy-done.3), custom_call_target="tpu_custom_call" | custom-call | flops 402653184 | bytes 1024000 | tf_op jit(solution)/shard_map/maps/pallas_call | solution.py:28
  11.7 0.6 %collective-permute-done.refs_0_ = bf16[16,64,128]{2,1,0:T(8,128)(2,1)S(1)} collective-permute-done((bf16[16,64,128]{2,1,0:T(8,128)(2,1)}, bf16[16,64,128]{2,1,0:T(8,128)(2,1)S(1)}, u32[]{:S(2)}, u32[]{:S(2)}) %collective-permute-start) | collective-permute-done | bytes 262176 | tf_op jit(solution)/shard_map/ppermute | solution.py:606
  12.3 0.0 copy-done.1
  12.3 0.3 outer_share.1.share_ref.outer_ref
  12.7 3.6 %collective-permute-start.1 = (bf16[320,128]{1,0:T(8,128)(2,1)S(1)}, bf16[320,128]{1,0:T(8,128)(2,1)S(1)}, u32[]{:S(2)}, u32[]{:S(2)}) collective-permute-start(bf16[320,128]{1,0:T(8,128)(2,1)S(1)} %get-tuple-element.26), channel_id=1, source_target_pairs={{4,0},{8,4},{12,8},{0,12},{5,1},{9,5},{13,9},{1,13},{6,2},{10,6},{... | collective-permute-start | bytes 245768 | tf_op jit(solution)/shard_map/ppermute | solution.py:709
  16.3 0.0 collective-permute-start.2
  16.3 0.3 tile_pack.1
  16.6 1.5 %collective-permute-done.3.refs_0_ = bf16[16,64,128]{2,1,0:T(8,128)(2,1)S(1)} collective-permute-done((bf16[16,64,128]{2,1,0:T(8,128)(2,1)S(1)}, bf16[16,64,128]{2,1,0:T(8,128)(2,1)S(1)}, u32[]{:S(2)}, u32[]{:S(2)}) %collective-permute-start.3) | collective-permute-done | bytes 262176 | tf_op jit(solution)/shard_map/ppermute | solution.py:606
  18.1 0.3 inner_share.1.inner_ref
  18.5 0.0 collective-permute-done.1.below_ref
  18.5 4.1 %collective-permute-done.2.above_ref = bf16[320,128]{1,0:T(8,128)(2,1)S(1)} collective-permute-done((bf16[320,128]{1,0:T(8,128)(2,1)S(1)}, bf16[320,128]{1,0:T(8,128)(2,1)S(1)}, u32[]{:S(2)}, u32[]{:S(2)}) %collective-permute-start.2) | collective-permute-done | bytes 81952 | tf_op jit(solution)/shard_map/ppermute | solution.py:708
  22.5 0.7 %merge.1 = (bf16[544,128]{1,0:T(8,128)(2,1)S(1)}, bf16[352,128]{1,0:T(8,128)(2,1)S(1)}, bf16[352,128]{1,0:T(8,128)(2,1)S(1)}, bf16[176,128]{1,0:T(8,128)(2,1)S(1)}, bf16[176,128]{1,0:T(8,128)(2,1)S(1)}) custom-call(s32[3]{0:T(128)S(1)} %pad_add_fusion.place_ref, bf16[192,128]{1,0:T(8,128)(2,1)S(1)} %outer_share.1.share_ref.outer_ref, ...), custom_call_target="tpu_custom_call" | custom-call | bytes 806924 | tf_op jit(solution)/shard_map/merge/pallas_call | solution.py:28
  23.3 0.1 collective-permute-start.6
  23.4 2.3 %collective-permute-start.4 = (bf16[544,128]{1,0:T(8,128)(2,1)S(1)}, bf16[544,128]{1,0:T(8,128)(2,1)S(1)}, u32[]{:S(2)}, u32[]{:S(2)}) collective-permute-start(bf16[544,128]{1,0:T(8,128)(2,1)S(1)} %get-tuple-element.31.own_ref), channel_id=1, source_target_pairs={{0,16},{16,0},{1,17},{17,1},{2,18},{18,2},{3,19},{19,3},{4,20},{20... | collective-permute-start | bytes 417800 | tf_op jit(solution)/shard_map/ppermute | solution.py:606
  25.6 1.4 %collective-permute-start.5 = (bf16[528,128]{1,0:T(8,128)(2,1)S(1)}, bf16[528,128]{1,0:T(8,128)(2,1)S(1)}, u32[]{:S(2)}, u32[]{:S(2)}) collective-permute-start(bf16[528,128]{1,0:T(8,128)(2,1)S(1)} %pad_maximum_fusion), channel_id=1, source_target_pairs={{1,0},{2,1},{3,2},{0,3},{5,4},{6,5},{7,6},{4,7},{9,8},{10,9},{11,1... | collective-permute-start | bytes 405512 | tf_op jit(solution)/shard_map/ppermute | solution.py:733
  27.1 0.0 collective-permute-start.7
  27.1 1.7 %collective-permute-start.8 = (bf16[176,128]{1,0:T(8,128)(2,1)S(1)}, bf16[176,128]{1,0:T(8,128)(2,1)S(1)}, u32[]{:S(2)}, u32[]{:S(2)}) collective-permute-start(bf16[176,128]{1,0:T(8,128)(2,1)S(1)} %get-tuple-element.35), channel_id=1, source_target_pairs={{0,17},{1,18},{2,19},{3,16},{16,1},{17,2},{18,3},{19,0},{4,21},{5,... | collective-permute-start | bytes 135176 | tf_op jit(solution)/shard_map/ppermute | solution.py:735
  28.8 0.6 %tall.1.tall_ref = f32[17,176,128]{2,1,0:T(8,128)S(1)} custom-call(s32[3]{0:T(128)S(1)} %pad_add_fusion.place_ref, f32[12,128,128]{2,1,0:T(8,128)S(1)} %get-tuple-element.23.maps_ref, f32[128,128]{1,0:T(8,128)S(1)} %copy-done.5, s32[128,128]{1,0:T(8,128)S(1)} %copy-done.6, f32[3,128,128]{2,1,0:T(8,128)S(1)} %copy-done.4, f32[3,128,128]{2,1,0:T(8,128)S(1)} %copy-done.3, ...), custom_call_target="tpu_custom_call" | custom-call | bytes 3006476 | tf_op jit(solution)/shard_map/tall/pallas_call | solution.py:28
  29.5 0.0 collective-permute-done.6
  29.5 0.1 collective-permute-done.5
  29.7 1.0 %collective-permute-done.7.far_right_ref = bf16[176,128]{1,0:T(8,128)(2,1)S(1)} collective-permute-done((bf16[176,128]{1,0:T(8,128)(2,1)S(1)}, bf16[176,128]{1,0:T(8,128)(2,1)S(1)}, u32[]{:S(2)}, u32[]{:S(2)}) %collective-permute-start.7) | collective-permute-done | bytes 45088 | tf_op jit(solution)/shard_map/ppermute | solution.py:735
  30.6 1.3 %collective-permute-done.8.far_left_ref = bf16[176,128]{1,0:T(8,128)(2,1)S(1)} collective-permute-done((bf16[176,128]{1,0:T(8,128)(2,1)S(1)}, bf16[176,128]{1,0:T(8,128)(2,1)S(1)}, u32[]{:S(2)}, u32[]{:S(2)}) %collective-permute-start.8) | collective-permute-done | bytes 45088 | tf_op jit(solution)/shard_map/ppermute | solution.py:735
  32.0 0.0 collective-permute-done.4.other_ref
  32.0 4.1 %model.1 = (f32[3,128,128]{2,1,0:T(8,128)}, f32[16,128]{1,0:T(8,128)S(1)}, f32[3,128,128]{2,1,0:T(8,128)S(1)}) custom-call(s32[3]{0:T(128)S(1)} %pad_add_fusion.place_ref, f32[17,176,128]{2,1,0:T(8,128)S(1)} %tall.1.tall_ref, bf16[544,128]{1,0:T(8,128)(2,1)S(1)} %get-tuple-element.31.own_ref, bf16[544,128]{1,0:T(8,128)(2,1)S(1)} %collective-permute-done.4.other_ref, ...), custom_call_target="tpu_custom_call" | custom-call | bytes 2969612 | tf_op jit(solution)/shard_map/model/pallas_call | solution.py:28
  36.1 0.3 products.1.refs_0_
  36.4 1.8 %collective-permute-start.9 = (bf16[16,128,128]{2,1,0:T(8,128)(2,1)S(1)}, bf16[16,128,128]{2,1,0:T(8,128)(2,1)S(1)}, u32[]{:S(2)}, u32[]{:S(2)}) collective-permute-start(bf16[16,128,128]{2,1,0:T(8,128)(2,1)S(1)} %products.1.refs_0_), channel_id=1, source_target_pairs={{0,16},{16,0},{1,17},{17,1},{2,18},{18,2},{3,19},{19,3},{4,20},{20... | collective-permute-start | bytes 1572872 | tf_op jit(solution)/shard_map/ppermute | solution.py:606
  38.2 9.0 %all_to_all.11 = f32[16,1,128]{2,1,0:T(1,128)S(1)} all-to-all(f32[16,1,128]{2,1,0:T(1,128)S(1)} %bitcast.17), channel_id=1, replica_groups=mesh['ens'=2,'ty'=4,'tx'=4] {'ty','tx'}, dimensions={0} | all-to-all | bytes 16384 | tf_op jit(solution)/shard_map/all_to_all | solution.py:778
  47.2 3.3 %collective-permute-done.9.refs_1_ = bf16[16,128,128]{2,1,0:T(8,128)(2,1)S(1)} collective-permute-done((bf16[16,128,128]{2,1,0:T(8,128)(2,1)S(1)}, bf16[16,128,128]{2,1,0:T(8,128)(2,1)S(1)}, u32[]{:S(2)}, u32[]{:S(2)}) %collective-permute-start.9) | collective-permute-done | bytes 524320 | tf_op jit(solution)/shard_map/ppermute | solution.py:606
  50.5 1.4 %final.1 = (f32[16,128,128]{2,1,0:T(8,128)}, f32[1,1]{1,0:T(1,128)}) custom-call(bf16[16,128,128]{2,1,0:T(8,128)(2,1)S(1)} %products.1.refs_0_, bf16[16,128,128]{2,1,0:T(8,128)(2,1)S(1)} %collective-permute-done.9.refs_1_, bf16[2,256,256]{2,1,0:T(8,128)(2,1)S(1)} %get-tuple-element.39.refs_2_, f32[16,128,128]{2,1,0:T(8,128)S(1)} %copy-done.2, ...), custom_call_target="tpu_custom_call" | custom-call | bytes 3416068 | tf_op jit(solution)/shard_map/final/pallas_call | solution.py:28
  (19 shorter events, 0.1 us)
Async XLA Ops:
  0.6 5.0 %copy-start.2 = (f32[16,128,128]{2,1,0:T(8,128)S(1)}, f32[16,128,128]{2,1,0:T(8,128)}, u32[]{:S(2)}) copy-start(f32[16,128,128]{2,1,0:T(8,128)} %refs_3_.1) | copy-start | bytes 3145732
  2.5 9.8 %collective-permute-start = (bf16[16,64,128]{2,1,0:T(8,128)(2,1)}, bf16[16,64,128]{2,1,0:T(8,128)(2,1)S(1)}, u32[]{:S(2)}, u32[]{:S(2)}) collective-permute-start(bf16[16,64,128]{2,1,0:T(8,128)(2,1)} %send.2), channel_id=1, source_target_pairs={{0,16},{16,0},{1,17},{17,1},{2,18},{18,2},{3,19},{19,3},{4,20},{20... | collective-permute-start | bytes 786440 | tf_op jit(solution)/shard_map/ppermute | solution.py:606
  5.6 1.4 %copy-start = (bf16[16,3,128,128]{3,2,1,0:T(8,128)(2,1)S(1)}, bf16[16,3,128,128]{3,2,1,0:T(8,128)(2,1)}, u32[]{:S(2)}) copy-start(bf16[16,3,128,128]{3,2,1,0:T(8,128)(2,1)} %perturbations_ref.3) | copy-start | bytes 4718596
  7.0 0.7 %copy-start.7 = (s32[32]{0:T(128)S(1)}, s32[32]{0:T(128)}, u32[]{:S(2)}) copy-start(s32[32]{0:T(128)} %offsets_ref.1) | copy-start | bytes 388
  7.7 0.7 %copy-start.8 = (f32[32]{0:T(128)S(1)}, f32[32]{0:T(128)}, u32[]{:S(2)}) copy-start(f32[32]{0:T(128)} %weights_ref.1) | copy-start | bytes 388
  8.3 2.1 %copy-start.9 = (s32[1,1,6,512]{3,1,2,0:T(1,128)S(1)}, s32[1,1,6,512]{3,1,2,0:T(1,128)}, u32[]{:S(2)}) copy-start(s32[1,1,6,512]{3,1,2,0:T(1,128)} %param.19) | copy-start | bytes 36868
  8.3 2.1 %copy-start.10 = (f32[1,1,6,512]{3,1,2,0:T(1,128)S(1)}, f32[1,1,6,512]{3,1,2,0:T(1,128)}, u32[]{:S(2)}) copy-start(f32[1,1,6,512]{3,1,2,0:T(1,128)} %param.21) | copy-start | bytes 36868
  8.3 2.1 %copy-start.11 = (f32[1,1,6,512]{3,1,2,0:T(1,128)S(1)}, f32[1,1,6,512]{3,1,2,0:T(1,128)}, u32[]{:S(2)}) copy-start(f32[1,1,6,512]{3,1,2,0:T(1,128)} %param.20) | copy-start | bytes 36868
  8.3 2.1 %copy-start.3 = (f32[3,128,128]{2,1,0:T(8,128)S(1)}, f32[3,128,128]{2,1,0:T(8,128)}, u32[]{:S(2)}) copy-start(f32[3,128,128]{2,1,0:T(8,128)} %control_ref.9) | copy-start | bytes 589828
  10.2 2.1 %copy-start.1 = (bf16[16,3,128,128]{3,2,1,0:T(8,128)(2,1)S(1)}, bf16[16,3,128,128]{3,2,1,0:T(8,128)(2,1)}, u32[]{:S(2)}) copy-start(bf16[16,3,128,128]{3,2,1,0:T(8,128)(2,1)} %perturbations_ref.3) | copy-start | bytes 4718596
  10.3 7.8 %collective-permute-start.3 = (bf16[16,64,128]{2,1,0:T(8,128)(2,1)S(1)}, bf16[16,64,128]{2,1,0:T(8,128)(2,1)S(1)}, u32[]{:S(2)}, u32[]{:S(2)}) collective-permute-start(bf16[16,64,128]{2,1,0:T(8,128)(2,1)S(1)} %send.3), channel_id=1, source_target_pairs={{0,16},{16,0},{1,17},{17,1},{2,18},{18,2},{3,19},{19,3},{4,20},{20... | collective-permute-start | bytes 786440 | tf_op jit(solution)/shard_map/ppermute | solution.py:606
  10.5 2.2 %copy-start.4 = (f32[3,128,128]{2,1,0:T(8,128)S(1)}, f32[3,128,128]{2,1,0:T(8,128)}, u32[]{:S(2)}) copy-start(f32[3,128,128]{2,1,0:T(8,128)} %std_ref.7) | copy-start | bytes 589828
  10.5 2.2 %copy-start.5 = (f32[128,128]{1,0:T(8,128)S(1)}, f32[128,128]{1,0:T(8,128)}, u32[]{:S(2)}) copy-start(f32[128,128]{1,0:T(8,128)} %courant_ref.5) | copy-start | bytes 196612
  10.5 2.2 %copy-start.6 = (s32[128,128]{1,0:T(8,128)S(1)}, s32[128,128]{1,0:T(8,128)}, u32[]{:S(2)}) copy-start(s32[128,128]{1,0:T(8,128)} %mask_ref.5) | copy-start | bytes 196612
  12.7 5.8 %collective-permute-start.1 = (bf16[320,128]{1,0:T(8,128)(2,1)S(1)}, bf16[320,128]{1,0:T(8,128)(2,1)S(1)}, u32[]{:S(2)}, u32[]{:S(2)}) collective-permute-start(bf16[320,128]{1,0:T(8,128)(2,1)S(1)} %get-tuple-element.26), channel_id=1, source_target_pairs={{4,0},{8,4},{12,8},{0,12},{5,1},{9,5},{13,9},{1,13},{6,2},{10,6},{... | collective-permute-start | bytes 245768 | tf_op jit(solution)/shard_map/ppermute | solution.py:709
  16.3 6.2 %collective-permute-start.2 = (bf16[320,128]{1,0:T(8,128)(2,1)S(1)}, bf16[320,128]{1,0:T(8,128)(2,1)S(1)}, u32[]{:S(2)}, u32[]{:S(2)}) collective-permute-start(bf16[320,128]{1,0:T(8,128)(2,1)S(1)} %get-tuple-element.27), channel_id=1, source_target_pairs={{0,4},{4,8},{8,12},{12,0},{1,5},{5,9},{9,13},{13,1},{2,6},{6,10},{... | collective-permute-start | bytes 245768 | tf_op jit(solution)/shard_map/ppermute | solution.py:708
  23.3 6.2 %collective-permute-start.6 = (bf16[528,128]{1,0:T(8,128)(2,1)S(1)}, bf16[528,128]{1,0:T(8,128)(2,1)S(1)}, u32[]{:S(2)}, u32[]{:S(2)}) collective-permute-start(bf16[528,128]{1,0:T(8,128)(2,1)S(1)} %pad_maximum_fusion.1), channel_id=1, source_target_pairs={{0,1},{1,2},{2,3},{3,0},{4,5},{5,6},{6,7},{7,4},{8,9},{9,10},{10,1... | collective-permute-start | bytes 405512 | tf_op jit(solution)/shard_map/ppermute | solution.py:733
  23.4 8.6 %collective-permute-start.4 = (bf16[544,128]{1,0:T(8,128)(2,1)S(1)}, bf16[544,128]{1,0:T(8,128)(2,1)S(1)}, u32[]{:S(2)}, u32[]{:S(2)}) collective-permute-start(bf16[544,128]{1,0:T(8,128)(2,1)S(1)} %get-tuple-element.31.own_ref), channel_id=1, source_target_pairs={{0,16},{16,0},{1,17},{17,1},{2,18},{18,2},{3,19},{19,3},{4,20},{20... | collective-permute-start | bytes 417800 | tf_op jit(solution)/shard_map/ppermute | solution.py:606
  25.6 4.0 %collective-permute-start.5 = (bf16[528,128]{1,0:T(8,128)(2,1)S(1)}, bf16[528,128]{1,0:T(8,128)(2,1)S(1)}, u32[]{:S(2)}, u32[]{:S(2)}) collective-permute-start(bf16[528,128]{1,0:T(8,128)(2,1)S(1)} %pad_maximum_fusion), channel_id=1, source_target_pairs={{1,0},{2,1},{3,2},{0,3},{5,4},{6,5},{7,6},{4,7},{9,8},{10,9},{11,1... | collective-permute-start | bytes 405512 | tf_op jit(solution)/shard_map/ppermute | solution.py:733
  27.1 3.6 %collective-permute-start.7 = (bf16[176,128]{1,0:T(8,128)(2,1)S(1)}, bf16[176,128]{1,0:T(8,128)(2,1)S(1)}, u32[]{:S(2)}, u32[]{:S(2)}) collective-permute-start(bf16[176,128]{1,0:T(8,128)(2,1)S(1)} %get-tuple-element.33), channel_id=1, source_target_pairs={{1,16},{2,17},{3,18},{0,19},{17,0},{18,1},{19,2},{16,3},{5,20},{6,... | collective-permute-start | bytes 135176 | tf_op jit(solution)/shard_map/ppermute | solution.py:735
  27.1 4.9 %collective-permute-start.8 = (bf16[176,128]{1,0:T(8,128)(2,1)S(1)}, bf16[176,128]{1,0:T(8,128)(2,1)S(1)}, u32[]{:S(2)}, u32[]{:S(2)}) collective-permute-start(bf16[176,128]{1,0:T(8,128)(2,1)S(1)} %get-tuple-element.35), channel_id=1, source_target_pairs={{0,17},{1,18},{2,19},{3,16},{16,1},{17,2},{18,3},{19,0},{4,21},{5,... | collective-permute-start | bytes 135176 | tf_op jit(solution)/shard_map/ppermute | solution.py:735
  36.4 14.1 %collective-permute-start.9 = (bf16[16,128,128]{2,1,0:T(8,128)(2,1)S(1)}, bf16[16,128,128]{2,1,0:T(8,128)(2,1)S(1)}, u32[]{:S(2)}, u32[]{:S(2)}) collective-permute-start(bf16[16,128,128]{2,1,0:T(8,128)(2,1)S(1)} %products.1.refs_0_), channel_id=1, source_target_pairs={{0,16},{16,0},{1,17},{17,1},{2,18},{18,2},{3,19},{19,3},{4,20},{20... | collective-permute-start | bytes 1572872 | tf_op jit(solution)/shard_map/ppermute | solution.py:606

commit v5 on v4

--- a/solution.py
+++ b/solution.py
@@ -337,8 +337,9 @@
         jnp.concatenate([out_ref[c * rows : (c + 1) * rows, :].astype(F32), beside[c]], axis=0) for c in range(3)
     ]
     left, right = lane_pack(shares_tall, [halo] * 3)
-    part_left_ref[...] = left.astype(BF16)
-    part_right_ref[...] = right.astype(BF16)
+    for ref, part_ref, part in ((left_ref, part_left_ref, left), (right_ref, part_right_ref, right)):
+        part_ref[...] = part.astype(BF16)
+        ref[2 * high :, :] = part.astype(BF16)
 
 
 def tall_kernel(
@@ -362,8 +363,6 @@
     other_ref,
     from_right_ref,
     from_left_ref,
-    part_right_ref,
-    part_left_ref,
     far_right_ref,
     far_left_ref,
     early_ref,
@@ -417,8 +416,8 @@
             up = jnp.where(last, self.up.get(k + 1, self.up[k]), self.up[k])
             return up - jnp.where(top, self.down.get(k - 1, self.down[k]), self.down[k])
 
-    part_right = part_right_ref[...].astype(F32) + far_right_ref[...].astype(F32)
-    part_left = part_left_ref[...].astype(F32) + far_left_ref[...].astype(F32)
+    part_right = from_right_ref[2 * height_ext :, :].astype(F32) + far_right_ref[...].astype(F32)
+    part_left = from_left_ref[2 * height_ext :, :].astype(F32) + far_left_ref[...].astype(F32)
     for c in range(3):
         here = slice(c * rows, (c + 1) * rows)
         total = own_ref[here, :].astype(F32) + other_ref[here, :].astype(F32)
@@ -719,7 +718,7 @@
     )
     share, to_left, to_right, part_left, part_right = call(
         functools.partial(merge_kernel, steps, halo, outer, inner),
-        [((3 * rows + 6 * halo + SUB, cols), BF16)] + [((2 * high, cols), BF16)] * 2 + [((high, cols), BF16)] * 2,
+        [((3 * rows + 6 * halo + SUB, cols), BF16)] + [((3 * high, cols), BF16)] * 2 + [((high, cols), BF16)] * 2,
         [place, outer_share, inner_share, below, above, square, tile_left, tile_right],
         smem=1,
         name="merge",
@@ -729,13 +728,13 @@
     def across(to, part, perm):
         if groups != 2:
             part = lax.psum(part.astype(F32), "ens")
-            return lax.ppermute(to, "tx", perm), lax.ppermute(part, "tx", perm), jnp.zeros_like(part)
-        got = lax.ppermute(jnp.concatenate([to, part], axis=0), "tx", perm)
+            sent = jnp.concatenate([to[: 2 * high].astype(F32), part], axis=0)
+            return lax.ppermute(sent, "tx", perm), jnp.zeros_like(part)
         far = [(e * n_tx + i, (1 - e) * n_tx + j) for e in (0, 1) for i, j in perm]
-        return got[: 2 * high], got[2 * high :], lax.ppermute(part, ("ens", "tx"), far)
-
-    from_left, near_left, far_left = across(to_right, part_right, right)
-    from_right, near_right, far_right = across(to_left, part_left, left)
+        return lax.ppermute(to, "tx", perm), lax.ppermute(part, ("ens", "tx"), far)
+
+    from_left, far_left = across(to_right, part_right, right)
+    from_right, far_right = across(to_left, part_left, left)
     (tall,) = call(
         functools.partial(tall_kernel, steps, halo),
         [((2 * steps + 5, high, cols), F32)],
@@ -754,8 +753,6 @@
             share_other,
             from_right,
             from_left,
-            near_right,
-            near_left,
             far_right,
             far_left,
             early,

time: 52.1 us -> 52.2 us (level)
  starting transfers between devices: 14.1 us -> 13.5 us
  waiting for transfers between devices: 12 us -> 12.6 us
    ppermute x2, starting transfers between devices: 1.5 us -> 0.51 us  [across(): lax.ppermute(to, 'tx', perm)]
    ppermute x2, waiting for transfers between devices: 2.33 us -> 3.18 us  [across(): lax.ppermute(part, ('ens', 'tx'), far)]
  transfers between devices with their start and end apart: 10 -> 10, of which waited for: 7 -> 6; matrix products, arithmetic and copies ran while one was open for 0% -> 0% of each run, Pallas kernels for 9% -> 9%
where the time goes in v5:
time: 52.2 us; the launch traced here: 52 us
  starting transfers between devices  13.5 us (26%)
  Pallas kernels  13.2 us (25%)
  waiting for transfers between devices  12.6 us (24%)
  blocking collectives  8.97 us (17%)
  local copies, waits for them, and re-layouts  2.77 us (5%)
  between operations  0.84 us (2%)
    pallas_call x13, Pallas kernels, call(): pl.pallas_call(kernel, out_shape=out_shape, grid=grid, in_specs=in_specs...  13.2 us
    all_to_all x1, blocking collectives, body(): terms = lax.all_to_all(cost_terms, ('ty', 'tx'), 0, 0, tiled=True)  8.97 us
    ppermute x4, starting transfers between devices, to_others(): lax.ppermute(x, 'ens', [(i, (i - k) % groups) for i in range(groups)])  7.65 us
    ppermute x4, waiting for transfers between devices, to_others(): lax.ppermute(x, 'ens', [(i, (i - k) % groups) for i in range(groups)])  5.38 us
    ppermute x1, waiting for transfers between devices, body(): above = lax.ppermute(bottom, 'ty', down)  4.07 us
    ppermute x1, starting transfers between devices, body(): below = lax.ppermute(top, 'ty', up)  3.62 us
    ppermute x2, waiting for transfers between devices, across(): lax.ppermute(part, ('ens', 'tx'), far)  3.18 us
    unnamed x26, local copies, waits for them, and re-layouts  2.77 us
  transfers between devices with their start and end apart: 10, of which 6 were waited for; matrix products, arithmetic and copies ran while one was open for 0% of the time, Pallas kernels for 9%

profile of v5, /device:TPU:0, one launch (start us, length us, event | category | flops | bytes accessed | tf_op | source)
XLA Modules:
  0.0 52.0 jit_solution(910993803427998669)
XLA Ops:
  0.6 0.0 copy-start.2
  0.6 1.9 %send.2 = bf16[16,64,128]{2,1,0:T(8,128)(2,1)} custom-call(f32[16,128,128]{2,1,0:T(8,128)} %refs_3_.1), custom_call_target="tpu_custom_call" | custom-call | bytes 1310720 | tf_op jit(solution)/shard_map/send/pallas_call | solution.py:28
  2.5 3.0 %collective-permute-start = (bf16[16,64,128]{2,1,0:T(8,128)(2,1)}, bf16[16,64,128]{2,1,0:T(8,128)(2,1)S(1)}, u32[]{:S(2)}, u32[]{:S(2)}) collective-permute-start(bf16[16,64,128]{2,1,0:T(8,128)(2,1)} %send.2), channel_id=1, source_target_pairs={{0,16},{16,0},{1,17},{17,1},{2,18},{18,2},{3,19},{19,3},{4,20},{20... | collective-permute-start | bytes 786440 | tf_op jit(solution)/shard_map/ppermute | solution.py:605
  5.5 0.1 pad_add_fusion.place_ref
  5.6 0.0 copy-done.2
  5.6 1.4 %copy-done = bf16[16,3,128,128]{3,2,1,0:T(8,128)(2,1)S(1)} copy-done((bf16[16,3,128,128]{3,2,1,0:T(8,128)(2,1)S(1)}, bf16[16,3,128,128]{3,2,1,0:T(8,128)(2,1)}, u32[]{:S(2)}) %copy-start) | copy-done | bytes 1572888
  7.0 0.7 %copy-done.7 = s32[32]{0:T(128)S(1)} copy-done((s32[32]{0:T(128)S(1)}, s32[32]{0:T(128)}, u32[]{:S(2)}) %copy-start.7) | copy-done | bytes 152
  7.7 0.7 %copy-done.8 = f32[32]{0:T(128)S(1)} copy-done((f32[32]{0:T(128)S(1)}, f32[32]{0:T(128)}, u32[]{:S(2)}) %copy-start.8) | copy-done | bytes 152
  8.3 1.9 %own.1 = (bf16[2,256,256]{2,1,0:T(8,128)(2,1)S(1)}, bf16[2,256,256]{2,1,0:T(8,128)(2,1)S(1)}, f32[3,128,128]{2,1,0:T(8,128)S(1)}, bf16[16,128]{1,0:T(8,128)(2,1)S(1)}) custom-call(s32[3]{0:T(128)S(1)} %pad_add_fusion.place_ref, s32[32]{0:T(128)S(1)} %copy-done.7, f32[32]{0:T(128)S(1)} %copy-done.8, f32[16,128,128]{2,1,0:T(8,128)S(1)} %copy-done.2, ...), custom_call_target="tpu_custom_call" | custom-call | bytes 3346700 | tf_op jit(solution)/shard_map/own/pallas_call | solution.py:28
  10.2 0.0 copy-start.1
  10.2 0.1 send.3
  10.3 0.1 collective-permute-start.3
  10.4 0.0 copy-done.9
  10.4 0.0 copy-done.10
  10.5 0.0 copy-start.4
  10.5 0.0 copy-start.5
  10.5 0.0 copy-start.6
  10.5 1.2 %maps.1 = (f32[12,128,128]{2,1,0:T(8,128)S(1)}, f32[8,128]{1,0:T(8,128)S(1)}) custom-call(s32[6,512]{1,0:T(8,128)S(1)} %bitcast.16, f32[6,512]{1,0:T(8,128)S(1)} %get-tuple-element.44.values_ref, f32[6,512]{1,0:T(8,128)S(1)} %get-tuple-element.43.weights_ref, f32[3,128,128]{2,1,0:T(8,128)S(1)} %copy-done.3), custom_call_target="tpu_custom_call" | custom-call | flops 402653184 | bytes 1024000 | tf_op jit(solution)/shard_map/maps/pallas_call | solution.py:28
  11.7 0.6 %collective-permute-done.refs_0_ = bf16[16,64,128]{2,1,0:T(8,128)(2,1)S(1)} collective-permute-done((bf16[16,64,128]{2,1,0:T(8,128)(2,1)}, bf16[16,64,128]{2,1,0:T(8,128)(2,1)S(1)}, u32[]{:S(2)}, u32[]{:S(2)}) %collective-permute-start) | collective-permute-done | bytes 262176 | tf_op jit(solution)/shard_map/ppermute | solution.py:605
  12.3 0.3 outer_share.1.share_ref.outer_ref
  12.6 0.0 copy-done.4
  12.6 0.0 copy-done.5
  12.6 0.0 copy-done.6
  12.7 3.6 %collective-permute-start.1 = (bf16[320,128]{1,0:T(8,128)(2,1)S(1)}, bf16[320,128]{1,0:T(8,128)(2,1)S(1)}, u32[]{:S(2)}, u32[]{:S(2)}) collective-permute-start(bf16[320,128]{1,0:T(8,128)(2,1)S(1)} %get-tuple-element.26), channel_id=1, source_target_pairs={{4,0},{8,4},{12,8},{0,12},{5,1},{9,5},{13,9},{1,13},{6,2},{10,6},{... | collective-permute-start | bytes 245768 | tf_op jit(solution)/shard_map/ppermute | solution.py:708
  16.3 0.0 collective-permute-start.2
  16.3 0.3 tile_pack.1
  16.6 1.5 %collective-permute-done.3.refs_0_ = bf16[16,64,128]{2,1,0:T(8,128)(2,1)S(1)} collective-permute-done((bf16[16,64,128]{2,1,0:T(8,128)(2,1)S(1)}, bf16[16,64,128]{2,1,0:T(8,128)(2,1)S(1)}, u32[]{:S(2)}, u32[]{:S(2)}) %collective-permute-start.3) | collective-permute-done | bytes 262176 | tf_op jit(solution)/shard_map/ppermute | solution.py:605
  18.1 0.3 inner_share.1.inner_ref
  18.5 0.0 collective-permute-done.1.below_ref
  18.5 4.1 %collective-permute-done.2.above_ref = bf16[320,128]{1,0:T(8,128)(2,1)S(1)} collective-permute-done((bf16[320,128]{1,0:T(8,128)(2,1)S(1)}, bf16[320,128]{1,0:T(8,128)(2,1)S(1)}, u32[]{:S(2)}, u32[]{:S(2)}) %collective-permute-start.2) | collective-permute-done | bytes 81952 | tf_op jit(solution)/shard_map/ppermute | solution.py:707
  22.5 0.7 %merge.1 = (bf16[544,128]{1,0:T(8,128)(2,1)S(1)}, bf16[528,128]{1,0:T(8,128)(2,1)S(1)}, bf16[528,128]{1,0:T(8,128)(2,1)S(1)}, bf16[176,128]{1,0:T(8,128)(2,1)S(1)}, bf16[176,128]{1,0:T(8,128)(2,1)S(1)}) custom-call(s32[3]{0:T(128)S(1)} %pad_add_fusion.place_ref, bf16[192,128]{1,0:T(8,128)(2,1)S(1)} %outer_share.1.share_ref.outer_ref, ...), custom_call_target="tpu_custom_call" | custom-call | bytes 897036 | tf_op jit(solution)/shard_map/merge/pallas_call | solution.py:28
  23.3 2.3 %collective-permute-start.4 = (bf16[544,128]{1,0:T(8,128)(2,1)S(1)}, bf16[544,128]{1,0:T(8,128)(2,1)S(1)}, u32[]{:S(2)}, u32[]{:S(2)}) collective-permute-start(bf16[544,128]{1,0:T(8,128)(2,1)S(1)} %get-tuple-element.31.own_ref), channel_id=1, source_target_pairs={{0,16},{16,0},{1,17},{17,1},{2,18},{18,2},{3,19},{19,3},{4,20},{20... | collective-permute-start | bytes 417800 | tf_op jit(solution)/shard_map/ppermute | solution.py:605
  25.5 0.0 collective-permute-start.5
  25.6 0.5 collective-permute-start.6
  26.1 0.8 %collective-permute-start.7 = (bf16[176,128]{1,0:T(8,128)(2,1)S(1)}, bf16[176,128]{1,0:T(8,128)(2,1)S(1)}, u32[]{:S(2)}, u32[]{:S(2)}) collective-permute-start(bf16[176,128]{1,0:T(8,128)(2,1)S(1)} %get-tuple-element.34), channel_id=1, source_target_pairs={{1,16},{2,17},{3,18},{0,19},{17,0},{18,1},{19,2},{16,3},{5,20},{6,... | collective-permute-start | bytes 135176 | tf_op jit(solution)/shard_map/ppermute | solution.py:734
  26.9 0.9 %collective-permute-start.8 = (bf16[176,128]{1,0:T(8,128)(2,1)S(1)}, bf16[176,128]{1,0:T(8,128)(2,1)S(1)}, u32[]{:S(2)}, u32[]{:S(2)}) collective-permute-start(bf16[176,128]{1,0:T(8,128)(2,1)S(1)} %get-tuple-element.35), channel_id=1, source_target_pairs={{0,17},{1,18},{2,19},{3,16},{16,1},{17,2},{18,3},{19,0},{4,21},{5,... | collective-permute-start | bytes 135176 | tf_op jit(solution)/shard_map/ppermute | solution.py:734
  27.8 0.6 %tall.1.tall_ref = f32[17,176,128]{2,1,0:T(8,128)S(1)} custom-call(s32[3]{0:T(128)S(1)} %pad_add_fusion.place_ref, f32[12,128,128]{2,1,0:T(8,128)S(1)} %get-tuple-element.23.maps_ref, f32[128,128]{1,0:T(8,128)S(1)} %copy-done.5, s32[128,128]{1,0:T(8,128)S(1)} %copy-done.6, f32[3,128,128]{2,1,0:T(8,128)S(1)} %copy-done.4, f32[3,128,128]{2,1,0:T(8,128)S(1)} %copy-done.3, ...), custom_call_target="tpu_custom_call" | custom-call | bytes 3006476 | tf_op jit(solution)/shard_map/tall/pallas_call | solution.py:28
  28.5 1.1 %collective-permute-done.7.far_right_ref = bf16[176,128]{1,0:T(8,128)(2,1)S(1)} collective-permute-done((bf16[176,128]{1,0:T(8,128)(2,1)S(1)}, bf16[176,128]{1,0:T(8,128)(2,1)S(1)}, u32[]{:S(2)}, u32[]{:S(2)}) %collective-permute-start.7) | collective-permute-done | bytes 45088 | tf_op jit(solution)/shard_map/ppermute | solution.py:734
  29.6 2.0 %collective-permute-done.8.far_left_ref = bf16[176,128]{1,0:T(8,128)(2,1)S(1)} collective-permute-done((bf16[176,128]{1,0:T(8,128)(2,1)S(1)}, bf16[176,128]{1,0:T(8,128)(2,1)S(1)}, u32[]{:S(2)}, u32[]{:S(2)}) %collective-permute-start.8) | collective-permute-done | bytes 45088 | tf_op jit(solution)/shard_map/ppermute | solution.py:734
  31.6 0.0 collective-permute-done.5.from_right_ref
  31.6 0.0 collective-permute-done.6.from_left_ref
  31.6 0.0 collective-permute-done.4.other_ref
  31.6 4.1 %model.1 = (f32[3,128,128]{2,1,0:T(8,128)}, f32[16,128]{1,0:T(8,128)S(1)}, f32[3,128,128]{2,1,0:T(8,128)S(1)}) custom-call(s32[3]{0:T(128)S(1)} %pad_add_fusion.place_ref, f32[17,176,128]{2,1,0:T(8,128)S(1)} %tall.1.tall_ref, bf16[544,128]{1,0:T(8,128)(2,1)S(1)} %get-tuple-element.31.own_ref, bf16[544,128]{1,0:T(8,128)(2,1)S(1)} %collective-permute-done.4.other_ref, ...), custom_call_target="tpu_custom_call" | custom-call | bytes 2969612 | tf_op jit(solution)/shard_map/model/pallas_call | solution.py:28
  35.8 0.3 products.1.refs_0_
  36.1 2.3 %collective-permute-start.9 = (bf16[16,128,128]{2,1,0:T(8,128)(2,1)S(1)}, bf16[16,128,128]{2,1,0:T(8,128)(2,1)S(1)}, u32[]{:S(2)}, u32[]{:S(2)}) collective-permute-start(bf16[16,128,128]{2,1,0:T(8,128)(2,1)S(1)} %products.1.refs_0_), channel_id=1, source_target_pairs={{0,16},{16,0},{1,17},{17,1},{2,18},{18,2},{3,19},{19,3},{4,20},{20... | collective-permute-start | bytes 1572872 | tf_op jit(solution)/shard_map/ppermute | solution.py:605
  38.4 9.0 %all_to_all.11 = f32[16,1,128]{2,1,0:T(1,128)S(1)} all-to-all(f32[16,1,128]{2,1,0:T(1,128)S(1)} %bitcast.17), channel_id=1, replica_groups=mesh['ens'=2,'ty'=4,'tx'=4] {'ty','tx'}, dimensions={0} | all-to-all | bytes 16384 | tf_op jit(solution)/shard_map/all_to_all | solution.py:775
  47.3 3.2 %collective-permute-done.9.refs_1_ = bf16[16,128,128]{2,1,0:T(8,128)(2,1)S(1)} collective-permute-done((bf16[16,128,128]{2,1,0:T(8,128)(2,1)S(1)}, bf16[16,128,128]{2,1,0:T(8,128)(2,1)S(1)}, u32[]{:S(2)}, u32[]{:S(2)}) %collective-permute-start.9) | collective-permute-done | bytes 524320 | tf_op jit(solution)/shard_map/ppermute | solution.py:605
  50.6 1.4 %final.1 = (f32[16,128,128]{2,1,0:T(8,128)}, f32[1,1]{1,0:T(1,128)}) custom-call(bf16[16,128,128]{2,1,0:T(8,128)(2,1)S(1)} %products.1.refs_0_, bf16[16,128,128]{2,1,0:T(8,128)(2,1)S(1)} %collective-permute-done.9.refs_1_, bf16[2,256,256]{2,1,0:T(8,128)(2,1)S(1)} %get-tuple-element.39.refs_2_, f32[16,128,128]{2,1,0:T(8,128)S(1)} %copy-done.2, ...), custom_call_target="tpu_custom_call" | custom-call | bytes 3416068 | tf_op jit(solution)/shard_map/final/pallas_call | solution.py:28
  (13 shorter events, 0.1 us)
Async XLA Ops:
  0.6 5.0 %copy-start.2 = (f32[16,128,128]{2,1,0:T(8,128)S(1)}, f32[16,128,128]{2,1,0:T(8,128)}, u32[]{:S(2)}) copy-start(f32[16,128,128]{2,1,0:T(8,128)} %refs_3_.1) | copy-start | bytes 3145732
  2.5 9.8 %collective-permute-start = (bf16[16,64,128]{2,1,0:T(8,128)(2,1)}, bf16[16,64,128]{2,1,0:T(8,128)(2,1)S(1)}, u32[]{:S(2)}, u32[]{:S(2)}) collective-permute-start(bf16[16,64,128]{2,1,0:T(8,128)(2,1)} %send.2), channel_id=1, source_target_pairs={{0,16},{16,0},{1,17},{17,1},{2,18},{18,2},{3,19},{19,3},{4,20},{20... | collective-permute-start | bytes 786440 | tf_op jit(solution)/shard_map/ppermute | solution.py:605
  5.6 1.4 %copy-start = (bf16[16,3,128,128]{3,2,1,0:T(8,128)(2,1)S(1)}, bf16[16,3,128,128]{3,2,1,0:T(8,128)(2,1)}, u32[]{:S(2)}) copy-start(bf16[16,3,128,128]{3,2,1,0:T(8,128)(2,1)} %perturbations_ref.3) | copy-start | bytes 4718596
  7.0 0.7 %copy-start.7 = (s32[32]{0:T(128)S(1)}, s32[32]{0:T(128)}, u32[]{:S(2)}) copy-start(s32[32]{0:T(128)} %offsets_ref.1) | copy-start | bytes 388
  7.7 0.7 %copy-start.8 = (f32[32]{0:T(128)S(1)}, f32[32]{0:T(128)}, u32[]{:S(2)}) copy-start(f32[32]{0:T(128)} %weights_ref.1) | copy-start | bytes 388
  8.3 2.1 %copy-start.9 = (s32[1,1,6,512]{3,1,2,0:T(1,128)S(1)}, s32[1,1,6,512]{3,1,2,0:T(1,128)}, u32[]{:S(2)}) copy-start(s32[1,1,6,512]{3,1,2,0:T(1,128)} %param.19) | copy-start | bytes 36868
  8.3 2.1 %copy-start.10 = (f32[1,1,6,512]{3,1,2,0:T(1,128)S(1)}, f32[1,1,6,512]{3,1,2,0:T(1,128)}, u32[]{:S(2)}) copy-start(f32[1,1,6,512]{3,1,2,0:T(1,128)} %param.21) | copy-start | bytes 36868
  8.3 2.1 %copy-start.11 = (f32[1,1,6,512]{3,1,2,0:T(1,128)S(1)}, f32[1,1,6,512]{3,1,2,0:T(1,128)}, u32[]{:S(2)}) copy-start(f32[1,1,6,512]{3,1,2,0:T(1,128)} %param.20) | copy-start | bytes 36868
  8.3 2.1 %copy-start.3 = (f32[3,128,128]{2,1,0:T(8,128)S(1)}, f32[3,128,128]{2,1,0:T(8,128)}, u32[]{:S(2)}) copy-start(f32[3,128,128]{2,1,0:T(8,128)} %control_ref.9) | copy-start | bytes 589828
  10.2 2.1 %copy-start.1 = (bf16[16,3,128,128]{3,2,1,0:T(8,128)(2,1)S(1)}, bf16[16,3,128,128]{3,2,1,0:T(8,128)(2,1)}, u32[]{:S(2)}) copy-start(bf16[16,3,128,128]{3,2,1,0:T(8,128)(2,1)} %perturbations_ref.3) | copy-start | bytes 4718596
  10.3 7.8 %collective-permute-start.3 = (bf16[16,64,128]{2,1,0:T(8,128)(2,1)S(1)}, bf16[16,64,128]{2,1,0:T(8,128)(2,1)S(1)}, u32[]{:S(2)}, u32[]{:S(2)}) collective-permute-start(bf16[16,64,128]{2,1,0:T(8,128)(2,1)S(1)} %send.3), channel_id=1, source_target_pairs={{0,16},{16,0},{1,17},{17,1},{2,18},{18,2},{3,19},{19,3},{4,20},{20... | collective-permute-start | bytes 786440 | tf_op jit(solution)/shard_map/ppermute | solution.py:605
  10.5 2.2 %copy-start.4 = (f32[3,128,128]{2,1,0:T(8,128)S(1)}, f32[3,128,128]{2,1,0:T(8,128)}, u32[]{:S(2)}) copy-start(f32[3,128,128]{2,1,0:T(8,128)} %std_ref.7) | copy-start | bytes 589828
  10.5 2.2 %copy-start.5 = (f32[128,128]{1,0:T(8,128)S(1)}, f32[128,128]{1,0:T(8,128)}, u32[]{:S(2)}) copy-start(f32[128,128]{1,0:T(8,128)} %courant_ref.5) | copy-start | bytes 196612
  10.5 2.1 %copy-start.6 = (s32[128,128]{1,0:T(8,128)S(1)}, s32[128,128]{1,0:T(8,128)}, u32[]{:S(2)}) copy-start(s32[128,128]{1,0:T(8,128)} %mask_ref.5) | copy-start | bytes 196612
  12.7 5.8 %collective-permute-start.1 = (bf16[320,128]{1,0:T(8,128)(2,1)S(1)}, bf16[320,128]{1,0:T(8,128)(2,1)S(1)}, u32[]{:S(2)}, u32[]{:S(2)}) collective-permute-start(bf16[320,128]{1,0:T(8,128)(2,1)S(1)} %get-tuple-element.26), channel_id=1, source_target_pairs={{4,0},{8,4},{12,8},{0,12},{5,1},{9,5},{13,9},{1,13},{6,2},{10,6},{... | collective-permute-start | bytes 245768 | tf_op jit(solution)/shard_map/ppermute | solution.py:708
  16.3 6.2 %collective-permute-start.2 = (bf16[320,128]{1,0:T(8,128)(2,1)S(1)}, bf16[320,128]{1,0:T(8,128)(2,1)S(1)}, u32[]{:S(2)}, u32[]{:S(2)}) collective-permute-start(bf16[320,128]{1,0:T(8,128)(2,1)S(1)} %get-tuple-element.27), channel_id=1, source_target_pairs={{0,4},{4,8},{8,12},{12,0},{1,5},{5,9},{9,13},{13,1},{2,6},{6,10},{... | collective-permute-start | bytes 245768 | tf_op jit(solution)/shard_map/ppermute | solution.py:707
  23.3 8.4 %collective-permute-start.4 = (bf16[544,128]{1,0:T(8,128)(2,1)S(1)}, bf16[544,128]{1,0:T(8,128)(2,1)S(1)}, u32[]{:S(2)}, u32[]{:S(2)}) collective-permute-start(bf16[544,128]{1,0:T(8,128)(2,1)S(1)} %get-tuple-element.31.own_ref), channel_id=1, source_target_pairs={{0,16},{16,0},{1,17},{17,1},{2,18},{18,2},{3,19},{19,3},{4,20},{20... | collective-permute-start | bytes 417800 | tf_op jit(solution)/shard_map/ppermute | solution.py:605
  25.5 6.1 %collective-permute-start.5 = (bf16[528,128]{1,0:T(8,128)(2,1)S(1)}, bf16[528,128]{1,0:T(8,128)(2,1)S(1)}, u32[]{:S(2)}, u32[]{:S(2)}) collective-permute-start(bf16[528,128]{1,0:T(8,128)(2,1)S(1)} %get-tuple-element.32), channel_id=1, source_target_pairs={{1,0},{2,1},{3,2},{0,3},{5,4},{6,5},{7,6},{4,7},{9,8},{10,9},{11,1... | collective-permute-start | bytes 405512 | tf_op jit(solution)/shard_map/ppermute | solution.py:734
  25.6 6.1 %collective-permute-start.6 = (bf16[528,128]{1,0:T(8,128)(2,1)S(1)}, bf16[528,128]{1,0:T(8,128)(2,1)S(1)}, u32[]{:S(2)}, u32[]{:S(2)}) collective-permute-start(bf16[528,128]{1,0:T(8,128)(2,1)S(1)} %get-tuple-element.33), channel_id=1, source_target_pairs={{0,1},{1,2},{2,3},{3,0},{4,5},{5,6},{6,7},{7,4},{8,9},{9,10},{10,1... | collective-permute-start | bytes 405512 | tf_op jit(solution)/shard_map/ppermute | solution.py:734
  26.1 3.5 %collective-permute-start.7 = (bf16[176,128]{1,0:T(8,128)(2,1)S(1)}, bf16[176,128]{1,0:T(8,128)(2,1)S(1)}, u32[]{:S(2)}, u32[]{:S(2)}) collective-permute-start(bf16[176,128]{1,0:T(8,128)(2,1)S(1)} %get-tuple-element.34), channel_id=1, source_target_pairs={{1,16},{2,17},{3,18},{0,19},{17,0},{18,1},{19,2},{16,3},{5,20},{6,... | collective-permute-start | bytes 135176 | tf_op jit(solution)/shard_map/ppermute | solution.py:734
  26.9 4.8 %collective-permute-start.8 = (bf16[176,128]{1,0:T(8,128)(2,1)S(1)}, bf16[176,128]{1,0:T(8,128)(2,1)S(1)}, u32[]{:S(2)}, u32[]{:S(2)}) collective-permute-start(bf16[176,128]{1,0:T(8,128)(2,1)S(1)} %get-tuple-element.35), channel_id=1, source_target_pairs={{0,17},{1,18},{2,19},{3,16},{16,1},{17,2},{18,3},{19,0},{4,21},{5,... | collective-permute-start | bytes 135176 | tf_op jit(solution)/shard_map/ppermute | solution.py:734
  36.1 14.5 %collective-permute-start.9 = (bf16[16,128,128]{2,1,0:T(8,128)(2,1)S(1)}, bf16[16,128,128]{2,1,0:T(8,128)(2,1)S(1)}, u32[]{:S(2)}, u32[]{:S(2)}) collective-permute-start(bf16[16,128,128]{2,1,0:T(8,128)(2,1)S(1)} %products.1.refs_0_), channel_id=1, source_target_pairs={{0,16},{16,0},{1,17},{17,1},{2,18},{18,2},{3,19},{19,3},{4,20},{20... | collective-permute-start | bytes 1572872 | tf_op jit(solution)/shard_map/ppermute | solution.py:605
